TPU v7x, 32 devices: a whole 2x2x4 slice. The times are simulated.
32 devices in a mesh: lon: 8 (over y, x, core), lat: 4 (over z).
Axes of the slice: x: 2, y: 2, z: 4, core: 2. Of those that a mesh axis runs over, the one named last changes fastest.
Arguments:
- control: float32 [4, 137, 32, 1024], P(None, None, 'lat', 'lon'), may hold values from -6 to 6
- smoothing: float32 [4, 137, 32, 1024], P(None, None, 'lat', 'lon'), may hold values from 0.45 to 1, as said below
- lat_taps: float32 [4, 5, 32], P(None, None, 'lat'), may hold values from 0.1 to 0.6
- vert_corr: float32 [4, 137, 137], replicated, may hold values from -0.5 to 1.5
- obs_cell: int32 [32, 32, 128], P(('lon', 'lat')), may hold values from 0 to 1023
- obs_field: int32 [32, 32], P(('lon', 'lat')), may hold values from 0 to 3
- obs_count: int32 [32, 32], P(('lon', 'lat')), may hold values from 1 to 128, as said below
- obs_owner: int32 [32, 32], P(('lon', 'lat')), may hold values from 0 to 31, as said below
- obs_jacobian: bfloat16 [32, 137, 32, 128], P(('lon', 'lat')), may hold values from -1 to 1
- obs_value: bfloat16 [32, 32, 128], P(('lon', 'lat')), may hold values from -6 to 6
- obs_precision: bfloat16 [32, 32, 128], P(('lon', 'lat')), may hold values from 0.29882812 to 3
Outputs:
- gradient: float32 [4, 137, 32, 1024], P(None, None, 'lat', 'lon')
- obs_residual: float32 [32, 32, 128], P(('lon', 'lat'))
Inputs may be any that keep to these rules, and one draw needn't show every extreme that they name: `smoothing`: each coefficient is positive and below 1. `obs_count`: slots of a block at or past its count are empty; on every device some block has all 128 slots live. `obs_owner`: on each device every owner index names exactly 1 of the 32 blocks.
All inputs are finite; a program needn't handle non-finite values.
Results may differ from a plain program's by a relative error of at most 0.0029.
Values may be sent and summed in bfloat16 or wider, within the bound.
No kernel may reach another device: no remote copies, remote signals or barrier semaphores. Data moves between devices by JAX's collectives and lax.ppermute only.
A program may use at most 192 MiB of HBM per device.

v0:
```python
import functools

import jax
import jax.numpy as jnp
from jax import lax
from jax.experimental import pallas as pl
from jax.experimental.pallas import tpu as pltpu
from jax.sharding import PartitionSpec as P

LANES = 128
HALO = 2
BF = jnp.bfloat16
F32 = jnp.float32
NT = (((1,), (1,)), ((), ()))
VMEM = pl.BlockSpec(memory_space=pltpu.VMEM)
SMEM = pl.BlockSpec(memory_space=pltpu.SMEM)


def params(mib):
    return pltpu.CompilerParams(vmem_limit_bytes=mib * 1024 * 1024)


def sds(shape, dtype=F32):
    return jax.ShapeDtypeStruct(shape, dtype)


def split(x):
    high = x.astype(BF)
    return high, (x - high.astype(F32)).astype(BF)


def step_rows(i, per):
    return pl.ds(pl.multiple_of(i * per, 8), per)


def solve_sectors(me, products, ends, cross, backs):
    count = len(products)
    whole, state = products[0], ends[0]
    for s in range(1, count):
        state = products[s] * state + ends[s]
        whole = whole * products[s]
    gap = 1.0 - whole
    east = state / gap
    east_in = jnp.zeros_like(east)
    turned = []
    for s in range(count):
        east_in = jnp.where(me == s, east, east_in)
        turned.append(backs[s] + cross[s] * east)
        east = products[s] * east + ends[s]
    state = turned[count - 1]
    for s in range(count - 2, -1, -1):
        state = products[s] * state + turned[s]
    west = state / gap
    west_in = jnp.zeros_like(west)
    for s in range(count - 1, -1, -1):
        west_in = jnp.where(me == s, west, west_in)
        west = products[s] * west + turned[s]
    return east_in, west_in


def to_lines(src, dst, extra, fields, levels, rows):
    per = (fields + 1) * rows
    over, room = levels - LANES, LANES // fields
    extra[...] = jnp.zeros_like(extra)
    for j in range(rows):
        for f in range(fields):
            tile = src[pl.ds(f * levels * rows + j, LANES, stride=rows), :]
            dst[pl.ds(f * rows + j, LANES, stride=per), :] = tile.T
            extra[j, pl.ds(f * room, over), :] = src[
                pl.ds((f * levels + LANES) * rows + j, over, stride=rows), :
            ]
        dst[pl.ds(fields * rows + j, LANES, stride=per), :] = extra[j].T


def filter_kernel(
    fields, levels, rows, control, smoothing,
    a_t, g_t, w0_t, w1_t, s_t, gq_t, gp_t, ends, x_t, e_t, pe_t, extra,
):
    per = (fields + 1) * rows
    to_lines(smoothing, a_t, extra, fields, levels, rows)
    to_lines(control, x_t, extra, fields, levels, rows)

    def east(i, carry):
        e, p = carry
        at = step_rows(i, per)
        a = a_t[at, :]
        g = jnp.sqrt((1.0 - a) * (1.0 + a))
        g_t[at, :] = g
        pe_t[at, :] = p
        e = a * e + g * x_t[at, :]
        e_t[at, :] = e
        return e, p * a

    zero = jnp.zeros((per, LANES), F32)
    one = jnp.ones((per, LANES), F32)
    e, p = lax.fori_loop(0, LANES, east, (zero, one), unroll=4)

    def west(k, carry):
        w0, w1, s = carry
        at = step_rows(LANES - 1 - k, per)
        a, g = a_t[at, :], g_t[at, :]
        w0 = a * w0 + g * e_t[at, :]
        t = w1 + g * pe_t[at, :]
        gq_t[at, :] = g * t
        w1 = a * t
        gp_t[at, :] = g * s
        s = a * s
        w0_t[at, :] = w0
        w1_t[at, :] = w1
        s_t[at, :] = s
        return w0, w1, s

    w0, w1, _ = lax.fori_loop(0, LANES, west, (zero, zero, one), unroll=4)
    ends[0] = p
    ends[1] = e
    ends[2] = w0
    ends[3] = w1


def pack_halo(src, low, high, fields, rows):
    per = (fields + 1) * rows
    for b in range(fields + 1):
        for j in range(HALO):
            low[b, j] = src[pl.ds(b * rows + j, LANES, stride=per), :].astype(BF)
            high[b, j] = src[pl.ds(b * rows + rows - HALO + j, LANES, stride=per), :].astype(BF)


def unpack_halo(low, high, dst, fields, rows):
    per = (fields + 1) * rows
    for b in range(fields + 1):
        for j in range(HALO):
            dst[pl.ds(b * rows + j, LANES, stride=per), :] = low[b, j].astype(F32)
            dst[pl.ds(b * rows + rows - HALO + j, LANES, stride=per), :] = high[b, j].astype(F32)


def western_kernel(fields, rows, count, me, gathered, w0_t, w1_t, s_t, western, low, high):
    per = (fields + 1) * rows
    part = [[gathered[s, q] for s in range(count)] for q in range(4)]
    east_in, west_in = solve_sectors(me[0], part[0], part[1], part[3], part[2])

    def one(i, _):
        at = step_rows(i, per)
        western[at, :] = w0_t[at, :] + w1_t[at, :] * east_in + s_t[at, :] * west_in
        return 0

    lax.fori_loop(0, LANES, one, 0, unroll=8)
    pack_halo(western, low, high, fields, rows)


def state_kernel(fields, rows, western, low, high, taps, vert, state, halo, mh, ml):
    blocks = fields + 1
    per = blocks * rows
    unpack_halo(low, high, halo, fields, rows)
    tap = [taps[t] for t in range(2 * HALO + 1)]
    row = lax.broadcasted_iota(jnp.int32, (blocks, rows, LANES), 1)

    def mix(i):
        at = step_rows(i, per)
        w = western[at, :].reshape(blocks, rows, LANES)
        h = halo[at, :].reshape(blocks, rows, LANES)
        total = tap[HALO] * w
        for s in range(1, HALO + 1):
            total += tap[HALO + s] * pltpu.roll(jnp.where(row < s, h, w), rows - s, 1)
            total += tap[HALO - s] * pltpu.roll(jnp.where(row >= rows - s, h, w), s, 1)
        return total

    def pair(k, _):
        m = jnp.concatenate([mix(2 * k), mix(2 * k + 1)], axis=1)
        high_part, low_part = split(m)
        at = pl.ds(pl.multiple_of(k * 2 * rows, 16), 2 * rows)
        mh[:, at, :] = high_part
        ml[:, at, :] = low_part
        return 0

    lax.fori_loop(0, LANES // 2, pair, 0, unroll=2)
    for f in range(fields):
        vh, vl = split(vert[f])
        xh = jnp.concatenate([mh[f], mh[fields]], axis=1)
        xl = jnp.concatenate([ml[f], ml[fields]], axis=1)
        out = lax.dot_general(vh, xh, NT, preferred_element_type=F32)
        out += lax.dot_general(vh, xl, NT, preferred_element_type=F32)
        out += lax.dot_general(vl, xh, NT, preferred_element_type=F32)
        state[f] = out.astype(BF)


def obs_kernel(
    fields, levels, rows, field, owner, cells, state, jacobian, taps, vert,
    residual, spread, low, high, order, number, acc, lift, outward,
):
    blocks = fields + 1
    per = blocks * rows
    total = field.shape[0]
    sites = rows * LANES
    for f in range(fields):
        number[f] = 0

    def place(k, _):
        f = field[k]
        n = number[f]
        order[f * total + n] = k
        number[f] = n + 1
        return 0

    lax.fori_loop(0, total, place, 0)
    site = lax.broadcasted_iota(jnp.int32, (sites, 2 * LANES), 0)

    for f in range(fields):
        acc[...] = jnp.zeros_like(acc)
        found = number[f]

        def two(p, _):
            k0 = order[f * total + 2 * p]
            second = 2 * p + 1 < found
            k1 = jnp.where(second, order[f * total + jnp.where(second, 2 * p + 1, 0)], k0)
            c0 = cells[pl.ds(k0, 1), :]
            c1 = jnp.where(second, cells[pl.ds(k1, 1), :], -1)
            onehot = (site == jnp.concatenate([c0, c1], axis=1)).astype(F32).astype(BF)
            o0, o1 = owner[k0], owner[k1]
            j = jnp.concatenate([jacobian[o0], jacobian[o1]], axis=1).astype(F32)
            columns = jnp.dot(state[f], onehot, preferred_element_type=F32)
            model = jnp.sum(j * columns, axis=0, keepdims=True)
            value, precision = j[levels : levels + 1], j[levels + 1 : levels + 2]
            res = precision * (model - value)
            residual[pl.ds(o0, 1), :] = res[:, :LANES]

            @pl.when(second)
            def _():
                residual[pl.ds(o1, 1), :] = res[:, LANES:]

            adjoint = (j * res).astype(BF)
            acc[...] += lax.dot_general(onehot, adjoint, NT, preferred_element_type=F32)
            return 0

        lax.fori_loop(0, (found + 1) // 2, two, 0)
        vh, vl = split(vert[f])
        fh, fl = split(acc[...])
        out = jnp.dot(fh, vh, preferred_element_type=F32)
        out += jnp.dot(fl, vh, preferred_element_type=F32)
        out += jnp.dot(fh, vl, preferred_element_type=F32)
        lift[f] = out[:, :LANES]
        if f == 0:
            lift[fields] = out[:, LANES:]
        else:
            lift[fields] += out[:, LANES:]

    tap = [taps[t] for t in range(2 * HALO + 1)]
    row = lax.broadcasted_iota(jnp.int32, (blocks, rows, LANES), 1)

    def one(i, _):
        x = lift[:, pl.ds(pl.multiple_of(i * rows, 8), rows), :]
        inside = tap[HALO] * x
        beyond = jnp.zeros_like(inside)
        for s in range(1, HALO + 1):
            up = pltpu.roll(tap[HALO - s] * x, rows - s, 1)
            down = pltpu.roll(tap[HALO + s] * x, s, 1)
            up_out, down_out = row >= rows - s, row < s
            inside += jnp.where(up_out, 0.0, up) + jnp.where(down_out, 0.0, down)
            beyond += jnp.where(up_out, up, 0.0) + jnp.where(down_out, down, 0.0)
        at = step_rows(i, per)
        spread[at, :] = inside.reshape(per, LANES)
        outward[at, :] = beyond.reshape(per, LANES)
        return 0

    lax.fori_loop(0, LANES, one, 0, unroll=2)
    pack_halo(outward, low, high, fields, rows)


def adjoint_kernel(fields, rows, spread, low, high, a_t, g_t, u_t, ends, halo, pass_t):
    per = (fields + 1) * rows
    unpack_halo(low, high, halo, fields, rows)
    row = lax.broadcasted_iota(jnp.int32, (per, LANES), 0) % rows
    edge = (row < HALO) | (row >= rows - HALO)

    def east(i, q):
        at = step_rows(i, per)
        t = spread[at, :] + jnp.where(edge, halo[at, :], 0.0) + q
        pass_t[at, :] = g_t[at, :] * t
        return a_t[at, :] * t

    zero = jnp.zeros((per, LANES), F32)
    ends[0] = lax.fori_loop(0, LANES, east, zero, unroll=4)

    def west(k, p):
        at = step_rows(LANES - 1 - k, per)
        t = pass_t[at, :] + p
        u_t[at, :] = g_t[at, :] * t
        return a_t[at, :] * t

    ends[1] = lax.fori_loop(0, LANES, west, zero, unroll=4)


def gradient_kernel(
    fields, levels, rows, count, me, before, gathered, u_t, gq_t, gp_t, control, gradient, full
):
    per = (fields + 1) * rows
    over, room = levels - LANES, LANES // fields
    east_in, west_in = solve_sectors(
        me[0],
        [before[s, 0] for s in range(count)],
        [gathered[s, 0] for s in range(count)],
        [before[s, 3] for s in range(count)],
        [gathered[s, 1] for s in range(count)],
    )

    def one(i, _):
        at = step_rows(i, per)
        full[at, :] = u_t[at, :] + gq_t[at, :] * east_in + gp_t[at, :] * west_in
        return 0

    lax.fori_loop(0, LANES, one, 0, unroll=8)
    for j in range(rows):
        for f in range(fields):
            at = pl.ds(f * levels * rows + j, LANES, stride=rows)
            tile = full[pl.ds(f * rows + j, LANES, stride=per), :].T
            gradient[at, :] = control[at, :] + tile
        rest = full[pl.ds(fields * rows + j, LANES, stride=per), :].T
        for f in range(fields):
            at = pl.ds((f * levels + LANES) * rows + j, over, stride=rows)
            gradient[at, :] = control[at, :] + rest[f * room : f * room + over]


def local(
    control, smoothing, lat_taps, vert_corr, obs_cell, obs_field, obs_count, obs_owner,
    obs_jacobian, obs_value, obs_precision,
):
    fields, levels, rows, longitudes = control.shape
    blocks = fields + 1
    per = blocks * rows
    over, room = levels - LANES, LANES // fields
    count = lax.axis_size("lon")
    both = ("lon", "lat")
    total, slots = obs_cell.shape[1:]
    padded = -(-(levels + 2) // 16) * 16
    lines = longitudes * per
    line = sds((lines, LANES))

    spare = jnp.zeros((padded - levels - 2, total, slots), BF)
    sent = jnp.concatenate([obs_jacobian[0], obs_value, obs_precision, spare], axis=0)
    jacobian = lax.all_to_all(
        jnp.transpose(sent, (1, 0, 2)), both, split_axis=0, concat_axis=0, tiled=True
    )

    me = lax.axis_index("lon").astype(jnp.int32).reshape(1)
    wide = jnp.broadcast_to(
        jnp.transpose(lat_taps, (1, 0, 2))[..., None], (2 * HALO + 1, fields, rows, LANES)
    )
    rest = jnp.repeat(jnp.transpose(lat_taps, (1, 2, 0)), room, axis=2)[:, None]
    taps = jnp.concatenate([wide, rest], axis=1)
    vert = jnp.zeros((fields, padded, 2 * LANES), F32)
    vert = vert.at[:, :levels, :LANES].set(vert_corr[:, :, :LANES])
    for f in range(fields):
        begin = LANES + f * room
        vert = vert.at[f, :levels, begin : begin + over].set(vert_corr[f, :, LANES:])
    live = jnp.arange(slots, dtype=jnp.int32)[None, :] < obs_count[0][:, None]
    cells = jnp.where(live, obs_cell[0] % LANES * rows + obs_cell[0] // LANES, -1)

    flat_control = control.reshape(fields * levels * rows, longitudes)
    flat_smoothing = smoothing.reshape(fields * levels * rows, longitudes)
    sizes = (fields, levels, rows)
    tiles = pltpu.VMEM((lines, LANES), F32)
    a_t, g_t, w0_t, w1_t, s_t, gq_t, gp_t, ends = pl.pallas_call(
        functools.partial(filter_kernel, *sizes),
        out_shape=[line] * 7 + [sds((4, per, LANES))],
        in_specs=[VMEM] * 2,
        out_specs=[VMEM] * 8,
        scratch_shapes=[tiles] * 3 + [pltpu.VMEM((rows, LANES, LANES), F32)],
        compiler_params=params(40),
        name="filter_local",
    )(flat_control, flat_smoothing)
    gathered = lax.all_gather(ends, "lon")

    halo_shape = sds((blocks, HALO, longitudes, LANES), BF)
    western, low, high = pl.pallas_call(
        functools.partial(western_kernel, fields, rows, count),
        out_shape=[line, halo_shape, halo_shape],
        in_specs=[SMEM] + [VMEM] * 4,
        out_specs=[VMEM] * 3,
        compiler_params=params(24),
        name="western",
    )(me, gathered, w0_t, w1_t, s_t)

    bands = lax.axis_size("lat")
    up = [(i, i + 1) for i in range(bands - 1)]
    down = [(i + 1, i) for i in range(bands - 1)]
    after = lax.ppermute(low, "lat", down)
    before = lax.ppermute(high, "lat", up)
    state = pl.pallas_call(
        functools.partial(state_kernel, fields, rows),
        out_shape=sds((fields, padded, rows * longitudes), BF),
        in_specs=[VMEM] * 5,
        out_specs=VMEM,
        scratch_shapes=[tiles] + [pltpu.VMEM((blocks, rows * longitudes, LANES), BF)] * 2,
        compiler_params=params(32),
        name="state",
    )(western, after, before, taps, vert)

    residual, spread, low, high = pl.pallas_call(
        functools.partial(obs_kernel, *sizes),
        out_shape=[sds((total, slots)), line, halo_shape, halo_shape],
        in_specs=[SMEM] * 2 + [VMEM] * 5,
        out_specs=[VMEM] * 4,
        scratch_shapes=[
            pltpu.SMEM((fields * total + 1,), jnp.int32),
            pltpu.SMEM((fields,), jnp.int32),
            pltpu.VMEM((rows * longitudes, padded), F32),
            pltpu.VMEM((blocks, rows * longitudes, LANES), F32),
            tiles,
        ],
        compiler_params=params(48),
        name="observe",
    )(obs_field[0], obs_owner[0], cells, state, jacobian, taps, vert)
    returned = lax.all_to_all(residual, both, split_axis=0, concat_axis=0, tiled=True)

    from_before = lax.ppermute(low, "lat", up)
    from_after = lax.ppermute(high, "lat", down)
    u_t, ends = pl.pallas_call(
        functools.partial(adjoint_kernel, fields, rows),
        out_shape=[line, sds((2, per, LANES))],
        in_specs=[VMEM] * 5,
        out_specs=[VMEM] * 2,
        scratch_shapes=[tiles] * 2,
        compiler_params=params(24),
        name="adjoint_local",
    )(spread, from_before, from_after, a_t, g_t)
    gathered_back = lax.all_gather(ends, "lon")
    gradient = pl.pallas_call(
        functools.partial(gradient_kernel, *sizes, count),
        out_shape=sds(flat_control.shape),
        in_specs=[SMEM] + [VMEM] * 6,
        out_specs=VMEM,
        scratch_shapes=[tiles],
        compiler_params=params(24),
        name="gradient",
    )(me, gathered, gathered_back, u_t, gq_t, gp_t, flat_control)
    return gradient.reshape(control.shape), returned[None]


def solution(mesh):
    return jax.shard_map(
        local,
        mesh=mesh,
        in_specs=(
            P(None, None, "lat", "lon"),
            P(None, None, "lat", "lon"),
            P(None, None, "lat"),
            P(),
            P(("lon", "lat"), None, None),
            P(("lon", "lat"), None),
            P(("lon", "lat"), None),
            P(("lon", "lat"), None),
            P(("lon", "lat"), None, None, None),
            P(("lon", "lat"), None, None),
            P(("lon", "lat"), None, None),
        ),
        out_specs=(P(None, None, "lat", "lon"), P(("lon", "lat"), None, None)),
        check_vma=False,
    )
```

profile of v0, /device:TPU:0, one launch (start us, length us, event | category | flops | bytes accessed | tf_op | source)
XLA Modules:
  0.0 130.6 jit_solution(17372577024496712779)
XLA Ops:
  0.6 1.7 %copy.38 = bf16[1,137,32,128]{3,1,2,0:T(8,128)(2,1)S(1)} copy(bf16[1,137,32,128]{3,2,1,0:T(8,128)(2,1)} %param.29) | data formatting | bytes 2244608 | tf_op args[8]
  3.8 1.4 %maximum_bitcast_fusion = bf16[32,144,128]{2,1,0:T(8,128)(2,1)} fusion(bf16[1,32,128]{2,0,1:T(2,128)(2,1)S(1)} %copy.30, bf16[1,32,128]{2,0,1:T(2,128)(2,1)S(1)} %copy.29, bf16[137,32,128]{2,0,1:T(8,128)(2,1)S(1)} %bitcast.49, bf16[144]{0:T(256)(128)(2,1)S(1)} %pad.24.clone), kind=kLoop, calls=%fused_computation | loop fusion | flops 4718592 | bytes 2318624 | tf_op jit(solution)/shard_map/transpose | solution.py:340
  5.2 7.4 %all-to-all-start = ((bf16[32,144,128]{2,1,0:T(8,128)(2,1)}), bf16[32,144,128]{2,1,0:T(8,128)(2,1)}, u32[]{:S(2)}, u32[]{:S(2)}) async-start(bf16[32,144,128]{2,1,0:T(8,128)(2,1)} %maximum_bitcast_fusion), calls=%async_computation | async-start | bytes 2359296 | tf_op jit(solution)/shard_map/all_to_all | solution.py:339
  12.7 1.6 %copy-done.14 = f32[4,137,8,128]{3,2,1,0:T(8,128)S(1)} copy-done((f32[4,137,8,128]{3,2,1,0:T(8,128)S(1)}, f32[4,137,8,128]{3,2,1,0:T(8,128)}, u32[]{:S(2)}) %copy-start.14) | copy-done | bytes 2244632
  14.3 8.2 %filter_local.1 = (f32[5120,128]{1,0:T(8,128)S(1)}, f32[5120,128]{1,0:T(8,128)S(1)}, f32[5120,128]{1,0:T(8,128)S(1)}, f32[5120,128]{1,0:T(8,128)}, f32[5120,128]...) custom-call(f32[4384,128]{1,0:T(8,128)S(1)} %bitcast.40, f32[4384,128]{1,0:T(8,128)S(1)} %bitcast.44), custom_call_target="tpu_custom_call" | custom-call | tf_op jit(solution)/shard_map/filter_local/pallas_call | solution.py:361
  22.5 11.4 %all-gather = f32[32,40,128]{2,1,0:T(8,128)S(1)} all-gather(f32[4,40,128]{2,1,0:T(8,128)S(1)} %get-tuple-element.79), channel_id=2, replica_groups=mesh['lon'=8,'lat'=4] {'lon'}, dimensions={0}, use_global_device_ids=true | all-gather | bytes 737280 | tf_op jit(solution)/shard_map/all_gather | solution.py:370
  33.9 1.7 %copy-done.8 = f32[5120,128]{1,0:T(8,128)S(1)} copy-done((f32[5120,128]{1,0:T(8,128)S(1)}, f32[5120,128]{1,0:T(8,128)}, u32[]{:S(2)}) %copy-start.8) | copy-done | bytes 2621464
  35.6 1.7 %copy-done.9 = f32[5120,128]{1,0:T(8,128)S(1)} copy-done((f32[5120,128]{1,0:T(8,128)S(1)}, f32[5120,128]{1,0:T(8,128)}, u32[]{:S(2)}) %copy-start.9) | copy-done | bytes 2621464
  37.4 1.5 %western.1 = (f32[5120,128]{1,0:T(8,128)S(1)}, bf16[5,2,128,128]{3,2,1,0:T(8,128)(2,1)}, bf16[5,2,128,128]{3,2,1,0:T(8,128)(2,1)}) custom-call(s32[1]{0:T(128)} %bitcast.me, f32[8,4,40,128]{3,2,1,0:T(8,128)S(1)} %bitcast.42, f32[5120,128]{1,0:T(8,128)S(1)} %get-tuple-element.80.w0_t, f32[5120,128]{1,0:T(8,128)S(1)} %copy-done.8, f32[5120,128]{1,0:T(8,128)S(1)} %copy-done.9), custom_call_target="tpu_custom_call" | custom-call | tf_op jit(solution)/shard_map/western/pallas_call | solution.py:373
  38.9 1.6 %copy-done.10 = f32[5120,128]{1,0:T(8,128)} copy-done((f32[5120,128]{1,0:T(8,128)}, f32[5120,128]{1,0:T(8,128)S(1)}, u32[]{:S(2)}) %copy-start.10) | copy-done | bytes 2621464
  40.5 1.4 %collective-permute-start = (bf16[5,2,128,128]{3,2,1,0:T(8,128)(2,1)}, bf16[5,2,128,128]{3,2,1,0:T(8,128)(2,1)}, u32[]{:S(2)}, u32[]{:S(2)}) collective-permute-start(bf16[5,2,128,128]{3,2,1,0:T(8,128)(2,1)} %get-tuple-element.84), channel_id=1, source_target_pairs={{1,0},{2,1},{3,2},{5,4},{6,5},{7,6},{9,8},{10,9},{11,10},{13,12},{... | collective-permute-start | bytes 983048 | tf_op jit(solution)/shard_map/ppermute | solution.py:385
  41.9 6.2 %collective-permute-start.1 = (bf16[5,2,128,128]{3,2,1,0:T(8,128)(2,1)}, bf16[5,2,128,128]{3,2,1,0:T(8,128)(2,1)}, u32[]{:S(2)}, u32[]{:S(2)}) collective-permute-start(bf16[5,2,128,128]{3,2,1,0:T(8,128)(2,1)} %get-tuple-element.85), channel_id=1, source_target_pairs={{0,1},{1,2},{2,3},{4,5},{5,6},{6,7},{8,9},{9,10},{10,11},{12,13},{... | collective-permute-start | bytes 983048 | tf_op jit(solution)/shard_map/ppermute | solution.py:386
  49.0 0.7 copy.32
  51.9 1.0 scatter.16
  53.0 2.0 %scatter.19 = f32[4,144,256]{2,1,0:T(8,128)S(1)} dynamic-update-slice(f32[4,144,256]{2,1,0:T(8,128)S(1)} %scatter.16, f32[1,137,9]{2,1,0:T(8,128)} %copy.33, s32[]{:T(128)} %constant.176.clone.1, s32[]{:T(128)} %constant.176.clone.1, s32[]{:T(128)} %constant.178.clone.1) | dynamic-update-slice | bytes 9868 | tf_op jit(solution)/shard_map/scatter | solution.py:353
  55.0 2.4 %scatter.20 = f32[4,144,256]{2,1,0:T(8,128)S(1)} dynamic-update-slice(f32[4,144,256]{2,1,0:T(8,128)S(1)} %scatter.19, f32[1,137,9]{2,1,0:T(8,128)} %copy.34, s32[]{:T(128)} %constant.180.clone.1, s32[]{:T(128)} %constant.176.clone.1, s32[]{:T(128)} %constant.184.clone.1) | dynamic-update-slice | bytes 9868 | tf_op jit(solution)/shard_map/scatter | solution.py:353
  57.4 2.4 %scatter.21 = f32[4,144,256]{2,1,0:T(8,128)S(1)} dynamic-update-slice(f32[4,144,256]{2,1,0:T(8,128)S(1)} %scatter.20, f32[1,137,9]{2,1,0:T(8,128)} %copy.35, s32[]{:T(128)} %constant.185.clone.1, s32[]{:T(128)} %constant.176.clone.1, s32[]{:T(128)} %constant.186.clone.1) | dynamic-update-slice | bytes 9868 | tf_op jit(solution)/shard_map/scatter | solution.py:353
  59.7 2.4 %scatter.24.vert = f32[4,144,256]{2,1,0:T(8,128)S(1)} dynamic-update-slice(f32[4,144,256]{2,1,0:T(8,128)S(1)} %scatter.21, f32[1,137,9]{2,1,0:T(8,128)} %copy.36, s32[]{:T(128)} %constant.187.clone.1, s32[]{:T(128)} %constant.176.clone.1, s32[]{:T(128)} %constant.188.clone.1) | dynamic-update-slice | bytes 9868 | tf_op jit(solution)/shard_map/scatter | solution.py:353
  62.3 1.7 %copy-done.11 = f32[5120,128]{1,0:T(8,128)S(1)} copy-done((f32[5120,128]{1,0:T(8,128)S(1)}, f32[5120,128]{1,0:T(8,128)}, u32[]{:S(2)}) %copy-start.11) | copy-done | bytes 2621464
  64.1 5.6 %state.1 = bf16[4,144,1024]{2,1,0:T(8,128)(2,1)S(1)} custom-call(f32[5120,128]{1,0:T(8,128)S(1)} %copy-done.11, bf16[5,2,128,128]{3,2,1,0:T(8,128)(2,1)} %collective-permute-done.low, bf16[5,2,128,128]{3,2,1,0:T(8,128)(2,1)} %collective-permute-done.1.high, f32[5,5,8,128]{3,2,1,0:T(8,128)S(1)} %pad_maximum_fusion.taps, f32[4,144,256]{2,1,0:T(8,128)S(1)} %scatter.24.vert), custom_call_target="tpu_custom_call" | custom-call | tf_op jit(solution)/shard_map/state/pallas_call | solution.py:387
  69.6 1.0 copy-done.1
  71.3 1.3 copy-done.2
  72.6 0.9 copy-done.16
  73.5 20.0 %observe.1 = (f32[32,128]{1,0:T(8,128)S(1)}, f32[5120,128]{1,0:T(8,128)}, bf16[5,2,128,128]{3,2,1,0:T(8,128)(2,1)S(1)}, bf16[5,2,128,128]{3,2,1,0:T(8,128)(2,1)S(1)}) custom-call(s32[32]{0:T(128)S(1)} %bitcast.47, s32[32]{0:T(128)S(1)} %bitcast.48, s32[32,128]{1,0:T(8,128)S(1)} %fusion.2.cells, bf16[4,144,1024]{2,1,0:T(8,128)(2,1)S(1)} %copy-done.2, ...), custom_call_target="tpu_custom_call" | custom-call | tf_op jit(solution)/shard_map/observe/pallas_call | solution.py:397
  93.5 3.9 %collective-permute-start.2 = (bf16[5,2,128,128]{3,2,1,0:T(8,128)(2,1)S(1)}, bf16[5,2,128,128]{3,2,1,0:T(8,128)(2,1)S(1)}, u32[]{:S(2)}, u32[]{:S(2)}) collective-permute-start(bf16[5,2,128,128]{3,2,1,0:T(8,128)(2,1)S(1)} %get-tuple-element.87), channel_id=1, source_target_pairs={{0,1},{1,2},{2,3},{4,5},{5,6},{6,7},{8,9},{9,10},{10,11},{12,13},{... | collective-permute-start | bytes 983048 | tf_op jit(solution)/shard_map/ppermute | solution.py:414
  97.4 1.3 collective-permute-start.3
  98.7 13.9 %all_to_all.14 = f32[32,1,128]{2,1,0:T(1,128)S(1)} all-to-all(f32[32,1,128]{2,1,0:T(1,128)S(1)} %bitcast.46), channel_id=1, replica_groups=mesh['lon'=8,'lat'=4] {'lon','lat'}, dimensions={0} | all-to-all | bytes 32768 | tf_op jit(solution)/shard_map/all_to_all | solution.py:412
  112.6 1.7 %copy-done.6 = f32[5120,128]{1,0:T(8,128)S(1)} copy-done((f32[5120,128]{1,0:T(8,128)S(1)}, f32[5120,128]{1,0:T(8,128)}, u32[]{:S(2)}) %copy-start.6) | copy-done | bytes 2621464
  114.4 1.7 %copy-done.7 = f32[5120,128]{1,0:T(8,128)S(1)} copy-done((f32[5120,128]{1,0:T(8,128)S(1)}, f32[5120,128]{1,0:T(8,128)}, u32[]{:S(2)}) %copy-start.7) | copy-done | bytes 2621464
  116.1 1.6 %adjoint_local.1 = (f32[5120,128]{1,0:T(8,128)S(1)}, f32[2,40,128]{2,1,0:T(8,128)S(1)}) custom-call(f32[5120,128]{1,0:T(8,128)S(1)} %copy-done.7, bf16[5,2,128,128]{3,2,1,0:T(8,128)(2,1)S(1)} %collective-permute-done.2.low, bf16[5,2,128,128]{3,2,1,0:T(8,128)(2,1)S(1)} %collective-permute-done.3.high, f32[5120,128]{1,0:T(8,128)S(1)} %copy-done.4, ...), custom_call_target="tpu_custom_call" | custom-call | tf_op jit(solution)/shard_map/adjoint_local/pallas_call | solution.py:416
  117.8 9.4 %all-gather.1 = f32[16,40,128]{2,1,0:T(8,128)S(1)} all-gather(f32[2,40,128]{2,1,0:T(8,128)S(1)} %get-tuple-element.91), channel_id=3, replica_groups=mesh['lon'=8,'lat'=4] {'lon'}, dimensions={0}, use_global_device_ids=true | all-gather | bytes 368640 | tf_op jit(solution)/shard_map/all_gather | solution.py:425
  127.2 2.9 %gradient.1 = f32[4384,128]{1,0:T(8,128)} custom-call(s32[1]{0:T(128)} %bitcast.me, f32[8,4,40,128]{3,2,1,0:T(8,128)S(1)} %bitcast.43, f32[8,2,40,128]{3,2,1,0:T(8,128)S(1)} %bitcast.45, f32[5120,128]{1,0:T(8,128)S(1)} %get-tuple-element.92.u_t, f32[5120,128]{1,0:T(8,128)S(1)} %copy-done.12, f32[5120,128]{1,0:T(8,128)S(1)} %copy-done.13, ...), custom_call_target="tpu_custom_call" | custom-call | tf_op jit(solution)/shard_map/gradient/pallas_call | solution.py:426
  (59 shorter events, 6.0 us)
Async XLA Ops:
  3.8 8.8 %copy-start = (f32[4,137,8,128]{3,2,1,0:T(8,128)S(1)}, f32[4,137,8,128]{3,2,1,0:T(8,128)}, u32[]{:S(2)}) copy-start(f32[4,137,8,128]{3,2,1,0:T(8,128)} %param.21) | copy-start | bytes 6733828
  5.2 66.1 %all-to-all-start = ((bf16[32,144,128]{2,1,0:T(8,128)(2,1)}), bf16[32,144,128]{2,1,0:T(8,128)(2,1)}, u32[]{:S(2)}, u32[]{:S(2)}) async-start(bf16[32,144,128]{2,1,0:T(8,128)(2,1)} %maximum_bitcast_fusion), calls=%async_computation | async-start | bytes 2359296 | tf_op jit(solution)/shard_map/all_to_all | solution.py:339
  12.7 1.6 %copy-start.14 = (f32[4,137,8,128]{3,2,1,0:T(8,128)S(1)}, f32[4,137,8,128]{3,2,1,0:T(8,128)}, u32[]{:S(2)}) copy-start(f32[4,137,8,128]{3,2,1,0:T(8,128)} %param.22) | copy-start | bytes 6733828
  22.5 16.5 %copy-start.3 = (f32[5120,128]{1,0:T(8,128)}, f32[5120,128]{1,0:T(8,128)S(1)}, u32[]{:S(2)}) copy-start(f32[5120,128]{1,0:T(8,128)S(1)} %get-tuple-element.89.a_t) | copy-start | bytes 7864324
  22.5 16.5 %copy-start.5 = (f32[5120,128]{1,0:T(8,128)}, f32[5120,128]{1,0:T(8,128)S(1)}, u32[]{:S(2)}) copy-start(f32[5120,128]{1,0:T(8,128)S(1)} %get-tuple-element.90.g_t) | copy-start | bytes 7864324
  33.9 1.7 %copy-start.8 = (f32[5120,128]{1,0:T(8,128)S(1)}, f32[5120,128]{1,0:T(8,128)}, u32[]{:S(2)}) copy-start(f32[5120,128]{1,0:T(8,128)} %get-tuple-element.81.w1_t) | copy-start | bytes 7864324
  35.6 1.7 %copy-start.9 = (f32[5120,128]{1,0:T(8,128)S(1)}, f32[5120,128]{1,0:T(8,128)}, u32[]{:S(2)}) copy-start(f32[5120,128]{1,0:T(8,128)} %get-tuple-element.82.s_t) | copy-start | bytes 7864324
  37.4 10.8 %copy-start.19 = (f32[4,137,137]{2,0,1:T(4,128)S(1)}, f32[4,137,137]{2,0,1:T(4,128)}, u32[]{:S(2)}) copy-start(f32[4,137,137]{2,0,1:T(4,128)} %param.24) | copy-start | bytes 900916
  37.4 11.6 %slice-start = ((f32[4,137,137]{2,0,1:T(4,128)}), f32[4,137,128]{2,0,1:T(4,128)S(1)}, s32[]{:S(2)}) async-start(f32[4,137,137]{2,0,1:T(4,128)} %param.24), calls=%async_computation.2 | async-start | bytes 561152 | tf_op jit(solution)/shard_map/slice | solution.py:350
  37.4 14.2 %copy-start.20 = (f32[4,5,8]{2,0,1:T(4,128)S(1)}, f32[4,5,8]{2,0,1:T(4,128)}, u32[]{:S(2)}) copy-start(f32[4,5,8]{2,0,1:T(4,128)} %param.23) | copy-start | bytes 1924
  38.9 1.6 %copy-start.10 = (f32[5120,128]{1,0:T(8,128)}, f32[5120,128]{1,0:T(8,128)S(1)}, u32[]{:S(2)}) copy-start(f32[5120,128]{1,0:T(8,128)S(1)} %get-tuple-element.83.western) | copy-start | bytes 7864324
  40.5 21.7 %copy-start.21 = (s32[1,32,128]{2,1,0:T(8,128)S(1)}, s32[1,32,128]{2,1,0:T(8,128)}, u32[]{:S(2)}) copy-start(s32[1,32,128]{2,1,0:T(8,128)} %param.25) | copy-start | bytes 49156
  40.5 21.7 %copy-start.22 = (s32[1,32]{1,0:T(1,128)S(1)}, s32[1,32]{1,0:T(1,128)}, u32[]{:S(2)}) copy-start(s32[1,32]{1,0:T(1,128)} %param.27) | copy-start | bytes 388
  40.5 21.8 %collective-permute-start = (bf16[5,2,128,128]{3,2,1,0:T(8,128)(2,1)}, bf16[5,2,128,128]{3,2,1,0:T(8,128)(2,1)}, u32[]{:S(2)}, u32[]{:S(2)}) collective-permute-start(bf16[5,2,128,128]{3,2,1,0:T(8,128)(2,1)} %get-tuple-element.84), channel_id=1, source_target_pairs={{1,0},{2,1},{3,2},{5,4},{6,5},{7,6},{9,8},{10,9},{11,10},{13,12},{... | collective-permute-start | bytes 983048 | tf_op jit(solution)/shard_map/ppermute | solution.py:385
  41.9 20.4 %collective-permute-start.1 = (bf16[5,2,128,128]{3,2,1,0:T(8,128)(2,1)}, bf16[5,2,128,128]{3,2,1,0:T(8,128)(2,1)}, u32[]{:S(2)}, u32[]{:S(2)}) collective-permute-start(bf16[5,2,128,128]{3,2,1,0:T(8,128)(2,1)} %get-tuple-element.85), channel_id=1, source_target_pairs={{0,1},{1,2},{2,3},{4,5},{5,6},{6,7},{8,9},{9,10},{10,11},{12,13},{... | collective-permute-start | bytes 983048 | tf_op jit(solution)/shard_map/ppermute | solution.py:386
  62.3 1.7 %copy-start.11 = (f32[5120,128]{1,0:T(8,128)S(1)}, f32[5120,128]{1,0:T(8,128)}, u32[]{:S(2)}) copy-start(f32[5120,128]{1,0:T(8,128)} %copy-done.10) | copy-start | bytes 7864324
  64.1 7.2 %copy-start.17 = (s32[1,32]{1,0:T(1,128)S(1)}, s32[1,32]{1,0:T(1,128)}, u32[]{:S(2)}) copy-start(s32[1,32]{1,0:T(1,128)} %param.26) | copy-start | bytes 388
  64.1 7.2 %copy-start.18 = (s32[1,32]{1,0:T(1,128)S(1)}, s32[1,32]{1,0:T(1,128)}, u32[]{:S(2)}) copy-start(s32[1,32]{1,0:T(1,128)} %param.28) | copy-start | bytes 388
  69.6 1.0 copy-start.1
  70.6 0.6 copy-start.15
  71.3 1.3 copy-start.2
  72.6 0.9 copy-start.16
  73.5 39.2 %copy-start.4 = (f32[5120,128]{1,0:T(8,128)S(1)}, f32[5120,128]{1,0:T(8,128)}, u32[]{:S(2)}) copy-start(f32[5120,128]{1,0:T(8,128)} %copy-done.3) | copy-start | bytes 7864324
  93.5 19.2 %collective-permute-start.2 = (bf16[5,2,128,128]{3,2,1,0:T(8,128)(2,1)S(1)}, bf16[5,2,128,128]{3,2,1,0:T(8,128)(2,1)S(1)}, u32[]{:S(2)}, u32[]{:S(2)}) collective-permute-start(bf16[5,2,128,128]{3,2,1,0:T(8,128)(2,1)S(1)} %get-tuple-element.87), channel_id=1, source_target_pairs={{0,1},{1,2},{2,3},{4,5},{5,6},{6,7},{8,9},{9,10},{10,11},{12,13},{... | collective-permute-start | bytes 983048 | tf_op jit(solution)/shard_map/ppermute | solution.py:414
  97.4 15.2 %collective-permute-start.3 = (bf16[5,2,128,128]{3,2,1,0:T(8,128)(2,1)S(1)}, bf16[5,2,128,128]{3,2,1,0:T(8,128)(2,1)S(1)}, u32[]{:S(2)}, u32[]{:S(2)}) collective-permute-start(bf16[5,2,128,128]{3,2,1,0:T(8,128)(2,1)S(1)} %get-tuple-element.88), channel_id=1, source_target_pairs={{1,0},{2,1},{3,2},{5,4},{6,5},{7,6},{9,8},{10,9},{11,10},{13,12},{... | collective-permute-start | bytes 983048 | tf_op jit(solution)/shard_map/ppermute | solution.py:415
  112.6 1.7 %copy-start.6 = (f32[5120,128]{1,0:T(8,128)S(1)}, f32[5120,128]{1,0:T(8,128)}, u32[]{:S(2)}) copy-start(f32[5120,128]{1,0:T(8,128)} %copy-done.5) | copy-start | bytes 7864324
  114.4 1.7 %copy-start.7 = (f32[5120,128]{1,0:T(8,128)S(1)}, f32[5120,128]{1,0:T(8,128)}, u32[]{:S(2)}) copy-start(f32[5120,128]{1,0:T(8,128)} %get-tuple-element.86.spread) | copy-start | bytes 7864324
  116.1 11.0 %copy-start.12 = (f32[5120,128]{1,0:T(8,128)S(1)}, f32[5120,128]{1,0:T(8,128)}, u32[]{:S(2)}) copy-start(f32[5120,128]{1,0:T(8,128)} %get-tuple-element.93.gq_t) | copy-start | bytes 7864324
  116.1 11.0 %copy-start.13 = (f32[5120,128]{1,0:T(8,128)S(1)}, f32[5120,128]{1,0:T(8,128)}, u32[]{:S(2)}) copy-start(f32[5120,128]{1,0:T(8,128)} %get-tuple-element.94.gp_t) | copy-start | bytes 7864324
where the time goes:
time: 132 us; the launch traced here: 131 us
  Pallas kernels  39.8 us (30%)
  blocking collectives  34.8 us (26%)
  local copies, waits for them, and re-layouts  33.5 us (25%)
  starting transfers between devices  20.2 us (15%)
  other arithmetic  1.47 us (1%)
    unnamed x55, local copies, waits for them, and re-layouts  22.8 us
    pallas_call x1, Pallas kernels, local(): pl.pallas_call(functools.partial(obs_kernel, *sizes), out_shape=[sds((tot...  20 us
    all_to_all x1, blocking collectives, local(): lax.all_to_all(residual, both, split_axis=0, concat_axis=0, tiled=True)  13.9 us
    all_gather x1, blocking collectives, local(): gathered = lax.all_gather(ends, 'lon')  11.4 us
    all_gather x1, blocking collectives, local(): gathered_back = lax.all_gather(ends, 'lon')  9.38 us
    scatter x4, local copies, waits for them, and re-layouts, local(): vert = vert.at[f, :levels, begin:begin + over].set(vert_corr[f, :, LANES:])  9.13 us
    pallas_call x1, Pallas kernels, local(): pl.pallas_call(functools.partial(filter_kernel, *sizes), out_shape=[line]...  8.15 us
    all_to_all x1, starting transfers between devices, local(): lax.all_to_all(jnp.transpose(sent, (1, 0, 2)), both, split_axis=0, concat...  7.41 us
  transfers between devices with their start and end apart: 5, of which 0 were waited for; matrix products, arithmetic and copies ran while one was open for 11% of the time, Pallas kernels for 12%

commit v1 on v0

v1 whole, which is shorter than its diff:
```python
import functools

import jax
import jax.numpy as jnp
from jax import lax
from jax.experimental import pallas as pl
from jax.experimental.pallas import tpu as pltpu
from jax.sharding import PartitionSpec as P

LANES = 128
HALO = 2
FAR_MIB = 60
CELLS = 256
GROUP = 4
BF = jnp.bfloat16
F32 = jnp.float32
NT = (((1,), (1,)), ((), ()))
TN = (((0,), (0,)), ((), ()))
VMEM = pl.BlockSpec(memory_space=pltpu.VMEM)
SMEM = pl.BlockSpec(memory_space=pltpu.SMEM)
HBM = pl.BlockSpec(memory_space=pltpu.HBM)


def params(mib):
    return pltpu.CompilerParams(vmem_limit_bytes=mib * 1024 * 1024)


def cost(microseconds):
    return pl.CostEstimate(
        flops=0, bytes_accessed=int(microseconds * 3.5e6), transcendentals=0
    )


def sds(shape, dtype=F32):
    return jax.ShapeDtypeStruct(shape, dtype)


def split(x):
    high = x.astype(BF)
    return high, (x - high.astype(F32)).astype(BF)


def step_rows(i, per):
    return pl.ds(pl.multiple_of(i * per, 8), per)


def solve_sectors(me, products, ends, cross, backs):
    count = len(products)
    whole, state = products[0], ends[0]
    for s in range(1, count):
        state = products[s] * state + ends[s]
        whole = whole * products[s]
    gap = 1.0 - whole
    east = state / gap
    east_in = jnp.zeros_like(east)
    turned = []
    for s in range(count):
        east_in = jnp.where(me == s, east, east_in)
        turned.append(backs[s] + cross[s] * east)
        east = products[s] * east + ends[s]
    state = turned[count - 1]
    for s in range(count - 2, -1, -1):
        state = products[s] * state + turned[s]
    west = state / gap
    west_in = jnp.zeros_like(west)
    for s in range(count - 1, -1, -1):
        west_in = jnp.where(me == s, west, west_in)
        west = products[s] * west + turned[s]
    return east_in, west_in


def fetch(pairs, arrived):
    copies = [pltpu.make_async_copy(a, b, arrived.at[n]) for n, (a, b) in enumerate(pairs)]
    for copy in copies:
        copy.start()
    return copies


def pack_kernel(levels, jacobian, value, precision, sent, held, small, wide, ready, arrived, left):
    blocks, padded = sent.shape[:2]
    chunk = held.shape[2]
    copies = fetch(
        [(value, small.at[0]), (precision, small.at[1])]
        + [
            (jacobian.at[:, pl.ds(c * chunk, chunk)], held.at[c])
            for c in range(blocks // chunk)
        ],
        arrived,
    )
    spare = (padded - levels - 2) * chunk
    wide[pl.ds((levels + 2) * chunk, spare), :] = jnp.zeros((spare, LANES), F32)
    copies[0].wait()
    copies[1].wait()
    leaving = []
    for c in range(blocks // chunk):
        copies[2 + c].wait()

        def put(l, _):
            wide[pl.ds(pl.multiple_of(l * chunk, 8), chunk), :] = held[c, l].astype(F32)
            return 0

        lax.fori_loop(0, levels, put, 0, unroll=8)
        for n in range(2):
            part = small[n, pl.ds(c * chunk, chunk), :].astype(F32)
            wide[pl.ds((levels + n) * chunk, chunk), :] = part
        for k in range(chunk):
            ready[c * chunk + k] = wide[pl.ds(k, padded, stride=chunk), :].astype(BF)
        at = pl.ds(c * chunk, chunk)
        leaving += fetch([(ready.at[at], sent.at[at])], left.at[pl.ds(c, 1)])
    for copy in leaving:
        copy.wait()


def prepare_kernel(fields, levels, rows, vert, lat_taps, both, taps, wide):
    over, room = levels - LANES, LANES // fields
    wide[...] = jnp.zeros_like(wide)
    for f in range(fields):
        v = vert[:, f, :]
        wide[f, :levels, :LANES] = v[:, :LANES]
        begin = LANES + f * room
        wide[f, :levels, begin : begin + over] = v[:, LANES:]
    both[:, :, : 2 * LANES], both[:, :, 2 * LANES :] = split(wide[...])
    diagonal = lax.broadcasted_iota(jnp.int32, (rows, rows), 0) == lax.broadcasted_iota(
        jnp.int32, (rows, rows), 1
    )
    lane = lax.broadcasted_iota(jnp.int32, (rows, LANES), 1) // room
    for t in range(2 * HALO + 1):
        last = jnp.zeros((rows, LANES), F32)
        for f in range(fields):
            line = jnp.broadcast_to(lat_taps[t, f : f + 1, :], (rows, rows))
            column = jnp.sum(jnp.where(diagonal, line, 0.0), axis=1, keepdims=True)
            column = jnp.broadcast_to(column, (rows, LANES))
            taps[t, f] = column
            last = jnp.where(lane == f, column, last)
        taps[t, fields] = last


def filter_kernel(
    fields, levels, rows, control, smoothing,
    a_t, w0_t, w1_t, s_t, ends, control_v, smoothing_v, g_t, x_t, e_t, pe_t, extra, arrived,
):
    per = (fields + 1) * rows
    over, room = levels - LANES, LANES // fields
    pairs = []
    for f in range(fields):
        at = pl.ds(f * levels * rows, levels * rows)
        pairs.append((smoothing.at[at], smoothing_v.at[at]))
        pairs.append((control.at[at], control_v.at[at]))
    copies = fetch(pairs, arrived)
    extra[...] = jnp.zeros_like(extra)
    for f in range(fields):
        for n, (src, dst) in enumerate(((smoothing_v, a_t), (control_v, x_t))):
            copies[2 * f + n].wait()
            for j in range(rows):
                tile = src[pl.ds(f * levels * rows + j, LANES, stride=rows), :]
                dst[pl.ds(f * rows + j, LANES, stride=per), :] = tile.T
                extra[n, j, pl.ds(f * room, over), :] = src[
                    pl.ds((f * levels + LANES) * rows + j, over, stride=rows), :
                ]
    for j in range(rows):
        at = pl.ds(fields * rows + j, LANES, stride=per)
        a_t[at, :] = extra[0, j].T
        x_t[at, :] = extra[1, j].T

    def east(i, carry):
        e, p = carry
        at = step_rows(i, per)
        a = a_t[at, :]
        g = jnp.sqrt((1.0 - a) * (1.0 + a))
        g_t[at, :] = g
        pe_t[at, :] = p
        e = a * e + g * x_t[at, :]
        e_t[at, :] = e
        return e, p * a

    zero = jnp.zeros((per, LANES), F32)
    one = jnp.ones((per, LANES), F32)
    e, p = lax.fori_loop(0, LANES, east, (zero, one), unroll=4)

    def west(k, carry):
        w0, w1, s = carry
        at = step_rows(LANES - 1 - k, per)
        a, g = a_t[at, :], g_t[at, :]
        w0 = a * w0 + g * e_t[at, :]
        w1 = a * (w1 + g * pe_t[at, :])
        s = a * s
        w0_t[at, :] = w0
        w1_t[at, :] = w1
        s_t[at, :] = s
        return w0, w1, s

    w0, w1, _ = lax.fori_loop(0, LANES, west, (zero, zero, one), unroll=4)
    ends[0] = p
    ends[1] = e
    ends[2] = w0
    ends[3] = w1


def edges_kernel(fields, rows, count, gathered, w0_t, w1_t, s_t, low, high, entering):
    per = (fields + 1) * rows
    part = [[gathered[s, q] for s in range(count)] for q in range(4)]
    east_in, west_in = solve_sectors(lax.axis_index("lon"), part[0], part[1], part[3], part[2])
    entering[0] = east_in
    entering[1] = west_in
    for b in range(fields + 1):
        for j in range(HALO):
            to = pl.ds((b * HALO + j) * LANES, LANES)
            for first, dst in ((b * rows, low), (b * rows + rows - HALO, high)):
                n = first + j
                at = pl.ds(n, LANES, stride=per)
                line = w0_t[at, :] + w1_t[at, :] * east_in[n : n + 1]
                dst[to, :] = (line + s_t[at, :] * west_in[n : n + 1]).astype(BF)


def vertical(vert, mixed):
    padded = vert.shape[0]
    v = jnp.concatenate([vert[:, : 2 * LANES], vert[:, 2 * LANES :]], axis=0)
    high, low = split(mixed)
    out = lax.dot_general(v, high, NT, preferred_element_type=F32)
    out = out[:padded] + out[padded:]
    out += lax.dot_general(v[:padded], low, NT, preferred_element_type=F32)
    return out.astype(BF)


def interior_kernel(fields, rows, entering, w0_t, w1_t, s_t, taps, vert, state, partial, western, mixed):
    blocks = fields + 1
    per = blocks * rows
    for n in range(per):
        at = pl.ds(n, LANES, stride=per)
        line = w0_t[at, :] + w1_t[at, :] * entering[0, n : n + 1, :]
        western[n] = line + s_t[at, :] * entering[1, n : n + 1, :]
    for b in range(blocks):
        for j in range(rows):
            total = taps[HALO, b, j : j + 1, :] * western[b * rows + j]
            for t in range(2 * HALO + 1):
                if t != HALO and 0 <= j + t - HALO < rows:
                    total += taps[t, b, j : j + 1, :] * western[b * rows + j + t - HALO]
            if HALO <= j < rows - HALO:
                mixed[b, pl.ds((j - HALO) * LANES, LANES), :] = total
            else:
                partial[b, j if j < HALO else j - rows + 2 * HALO] = total
    for f in range(fields):
        for h in range(state.shape[1]):
            at = pl.ds(h * CELLS, CELLS)
            both = jnp.concatenate([mixed[f, at, :], mixed[fields, at, :]], axis=1)
            state[f, h] = vertical(vert[f], both)


def route_of(delta, bands):
    cyclic = 2 + (delta + bands) % bands
    far = jnp.where(jnp.abs(delta) == bands - 1, 3, cyclic)
    near = jnp.where(delta == 1, 1, jnp.where(delta == -1, 2, 0))
    return jnp.where(jnp.abs(delta) <= 1, near, far)


def observe_kernel(
    fields, levels, rows, bands, field, owner, live, cells,
    inner_far, partial_far, before_far, after_far, taps_far, vert_far, jacobian_far, *rest,
):
    lift_far, low_far, high_far = rest[:3]
    residuals = rest[3 : 2 + bands]
    (
        inner, partial, before, after, taps, vert, jacobian, mixed, outer, lift, low, high,
        route, order, number, acc, arrived, left,
    ) = rest[2 + bands :]
    blocks = fields + 1
    copies = fetch(
        [(after_far, after), (before_far, before), (taps_far, taps), (partial_far, partial)]
        + [(vert_far, vert), (jacobian_far, jacobian), (inner_far, inner)],
        arrived,
    )
    total = field.shape[0]
    padded = vert.shape[1]
    parts = rows * LANES // CELLS
    wide = GROUP * LANES
    sectors = total // bands
    band = lax.axis_index("lat")
    for f in range(fields):
        number[f] = 0

    def place(k, _):
        f = field[k]
        n = number[f]
        order[f * total + n] = k
        number[f] = n + 1
        return 0

    lax.fori_loop(0, total, place, 0)
    route[...] = jnp.zeros_like(route)

    for n in range(4):
        copies[n].wait()

    def beside(src, b, n):
        return src[pl.ds((b * HALO + n) * LANES, LANES), :].astype(F32)

    def tap_of(t, b, j):
        return taps[t, b, j : j + 1, :]

    end = rows - 1
    for b in range(blocks):
        above, below = [beside(before, b, n) for n in range(2)], [beside(after, b, n) for n in range(2)]
        outer_rows = (
            partial[b, 0] + tap_of(0, b, 0) * above[0] + tap_of(1, b, 0) * above[1],
            partial[b, 1] + tap_of(0, b, 1) * above[1],
            partial[b, 2] + tap_of(4, b, end - 1) * below[0],
            partial[b, 3] + tap_of(3, b, end) * below[0] + tap_of(4, b, end) * below[1],
        )
        for n, line in enumerate(outer_rows):
            mixed[b, pl.ds(n * LANES, LANES), :] = line
    copies[4].wait()
    for f in range(fields):
        for h in range(2):
            at = pl.ds(h * CELLS, CELLS)
            both = jnp.concatenate([mixed[f, at, :], mixed[fields, at, :]], axis=1)
            outer[f, h] = vertical(vert[f], both)

    copies[5].wait()
    copies[6].wait()
    site = lax.broadcasted_iota(jnp.int32, (CELLS, wide), 0)
    slot = lax.broadcasted_iota(jnp.int32, (1, LANES), 1)
    leaving = []
    for f in range(fields):
        acc[...] = jnp.zeros_like(acc)
        found = number[f]

        def group(p, _):
            known, names, places = [], [], []
            for n in range(GROUP):
                known.append(GROUP * p + n < found)
                k = order[f * total + jnp.where(known[n], GROUP * p + n, 0)]
                count = jnp.where(known[n], live[k], 0)
                c = cells[pl.ds(k, 1), :]
                places.append(jnp.where(slot < count, c, -1))
                names.append(owner[k])
            at = [route_of(w % bands - band, bands) * sectors + w // bands for w in names]
            place = jnp.concatenate(places, axis=1)
            part = place // CELLS
            onehot = (site == jnp.where(place < 0, -1, place % CELLS)).astype(F32).astype(BF)
            j = jnp.concatenate([jacobian[w] for w in names], axis=1).astype(F32)
            columns = jnp.zeros_like(j)
            state = [outer[f, 0], *(inner[f, h] for h in range(parts - 2)), outer[f, 1]]
            found_all = jnp.dot(
                jnp.concatenate(state, axis=0), onehot, preferred_element_type=F32
            )
            for h in range(parts):
                columns = jnp.where(part == h, found_all[h * padded : (h + 1) * padded], columns)
            model = jnp.sum(j * columns, axis=0, keepdims=True)
            value, precision = j[levels : levels + 1], j[levels + 1 : levels + 2]
            res = precision * (model - value)
            for n in range(GROUP):

                @pl.when(known[n])
                def _():
                    route[pl.ds(at[n], 1), :] = res[:, n * LANES : (n + 1) * LANES]

            adjoint = j * res
            adjoint = jnp.concatenate(
                [jnp.where(part == h, adjoint, 0.0).astype(BF) for h in range(parts)], axis=0
            )
            acc[...] += lax.dot_general(adjoint, onehot, NT, preferred_element_type=F32)
            return 0

        lax.fori_loop(0, (found + GROUP - 1) // GROUP, group, 0)
        for h in range(parts):
            forcing = acc[pl.ds(h * padded, padded), :].astype(BF)
            out = lax.dot_general(forcing, vert[f], TN, preferred_element_type=F32)
            out = out[:, : 2 * LANES] + out[:, 2 * LANES :]
            at = pl.ds(h * CELLS, CELLS)
            lift[f, at, :] = out[:, :LANES]
            if f == 0:
                lift[fields, at, :] = out[:, LANES:]
            else:
                lift[fields, at, :] += out[:, LANES:]
        leaving += fetch([(lift.at[f], lift_far.at[f])], left.at[pl.ds(f, 1)])
    leaving += fetch([(lift.at[fields], lift_far.at[fields])], left.at[pl.ds(fields, 1)])

    for b in range(blocks):
        def line(j):
            return lift[b, pl.ds(j * LANES, LANES), :]

        for dst, first, second in (
            (low, tap_of(3, b, end) * line(end) + tap_of(4, b, end - 1) * line(end - 1),
             tap_of(4, b, end) * line(end)),
            (high, tap_of(0, b, 0) * line(0),
             tap_of(1, b, 0) * line(0) + tap_of(0, b, 1) * line(1)),
        ):
            dst[pl.ds(b * HALO * LANES, LANES), :] = first.astype(BF)
            dst[pl.ds((b * HALO + 1) * LANES, LANES), :] = second.astype(BF)
    for n, dst in ((1, low), (2, high)):
        both = jnp.concatenate(split(route[pl.ds(n * sectors, sectors), :]), axis=0)
        dst[pl.ds(blocks * HALO * LANES, 2 * sectors), :] = both
    leaving += fetch([(low, low_far), (high, high_far)], left.at[pl.ds(blocks, 2)])
    for n, dst in enumerate(residuals):
        source = 0 if n == 0 else n + 2
        dst[...] = route[pl.ds(source * sectors, sectors), :]
    for copy in leaving:
        copy.wait()


def respond_kernel(
    fields, rows, lift_far, taps_far, a_far, a_t, g_t, gq_t, gp_t, spread, lift, taps, pe_t, arrived
):
    blocks = fields + 1
    per = blocks * rows
    copies = fetch(
        [(a_far, a_t), (taps_far, taps)] + [(lift_far.at[b], lift.at[b]) for b in range(blocks)],
        arrived,
    )

    def east(i, p):
        at = step_rows(i, per)
        a = a_t[at, :]
        g_t[at, :] = jnp.sqrt((1.0 - a) * (1.0 + a))
        pe_t[at, :] = p
        return p * a

    def west(k, carry):
        w1, s = carry
        at = step_rows(LANES - 1 - k, per)
        a, g = a_t[at, :], g_t[at, :]
        t = w1 + g * pe_t[at, :]
        gq_t[at, :] = g * t
        gp_t[at, :] = g * s
        return a * t, a * s

    one = jnp.ones((per, LANES), F32)
    copies[0].wait()
    lax.fori_loop(0, LANES, east, one, unroll=4)
    lax.fori_loop(0, LANES, west, (jnp.zeros_like(one), one), unroll=4)
    copies[1].wait()
    for b in range(blocks):
        copies[2 + b].wait()
        for m in range(rows):
            total = taps[HALO, b, m : m + 1, :] * lift[b, pl.ds(m * LANES, LANES), :]
            for t in range(2 * HALO + 1):
                j = m - t + HALO
                if t != HALO and 0 <= j < rows:
                    total += taps[t, b, j : j + 1, :] * lift[b, pl.ds(j * LANES, LANES), :]
            spread[pl.ds(b * rows + m, LANES, stride=per), :] = total


def adjoint_kernel(fields, rows, spread, low, high, a_t, g_t, *rest):
    residuals = rest[:-4]
    u_t, ends, halo, pass_t = rest[-4:]
    blocks = fields + 1
    per = blocks * rows
    sectors = residuals[0].shape[0]
    riding = blocks * HALO * LANES
    parts = [residuals[0][...]]
    for src in (low, high):
        two = src[pl.ds(riding, 2 * sectors), :].astype(F32)
        parts.append(two[:sectors] + two[sectors:])
    parts += [a[...] for a in residuals[1:]]
    for n, part in enumerate(parts):
        ends[pl.ds(2 * per + n * sectors, sectors), :] = part

    for b in range(blocks):
        for n in range(HALO):
            at = pl.ds((b * HALO + n) * LANES, LANES)
            halo[pl.ds(b * rows + n, LANES, stride=per), :] = low[at, :].astype(F32)
            last = b * rows + rows - HALO + n
            halo[pl.ds(last, LANES, stride=per), :] = high[at, :].astype(F32)
    row = lax.broadcasted_iota(jnp.int32, (per, LANES), 0) % rows
    edge = (row < HALO) | (row >= rows - HALO)

    def east(i, q):
        at = step_rows(i, per)
        t = spread[at, :] + jnp.where(edge, halo[at, :], 0.0) + q
        pass_t[at, :] = g_t[at, :] * t
        return a_t[at, :] * t

    def west(k, p):
        at = step_rows(LANES - 1 - k, per)
        t = pass_t[at, :] + p
        u_t[at, :] = g_t[at, :] * t
        return a_t[at, :] * t

    zero = jnp.zeros((per, LANES), F32)
    ends[:per] = lax.fori_loop(0, LANES, east, zero, unroll=4)
    ends[per : 2 * per] = lax.fori_loop(0, LANES, west, zero, unroll=4)


def gradient_kernel(
    fields, levels, rows, count, bands, before, gathered, u_t, gq_t, gp_t, control,
    gradient, residual, full, extra, held, arrived,
):
    per = (fields + 1) * rows
    over, room = levels - LANES, LANES // fields
    me = lax.axis_index("lon")
    east_in, west_in = solve_sectors(
        me,
        [before[s, 0] for s in range(count)],
        [gathered[s, :per] for s in range(count)],
        [before[s, 3] for s in range(count)],
        [gathered[s, per : 2 * per] for s in range(count)],
    )
    for source in range(bands):
        route = route_of(lax.axis_index("lat") - source, bands)
        for s in range(count):
            line = gathered[s, pl.ds(2 * per + route * count + me, 1), :]
            residual[pl.ds(s * bands + source, 1), :] = line

    def one(i, _):
        at = step_rows(i, per)
        full[at, :] = u_t[at, :] + gq_t[at, :] * east_in + gp_t[at, :] * west_in
        return 0

    lax.fori_loop(0, LANES, one, 0, unroll=8)
    for j in range(rows):
        extra[j] = full[pl.ds(fields * rows + j, LANES, stride=per), :].T
    copies = []
    for f in range(fields):
        for j in range(rows):
            at = pl.ds(f * levels * rows + j, LANES, stride=rows)
            tile = full[pl.ds(f * rows + j, LANES, stride=per), :].T
            held[at, :] = control[at, :] + tile
            at = pl.ds((f * levels + LANES) * rows + j, over, stride=rows)
            held[at, :] = control[at, :] + extra[j, pl.ds(f * room, over), :]
        at = pl.ds(f * levels * rows, levels * rows)
        copies += fetch([(held.at[at], gradient.at[at])], arrived.at[pl.ds(f, 1)])
    for copy in copies:
        copy.wait()


def local(
    control, smoothing, lat_taps, vert_corr, obs_cell, obs_field, obs_count, obs_owner,
    obs_jacobian, obs_value, obs_precision,
):
    fields, levels, rows, longitudes = control.shape
    blocks = fields + 1
    per = blocks * rows
    count = lax.axis_size("lon")
    both = ("lon", "lat")
    total, slots = obs_cell.shape[1:]
    padded = -(-(levels + 2) // 16) * 16
    lines = longitudes * per
    line = sds((lines, LANES))

    sent = pl.pallas_call(
        functools.partial(pack_kernel, levels),
        out_shape=sds((total, padded, slots), BF),
        in_specs=[HBM] * 3,
        out_specs=HBM,
        scratch_shapes=[
            pltpu.VMEM((total // 16, levels, 16, slots), BF),
            pltpu.VMEM((2, total, slots), BF),
            pltpu.VMEM((padded * 16, slots), F32),
            pltpu.VMEM((total, padded, slots), BF),
            pltpu.SemaphoreType.DMA((2 + total // 16,)),
            pltpu.SemaphoreType.DMA((total // 16,)),
        ],
        compiler_params=params(FAR_MIB),
        cost_estimate=cost(3),
        name="pack",
    )(obs_jacobian[0], obs_value[0], obs_precision[0])
    jacobian = lax.all_to_all(sent, both, split_axis=0, concat_axis=0, tiled=True)

    vert_shape = (fields, padded, 4 * LANES)
    vert, taps = pl.pallas_call(
        functools.partial(prepare_kernel, fields, levels, rows),
        out_shape=[sds(vert_shape, BF), sds((2 * HALO + 1, blocks, rows, LANES))],
        in_specs=[VMEM] * 2,
        out_specs=[VMEM] * 2,
        scratch_shapes=[pltpu.VMEM((fields, padded, 2 * LANES), F32)],
        compiler_params=params(8),
        cost_estimate=cost(1),
        name="prepare",
    )(jnp.transpose(vert_corr, (1, 0, 2)), jnp.transpose(lat_taps, (1, 0, 2)))

    flat_control = control.reshape(fields * levels * rows, longitudes)
    flat_smoothing = smoothing.reshape(fields * levels * rows, longitudes)
    sizes = (fields, levels, rows)
    tiles = pltpu.VMEM((lines, LANES), F32)
    a_t, w0_t, w1_t, s_t, ends = pl.pallas_call(
        functools.partial(filter_kernel, *sizes),
        out_shape=[line] * 4 + [sds((4, per, LANES))],
        in_specs=[HBM] * 2,
        out_specs=[VMEM] * 5,
        scratch_shapes=[pltpu.VMEM(flat_control.shape, F32)] * 2
        + [tiles] * 4
        + [pltpu.VMEM((2, rows, LANES, LANES), F32), pltpu.SemaphoreType.DMA((2 * fields,))],
        compiler_params=params(34),
        cost_estimate=cost(6),
        name="filter_local",
    )(flat_control, flat_smoothing)
    gathered = lax.all_gather(ends, "lon")

    halo_rows = blocks * HALO * LANES
    halo_shape = sds((halo_rows, LANES), BF)
    low, high, entering = pl.pallas_call(
        functools.partial(edges_kernel, fields, rows, count),
        out_shape=[halo_shape, halo_shape, sds((2, per, LANES))],
        in_specs=[VMEM] * 4,
        out_specs=[VMEM] * 3,
        compiler_params=params(16),
        cost_estimate=cost(1),
        name="edges",
    )(gathered, w0_t, w1_t, s_t)

    bands = lax.axis_size("lat")
    up = [(i, i + 1) for i in range(bands - 1)]
    down = [(i + 1, i) for i in range(bands - 1)]
    after = lax.ppermute(low, "lat", down)
    before = lax.ppermute(high, "lat", up)
    sites = rows * longitudes
    inner_shape = (fields, sites // CELLS - 2, padded, CELLS)
    outer_shape = (fields, 2, padded, CELLS)
    partial_shape = (blocks, 2 * HALO, longitudes, LANES)
    inner, partial = pl.pallas_call(
        functools.partial(interior_kernel, fields, rows),
        out_shape=[sds(inner_shape, BF), sds(partial_shape)],
        in_specs=[VMEM] * 6,
        out_specs=[VMEM] * 2,
        scratch_shapes=[
            pltpu.VMEM((per, longitudes, LANES), F32),
            pltpu.VMEM((blocks, sites - 2 * CELLS, LANES), F32),
        ],
        compiler_params=params(16),
        cost_estimate=cost(3),
        name="interior",
    )(entering, w0_t, w1_t, s_t, taps, vert)

    outward = sds((halo_rows + 2 * count, LANES), BF)
    lift_shape = (blocks, sites, LANES)
    lift, low, high, *residuals = pl.pallas_call(
        functools.partial(observe_kernel, *sizes, bands),
        out_shape=[sds(lift_shape), outward, outward] + [sds((count, slots))] * (bands - 1),
        in_specs=[SMEM] * 3 + [VMEM] + [HBM] * 7,
        out_specs=[HBM] * 3 + [VMEM] * (bands - 1),
        scratch_shapes=[
            pltpu.VMEM(inner_shape, BF),
            pltpu.VMEM(partial_shape, F32),
            pltpu.VMEM(halo_shape.shape, BF),
            pltpu.VMEM(halo_shape.shape, BF),
            pltpu.VMEM(taps.shape, F32),
            pltpu.VMEM(vert.shape, BF),
            pltpu.VMEM(jacobian.shape, BF),
            pltpu.VMEM((blocks, 2 * CELLS, LANES), F32),
            pltpu.VMEM(outer_shape, BF),
            pltpu.VMEM(lift_shape, F32),
            pltpu.VMEM(outward.shape, BF),
            pltpu.VMEM(outward.shape, BF),
            pltpu.VMEM(((bands + 1) * count, slots), F32),
            pltpu.SMEM((fields * total,), jnp.int32),
            pltpu.SMEM((fields,), jnp.int32),
            pltpu.VMEM((sites // CELLS * padded, CELLS), F32),
            pltpu.SemaphoreType.DMA((7,)),
            pltpu.SemaphoreType.DMA((blocks + 2,)),
        ],
        compiler_params=params(FAR_MIB),
        cost_estimate=cost(14),
        name="observe",
    )(
        obs_field[0], obs_owner[0], obs_count[0], obs_cell[0],
        inner, partial, before, after, taps, vert, jacobian,
    )

    from_before = lax.ppermute(low, "lat", up)
    from_after = lax.ppermute(high, "lat", down)
    swap = [(0, bands - 1), (bands - 1, 0)]
    arrived = [residuals[0], lax.ppermute(residuals[1], "lat", swap)]
    for n in range(2, bands - 1):
        ring = [(i, (i + n) % bands) for i in range(bands)]
        arrived.append(lax.ppermute(residuals[n], "lat", ring))
    carried = 2 * per + (bands + 1) * count
    a_again, g_t, gq_t, gp_t, spread = pl.pallas_call(
        functools.partial(respond_kernel, fields, rows),
        out_shape=[line] * 5,
        in_specs=[HBM] * 3,
        out_specs=[VMEM] * 5,
        scratch_shapes=[
            pltpu.VMEM(lift_shape, F32),
            pltpu.VMEM(taps.shape, F32),
            tiles,
            pltpu.SemaphoreType.DMA((2 + blocks,)),
        ],
        compiler_params=params(36),
        cost_estimate=cost(5),
        name="respond",
    )(lift, taps, a_t)
    u_t, ends = pl.pallas_call(
        functools.partial(adjoint_kernel, fields, rows),
        out_shape=[line, sds((carried, LANES))],
        in_specs=[VMEM] * (5 + len(arrived)),
        out_specs=[VMEM] * 2,
        scratch_shapes=[tiles] * 2,
        compiler_params=params(20),
        cost_estimate=cost(3),
        name="adjoint_local",
    )(spread, from_before, from_after, a_again, g_t, *arrived)
    gathered_back = lax.all_gather(ends, "lon")
    gradient, returned = pl.pallas_call(
        functools.partial(gradient_kernel, *sizes, count, bands),
        out_shape=[sds(flat_control.shape), sds((total, slots))],
        in_specs=[VMEM] * 6,
        out_specs=[HBM, VMEM],
        scratch_shapes=[
            tiles,
            pltpu.VMEM((rows, LANES, LANES), F32),
            pltpu.VMEM(flat_control.shape, F32),
            pltpu.SemaphoreType.DMA((fields,)),
        ],
        compiler_params=params(20),
        cost_estimate=cost(3),
        name="gradient",
    )(gathered, gathered_back, u_t, gq_t, gp_t, flat_control)
    return gradient.reshape(control.shape), returned[None]


def solution(mesh):
    return jax.shard_map(
        local,
        mesh=mesh,
        in_specs=(
            P(None, None, "lat", "lon"),
            P(None, None, "lat", "lon"),
            P(None, None, "lat"),
            P(),
            P(("lon", "lat"), None, None),
            P(("lon", "lat"), None),
            P(("lon", "lat"), None),
            P(("lon", "lat"), None),
            P(("lon", "lat"), None, None, None),
            P(("lon", "lat"), None, None),
            P(("lon", "lat"), None, None),
        ),
        out_specs=(P(None, None, "lat", "lon"), P(("lon", "lat"), None, None)),
        check_vma=False,
    )
```

time: 132 us -> 93.5 us (0.71)
  local copies, waits for them, and re-layouts: 33.5 us -> 6.99 us
  blocking collectives: 34.8 us -> 21.7 us
  waiting for transfers between devices: 0.01 us -> 5.71 us
  Pallas kernels: 39.8 us -> 34.6 us
  starting transfers between devices: 20.2 us -> 22.7 us
  other arithmetic: 1.47 us -> 0 us
    unnamed x55 -> x28, local copies, waits for them, and re-layouts: 22.8 us -> 6.99 us
    all_to_all x1 -> x0, blocking collectives: 13.9 us -> none  [local(): lax.all_to_all(residual, both, split_axis=0, concat_axis=0, tiled=True)]
    scatter x5 -> x0, local copies, waits for them, and re-layouts: 10.1 us -> none  [the longest x4 9.13 us: local(): vert = vert.at[f, :levels, begin:begin + over].set(vert_corr[f, :, LANES:])]
    ppermute x1, waiting for transfers between devices: 0.01 us -> 4.23 us  [local(): after = lax.ppermute(low, 'lat', down)]
    ppermute x0 -> x2, starting transfers between devices: none -> 3.04 us  [the longest x1 2.97 us: local(): arrived = [residuals[0], lax.ppermute(residuals[1], 'lat', swap)]]
    pallas_call x1, Pallas kernels: 8.15 us -> 5.23 us  [local(): pl.pallas_call(functools.partial(filter_kernel, *sizes), out_shape=[line]...]
    pallas_call x4 -> x7, Pallas kernels: 30 us -> 27.7 us  [the longest x1 14.4 us: local(): pl.pallas_call(functools.partial(observe_kernel, *sizes, bands), out_shap...]
    ppermute x1, waiting for transfers between devices: 0.01 us -> 1.47 us  [local(): before = lax.ppermute(high, 'lat', up)]
  transfers between devices with their start and end apart: 5 -> 7, of which waited for: 0 -> 2; matrix products, arithmetic and copies ran while one was open for 11% -> 0% of each run, Pallas kernels for 12% -> 13%
where the time goes in v1:
time: 93.5 us; the launch traced here: 92.8 us
  Pallas kernels  34.6 us (37%)
  starting transfers between devices  22.7 us (24%)
  blocking collectives  21.7 us (23%)
  local copies, waits for them, and re-layouts  6.99 us (7%)
  waiting for transfers between devices  5.71 us (6%)
  between operations  1.06 us (1%)
    pallas_call x1, Pallas kernels, local(): pl.pallas_call(functools.partial(observe_kernel, *sizes, bands), out_shap...  14.4 us
    all_gather x1, blocking collectives, local(): gathered = lax.all_gather(ends, 'lon')  11.7 us
    all_gather x1, blocking collectives, local(): gathered_back = lax.all_gather(ends, 'lon')  10.1 us
    all_to_all x1, starting transfers between devices, local(): lax.all_to_all(sent, both, split_axis=0, concat_axis=0, tiled=True)  7.42 us
    unnamed x28, local copies, waits for them, and re-layouts  6.99 us
    ppermute x1, starting transfers between devices, local(): before = lax.ppermute(high, 'lat', up)  5.39 us
    pallas_call x1, Pallas kernels, local(): pl.pallas_call(functools.partial(filter_kernel, *sizes), out_shape=[line]...  5.23 us
    ppermute x1, starting transfers between devices, local(): from_before = lax.ppermute(low, 'lat', up)  4.25 us
  transfers between devices with their start and end apart: 7, of which 2 were waited for; matrix products, arithmetic and copies ran while one was open for 0% of the time, Pallas kernels for 13%

profile of v1, /device:TPU:0, one launch (start us, length us, event | category | flops | bytes accessed | tf_op | source)
XLA Modules:
  0.0 92.8 jit_solution(7257287063325093678)
XLA Ops:
  0.6 3.1 %pack.1 = bf16[32,144,128]{2,1,0:T(8,128)(2,1)} custom-call(bf16[137,32,128]{2,1,0:T(8,128)(2,1)} %bitcast.23, bf16[32,128]{1,0:T(8,128)(2,1)} %bitcast.25, bf16[32,128]{1,0:T(8,128)(2,1)} %bitcast.26), custom_call_target="tpu_custom_call" | custom-call | bytes 10500000 | tf_op jit(solution)/shard_map/pack/pallas_call | solution.py:540
  3.8 7.4 %all-to-all-start = ((bf16[32,144,128]{2,1,0:T(8,128)(2,1)}), bf16[32,144,128]{2,1,0:T(8,128)(2,1)}, u32[]{:S(2)}, u32[]{:S(2)}) async-start(bf16[32,144,128]{2,1,0:T(8,128)(2,1)} %pack.1), calls=%async_computation | async-start | bytes 2359296 | tf_op jit(solution)/shard_map/all_to_all | solution.py:557
  11.2 0.0 copy-start.5
  11.2 1.6 %copy-done.5 = f32[4,137,8,128]{3,2,1,0:T(8,128)S(1)} copy-done((f32[4,137,8,128]{3,2,1,0:T(8,128)S(1)}, f32[4,137,8,128]{3,2,1,0:T(8,128)}, u32[]{:S(2)}) %copy-start.5) | copy-done | bytes 2244632
  12.9 5.2 %filter_local.1 = (f32[5120,128]{1,0:T(8,128)S(1)}, f32[5120,128]{1,0:T(8,128)S(1)}, f32[5120,128]{1,0:T(8,128)S(1)}, f32[5120,128]{1,0:T(8,128)S(1)}, f32[4,40,128]{2,1,0:T(8,128)S(1)}) custom-call(f32[4384,128]{1,0:T(8,128)S(1)} %bitcast.15, f32[4384,128]{1,0:T(8,128)S(1)} %bitcast.19), custom_call_target="tpu_custom_call" | custom-call | bytes 21000000 | tf_op jit(solution)/shard_map/filter_local/pallas_call | solution.py:575
  18.1 11.7 %all-gather = f32[32,40,128]{2,1,0:T(8,128)S(1)} all-gather(f32[4,40,128]{2,1,0:T(8,128)S(1)} %get-tuple-element.29), channel_id=2, replica_groups=mesh['lon'=8,'lat'=4] {'lon'}, dimensions={0}, use_global_device_ids=true | all-gather | bytes 737280 | tf_op jit(solution)/shard_map/all_gather | solution.py:587
  29.8 0.9 edges.1
  30.7 5.4 %collective-permute-start = (bf16[1280,128]{1,0:T(8,128)(2,1)S(1)}, bf16[1280,128]{1,0:T(8,128)(2,1)S(1)}, u32[]{:S(2)}, u32[]{:S(2)}) collective-permute-start(bf16[1280,128]{1,0:T(8,128)(2,1)S(1)} %get-tuple-element.38), channel_id=1, source_target_pairs={{0,1},{1,2},{2,3},{4,5},{5,6},{6,7},{8,9},{9,10},{10,11},{12,13},{... | collective-permute-start | bytes 983048 | tf_op jit(solution)/shard_map/ppermute | solution.py:605
  36.1 1.3 %collective-permute-start.1 = (bf16[1280,128]{1,0:T(8,128)(2,1)S(1)}, bf16[1280,128]{1,0:T(8,128)(2,1)}, u32[]{:S(2)}, u32[]{:S(2)}) collective-permute-start(bf16[1280,128]{1,0:T(8,128)(2,1)S(1)} %get-tuple-element.39), channel_id=1, source_target_pairs={{1,0},{2,1},{3,2},{5,4},{6,5},{7,6},{9,8},{10,9},{11,10},{13,12},{... | collective-permute-start | bytes 983048 | tf_op jit(solution)/shard_map/ppermute | solution.py:604
  37.4 0.5 prepare.1
  37.9 2.3 %interior.1 = (bf16[4,2,144,256]{3,2,1,0:T(8,128)(2,1)S(1)}, f32[5,4,128,128]{3,2,1,0:T(8,128)S(1)}) custom-call(f32[2,40,128]{2,1,0:T(8,128)S(1)} %get-tuple-element.33.entering, f32[5120,128]{1,0:T(8,128)S(1)} %get-tuple-element.30.w0_t, f32[5120,128]{1,0:T(8,128)S(1)} %get-tuple-element.31.w1_t, f32[5120,128]{1,0:T(8,128)S(1)} %get-tuple-element.32.s_t, ...), custom_call_target="tpu_custom_call" | custom-call | bytes 10500000 | tf_op jit(solution)/shard_map/interior/pallas_call | solution.py:610
  40.2 0.0 copy-start.6
  40.2 1.0 %copy-done.6 = f32[5,4,128,128]{3,2,1,0:T(8,128)} copy-done((f32[5,4,128,128]{3,2,1,0:T(8,128)}, f32[5,4,128,128]{3,2,1,0:T(8,128)S(1)}, u32[]{:S(2)}) %copy-start.6) | copy-done | bytes 1310744
  41.3 0.8 copy-done.9
  42.1 1.5 %collective-permute-done.before_far = bf16[1280,128]{1,0:T(8,128)(2,1)S(1)} collective-permute-done((bf16[1280,128]{1,0:T(8,128)(2,1)S(1)}, bf16[1280,128]{1,0:T(8,128)(2,1)S(1)}, u32[]{:S(2)}, u32[]{:S(2)}) %collective-permute-start) | collective-permute-done | bytes 327712 | tf_op jit(solution)/shard_map/ppermute | solution.py:605
  43.5 4.2 %collective-permute-done.1.after_far = bf16[1280,128]{1,0:T(8,128)(2,1)} collective-permute-done((bf16[1280,128]{1,0:T(8,128)(2,1)S(1)}, bf16[1280,128]{1,0:T(8,128)(2,1)}, u32[]{:S(2)}, u32[]{:S(2)}) %collective-permute-start.1) | collective-permute-done | bytes 327712 | tf_op jit(solution)/shard_map/ppermute | solution.py:604
  47.8 0.0 all-to-all-done.jacobian_far
  47.8 14.4 %observe.1 = (f32[5,1024,128]{2,1,0:T(8,128)}, bf16[1296,128]{1,0:T(8,128)(2,1)}, bf16[1296,128]{1,0:T(8,128)(2,1)}, f32[8,128]{1,0:T(8,128)}, f32[8,128]{1,0:T(8,128)}, /*index=5*/f32[8,128]{1,0:T(8,128)}) custom-call(s32[32]{0:T(128)} %bitcast.27, s32[32]{0:T(128)} %bitcast.28, s32[32]{0:T(128)} %bitcast.29, s32[32,128]{1,0:T(8,128)} %bitcast.24, ...), custom_call_target="tpu_custom_call" | custom-call | bytes 49000000 | tf_op jit(solution)/shard_map/observe/pallas_call | solution.py:626
  62.2 4.2 %collective-permute-start.2 = (bf16[1296,128]{1,0:T(8,128)(2,1)}, bf16[1296,128]{1,0:T(8,128)(2,1)S(1)}, u32[]{:S(2)}, u32[]{:S(2)}) collective-permute-start(bf16[1296,128]{1,0:T(8,128)(2,1)} %get-tuple-element.43), channel_id=1, source_target_pairs={{0,1},{1,2},{2,3},{4,5},{5,6},{6,7},{8,9},{9,10},{10,11},{12,13},{... | collective-permute-start | bytes 995336 | tf_op jit(solution)/shard_map/ppermute | solution.py:659
  66.4 1.3 %collective-permute-start.3 = (bf16[1296,128]{1,0:T(8,128)(2,1)}, bf16[1296,128]{1,0:T(8,128)(2,1)S(1)}, u32[]{:S(2)}, u32[]{:S(2)}) collective-permute-start(bf16[1296,128]{1,0:T(8,128)(2,1)} %get-tuple-element.44), channel_id=1, source_target_pairs={{1,0},{2,1},{3,2},{5,4},{6,5},{7,6},{9,8},{10,9},{11,10},{13,12},{... | collective-permute-start | bytes 995336 | tf_op jit(solution)/shard_map/ppermute | solution.py:660
  67.7 3.0 %collective-permute-start.4 = (f32[8,128]{1,0:T(8,128)}, f32[8,128]{1,0:T(8,128)S(1)}, u32[]{:S(2)}, u32[]{:S(2)}) collective-permute-start(f32[8,128]{1,0:T(8,128)} %get-tuple-element.48), channel_id=1, source_target_pairs={{0,3},{3,0},{4,7},{7,4},{8,11},{11,8},{12,15},{15,12},{16,19},{19,... | collective-permute-start | bytes 12296 | tf_op jit(solution)/shard_map/ppermute | solution.py:662
  70.7 0.1 collective-permute-start.5
  70.8 1.7 %copy-done.2 = f32[5120,128]{1,0:T(8,128)S(1)} copy-done((f32[5120,128]{1,0:T(8,128)S(1)}, f32[5120,128]{1,0:T(8,128)}, u32[]{:S(2)}) %copy-start.2) | copy-done | bytes 2621464
  72.6 1.7 %copy-done.3 = f32[5,1024,128]{2,1,0:T(8,128)S(1)} copy-done((f32[5,1024,128]{2,1,0:T(8,128)S(1)}, f32[5,1024,128]{2,1,0:T(8,128)}, u32[]{:S(2)}) %copy-start.3) | copy-done | bytes 2621464
  74.3 3.4 %respond.1 = (f32[5120,128]{1,0:T(8,128)S(1)}, f32[5120,128]{1,0:T(8,128)S(1)}, f32[5120,128]{1,0:T(8,128)S(1)}, f32[5120,128]{1,0:T(8,128)S(1)}, f32[5120,128]{1,0:T(8,128)S(1)}) custom-call(f32[5,1024,128]{2,1,0:T(8,128)S(1)} %copy-done.3, f32[5,5,8,128]{3,2,1,0:T(8,128)S(1)} %copy-done.8, f32[5120,128]{1,0:T(8,128)S(1)} %copy-done.2), custom_call_target="tpu_custom_call" | custom-call | bytes 17500000 | tf_op jit(solution)/shard_map/respond/pallas_call | solution.py:667
  77.7 0.0 collective-permute-done.4.rest_1_
  77.7 0.0 collective-permute-done.5.rest_2_
  77.7 0.0 collective-permute-done.2.low
  77.7 0.0 collective-permute-done.3.high
  77.7 1.6 %adjoint_local.1 = (f32[5120,128]{1,0:T(8,128)S(1)}, f32[120,128]{1,0:T(8,128)S(1)}) custom-call(f32[5120,128]{1,0:T(8,128)S(1)} %get-tuple-element.42.spread, bf16[1296,128]{1,0:T(8,128)(2,1)S(1)} %collective-permute-done.2.low, bf16[1296,128]{1,0:T(8,128)(2,1)S(1)} %collective-permute-done.3.high, f32[5120,128]{1,0:T(8,128)S(1)} %get-tuple-element.45.a_t, ...), custom_call_target="tpu_custom_call" | custom-call | bytes 10500000 | tf_op jit(solution)/shard_map/adjoint_local/pallas_call | solution.py:682
  79.4 10.1 %all-gather.1 = f32[960,128]{1,0:T(8,128)S(1)} all-gather(f32[120,128]{1,0:T(8,128)S(1)} %get-tuple-element.50), channel_id=3, replica_groups=mesh['lon'=8,'lat'=4] {'lon'}, dimensions={0}, use_global_device_ids=true | all-gather | bytes 552960 | tf_op jit(solution)/shard_map/all_gather | solution.py:692
  89.5 3.2 %gradient.1 = (f32[4384,128]{1,0:T(8,128)}, f32[32,128]{1,0:T(8,128)}) custom-call(f32[8,4,40,128]{3,2,1,0:T(8,128)S(1)} %bitcast.18, f32[8,120,128]{2,1,0:T(8,128)S(1)} %bitcast.20, f32[5120,128]{1,0:T(8,128)S(1)} %get-tuple-element.51.u_t, f32[5120,128]{1,0:T(8,128)S(1)} %get-tuple-element.52.gq_t, f32[5120,128]{1,0:T(8,128)S(1)} %get-tuple-element.53.gp_t, ...), custom_call_target="tpu_custom_call" | custom-call | bytes 10500000 | tf_op jit(solution)/shard_map/gradient/pallas_call | solution.py:693
  (21 shorter events, 0.0 us)
Async XLA Ops:
  0.6 10.6 %copy-start = (f32[4,137,8,128]{3,2,1,0:T(8,128)S(1)}, f32[4,137,8,128]{3,2,1,0:T(8,128)}, u32[]{:S(2)}) copy-start(f32[4,137,8,128]{3,2,1,0:T(8,128)} %param.11) | copy-start | bytes 6733828
  3.8 44.0 %all-to-all-start = ((bf16[32,144,128]{2,1,0:T(8,128)(2,1)}), bf16[32,144,128]{2,1,0:T(8,128)(2,1)}, u32[]{:S(2)}, u32[]{:S(2)}) async-start(bf16[32,144,128]{2,1,0:T(8,128)(2,1)} %pack.1), calls=%async_computation | async-start | bytes 2359296 | tf_op jit(solution)/shard_map/all_to_all | solution.py:557
  11.2 1.6 %copy-start.5 = (f32[4,137,8,128]{3,2,1,0:T(8,128)S(1)}, f32[4,137,8,128]{3,2,1,0:T(8,128)}, u32[]{:S(2)}) copy-start(f32[4,137,8,128]{3,2,1,0:T(8,128)} %param.12) | copy-start | bytes 6733828
  18.1 12.6 %copy-start.1 = (f32[5120,128]{1,0:T(8,128)}, f32[5120,128]{1,0:T(8,128)S(1)}, u32[]{:S(2)}) copy-start(f32[5120,128]{1,0:T(8,128)S(1)} %get-tuple-element.41.a_far) | copy-start | bytes 7864324
  29.8 7.6 %copy-start.10 = (f32[4,137,137]{2,0,1:T(4,128)S(1)}, f32[4,137,137]{2,0,1:T(4,128)}, u32[]{:S(2)}) copy-start(f32[4,137,137]{2,0,1:T(4,128)} %param.14) | copy-start | bytes 900916
  29.8 7.6 %copy-start.11 = (f32[4,5,8]{2,0,1:T(4,128)S(1)}, f32[4,5,8]{2,0,1:T(4,128)}, u32[]{:S(2)}) copy-start(f32[4,5,8]{2,0,1:T(4,128)} %param.13) | copy-start | bytes 1924
  30.7 12.9 %collective-permute-start = (bf16[1280,128]{1,0:T(8,128)(2,1)S(1)}, bf16[1280,128]{1,0:T(8,128)(2,1)S(1)}, u32[]{:S(2)}, u32[]{:S(2)}) collective-permute-start(bf16[1280,128]{1,0:T(8,128)(2,1)S(1)} %get-tuple-element.38), channel_id=1, source_target_pairs={{0,1},{1,2},{2,3},{4,5},{5,6},{6,7},{8,9},{9,10},{10,11},{12,13},{... | collective-permute-start | bytes 983048 | tf_op jit(solution)/shard_map/ppermute | solution.py:605
  36.1 11.7 %collective-permute-start.1 = (bf16[1280,128]{1,0:T(8,128)(2,1)S(1)}, bf16[1280,128]{1,0:T(8,128)(2,1)}, u32[]{:S(2)}, u32[]{:S(2)}) collective-permute-start(bf16[1280,128]{1,0:T(8,128)(2,1)S(1)} %get-tuple-element.39), channel_id=1, source_target_pairs={{1,0},{2,1},{3,2},{5,4},{6,5},{7,6},{9,8},{10,9},{11,10},{13,12},{... | collective-permute-start | bytes 983048 | tf_op jit(solution)/shard_map/ppermute | solution.py:604
  37.9 2.3 %copy-start.4 = (bf16[4,144,512]{2,1,0:T(8,128)(2,1)}, bf16[4,144,512]{2,1,0:T(8,128)(2,1)S(1)}, u32[]{:S(2)}) copy-start(bf16[4,144,512]{2,1,0:T(8,128)(2,1)S(1)} %get-tuple-element.35.vert.vert_far) | copy-start | bytes 1769476
  37.9 2.3 %copy-start.7 = (f32[5,5,8,128]{3,2,1,0:T(8,128)}, f32[5,5,8,128]{3,2,1,0:T(8,128)S(1)}, u32[]{:S(2)}) copy-start(f32[5,5,8,128]{3,2,1,0:T(8,128)S(1)} %get-tuple-element.34.taps.taps_far) | copy-start | bytes 307204
  40.2 1.1 %copy-start.6 = (f32[5,4,128,128]{3,2,1,0:T(8,128)}, f32[5,4,128,128]{3,2,1,0:T(8,128)S(1)}, u32[]{:S(2)}) copy-start(f32[5,4,128,128]{3,2,1,0:T(8,128)S(1)} %get-tuple-element.37.partial_far) | copy-start | bytes 3932164
  41.3 0.8 copy-start.9
  43.5 4.2 %copy-start.13 = (bf16[1280,128]{1,0:T(8,128)(2,1)}, bf16[1280,128]{1,0:T(8,128)(2,1)S(1)}, u32[]{:S(2)}) copy-start(bf16[1280,128]{1,0:T(8,128)(2,1)S(1)} %collective-permute-done.before_far) | copy-start | bytes 983044
  43.5 27.3 %copy-start.8 = (f32[5,5,8,128]{3,2,1,0:T(8,128)S(1)}, f32[5,5,8,128]{3,2,1,0:T(8,128)}, u32[]{:S(2)}) copy-start(f32[5,5,8,128]{3,2,1,0:T(8,128)} %copy-done.7) | copy-start | bytes 307204
  62.2 15.5 %collective-permute-start.2 = (bf16[1296,128]{1,0:T(8,128)(2,1)}, bf16[1296,128]{1,0:T(8,128)(2,1)S(1)}, u32[]{:S(2)}, u32[]{:S(2)}) collective-permute-start(bf16[1296,128]{1,0:T(8,128)(2,1)} %get-tuple-element.43), channel_id=1, source_target_pairs={{0,1},{1,2},{2,3},{4,5},{5,6},{6,7},{8,9},{9,10},{10,11},{12,13},{... | collective-permute-start | bytes 995336 | tf_op jit(solution)/shard_map/ppermute | solution.py:659
  66.4 11.3 %collective-permute-start.3 = (bf16[1296,128]{1,0:T(8,128)(2,1)}, bf16[1296,128]{1,0:T(8,128)(2,1)S(1)}, u32[]{:S(2)}, u32[]{:S(2)}) collective-permute-start(bf16[1296,128]{1,0:T(8,128)(2,1)} %get-tuple-element.44), channel_id=1, source_target_pairs={{1,0},{2,1},{3,2},{5,4},{6,5},{7,6},{9,8},{10,9},{11,10},{13,12},{... | collective-permute-start | bytes 995336 | tf_op jit(solution)/shard_map/ppermute | solution.py:660
  67.7 9.9 %collective-permute-start.4 = (f32[8,128]{1,0:T(8,128)}, f32[8,128]{1,0:T(8,128)S(1)}, u32[]{:S(2)}, u32[]{:S(2)}) collective-permute-start(f32[8,128]{1,0:T(8,128)} %get-tuple-element.48), channel_id=1, source_target_pairs={{0,3},{3,0},{4,7},{7,4},{8,11},{11,8},{12,15},{15,12},{16,19},{19,... | collective-permute-start | bytes 12296 | tf_op jit(solution)/shard_map/ppermute | solution.py:662
  70.7 7.0 %collective-permute-start.5 = (f32[8,128]{1,0:T(8,128)}, f32[8,128]{1,0:T(8,128)S(1)}, u32[]{:S(2)}, u32[]{:S(2)}) collective-permute-start(f32[8,128]{1,0:T(8,128)} %get-tuple-element.49), channel_id=1, source_target_pairs={{0,2},{1,3},{2,0},{3,1},{4,6},{5,7},{6,4},{7,5},{8,10},{9,11},{10,... | collective-permute-start | bytes 12296 | tf_op jit(solution)/shard_map/ppermute | solution.py:665
  70.8 1.7 %copy-start.2 = (f32[5120,128]{1,0:T(8,128)S(1)}, f32[5120,128]{1,0:T(8,128)}, u32[]{:S(2)}) copy-start(f32[5120,128]{1,0:T(8,128)} %copy-done.1) | copy-start | bytes 7864324
  72.6 1.7 %copy-start.3 = (f32[5,1024,128]{2,1,0:T(8,128)S(1)}, f32[5,1024,128]{2,1,0:T(8,128)}, u32[]{:S(2)}) copy-start(f32[5,1024,128]{2,1,0:T(8,128)} %get-tuple-element.40.lift_far) | copy-start | bytes 7864324
  74.3 3.4 %copy-start.12 = (f32[8,128]{1,0:T(8,128)S(1)}, f32[8,128]{1,0:T(8,128)}, u32[]{:S(2)}) copy-start(f32[8,128]{1,0:T(8,128)} %get-tuple-element.47.rest_0_) | copy-start | bytes 12292

commit v2 on v1

--- a/solution.py
+++ b/solution.py
@@ -10,6 +10,7 @@
 LANES = 128
 HALO = 2
 FAR_MIB = 60
+ROOM = 12
 CELLS = 256
 GROUP = 4
 BF = jnp.bfloat16
@@ -137,7 +138,8 @@
 
 def filter_kernel(
     fields, levels, rows, control, smoothing,
-    a_t, w0_t, w1_t, s_t, ends, control_v, smoothing_v, g_t, x_t, e_t, pe_t, extra, arrived,
+    a_far, w0_t, w1_t, s_t, ends,
+    control_v, smoothing_v, a_t, g_t, x_t, e_t, pe_t, extra, arrived, left,
 ):
     per = (fields + 1) * rows
     over, room = levels - LANES, LANES // fields
@@ -162,6 +164,8 @@
         a_t[at, :] = extra[0, j].T
         x_t[at, :] = extra[1, j].T
 
+    leaving = fetch([(a_t, a_far.at[pl.ds(0, a_t.shape[0])])], left)
+
     def east(i, carry):
         e, p = carry
         at = step_rows(i, per)
@@ -194,22 +198,45 @@
     ends[1] = e
     ends[2] = w0
     ends[3] = w1
-
-
-def edges_kernel(fields, rows, count, gathered, w0_t, w1_t, s_t, low, high, entering):
+    for copy in leaving:
+        copy.wait()
+
+
+def put_halo(dst, b, fields, first, second):
+    if b < fields:
+        dst[pl.ds(b * HALO * LANES, LANES), :] = first.astype(BF)
+        dst[pl.ds((b * HALO + 1) * LANES, LANES), :] = second.astype(BF)
+    else:
+        half = LANES // fields // 2
+        both = first + pltpu.roll(second, half, 1)
+        dst[pl.ds(b * HALO * LANES, LANES), :] = both.astype(BF)
+
+
+def get_halo(src, b, fields):
+    first = src[pl.ds(b * HALO * LANES, LANES), :].astype(F32)
+    if b < fields:
+        return first, src[pl.ds((b * HALO + 1) * LANES, LANES), :].astype(F32)
+    return first, pltpu.roll(first, LANES - LANES // fields // 2, 1)
+
+
+def edges_kernel(fields, rows, count, gathered, w0_t, w1_t, s_t, first, second, entering, sides):
     per = (fields + 1) * rows
     part = [[gathered[s, q] for s in range(count)] for q in range(4)]
     east_in, west_in = solve_sectors(lax.axis_index("lon"), part[0], part[1], part[3], part[2])
     entering[0] = east_in
     entering[1] = west_in
+    odd = lax.axis_index("lat") % 2
+    high, low = sides.at[odd], sides.at[1 - odd]
     for b in range(fields + 1):
-        for j in range(HALO):
-            to = pl.ds((b * HALO + j) * LANES, LANES)
-            for first, dst in ((b * rows, low), (b * rows + rows - HALO, high)):
-                n = first + j
+        for begin, dst in ((b * rows, low), (b * rows + rows - HALO, high)):
+            lines = []
+            for n in range(begin, begin + HALO):
                 at = pl.ds(n, LANES, stride=per)
                 line = w0_t[at, :] + w1_t[at, :] * east_in[n : n + 1]
-                dst[to, :] = (line + s_t[at, :] * west_in[n : n + 1]).astype(BF)
+                lines.append(line + s_t[at, :] * west_in[n : n + 1])
+            put_halo(dst, b, fields, *lines)
+    first[...] = sides[0]
+    second[...] = sides[1]
 
 
 def vertical(vert, mixed):
@@ -239,11 +266,12 @@
                 mixed[b, pl.ds((j - HALO) * LANES, LANES), :] = total
             else:
                 partial[b, j if j < HALO else j - rows + 2 * HALO] = total
-    for f in range(fields):
-        for h in range(state.shape[1]):
+    padded = vert.shape[1]
+    for f in range(fields):
+        for h in range(state.shape[1] // padded):
             at = pl.ds(h * CELLS, CELLS)
             both = jnp.concatenate([mixed[f, at, :], mixed[fields, at, :]], axis=1)
-            state[f, h] = vertical(vert[f], both)
+            state[f, pl.ds(h * padded, padded), :] = vertical(vert[f], both)
 
 
 def route_of(delta, bands):
@@ -255,18 +283,23 @@
 
 def observe_kernel(
     fields, levels, rows, bands, field, owner, live, cells,
-    inner_far, partial_far, before_far, after_far, taps_far, vert_far, jacobian_far, *rest,
+    inner_far, partial_far, first_far, second_far, taps_far, vert_far, jacobian_far, *rest,
 ):
-    lift_far, low_far, high_far = rest[:3]
+    lift_far, first_out, second_out = rest[:3]
     residuals = rest[3 : 2 + bands]
     (
-        inner, partial, before, after, taps, vert, jacobian, mixed, outer, lift, low, high,
-        route, order, number, acc, arrived, left,
+        state, partial, beside, taps, vert, jacobian, mixed, lift, sides,
+        route, order, number, group_field, group_start, acc, arrived, left,
     ) = rest[2 + bands :]
     blocks = fields + 1
+    band = lax.axis_index("lat")
+    odd = band % 2
+    after, before = beside.at[0], beside.at[1]
+    low, high = sides.at[odd], sides.at[1 - odd]
     copies = fetch(
-        [(after_far, after), (before_far, before), (taps_far, taps), (partial_far, partial)]
-        + [(vert_far, vert), (jacobian_far, jacobian), (inner_far, inner)],
+        [(first_far, beside.at[odd]), (second_far, beside.at[1 - odd])]
+        + [(taps_far, taps), (partial_far, partial)]
+        + [(vert_far, vert)],
         arrived,
     )
     total = field.shape[0]
@@ -274,7 +307,6 @@
     parts = rows * LANES // CELLS
     wide = GROUP * LANES
     sectors = total // bands
-    band = lax.axis_index("lat")
     for f in range(fields):
         number[f] = 0
 
@@ -286,20 +318,36 @@
         return 0
 
     lax.fori_loop(0, total, place, 0)
-    route[...] = jnp.zeros_like(route)
+    groups = 0
+    for f in range(fields):
+        here = (number[f] + GROUP - 1) // GROUP
+
+        def put(p, _, f=f, first=groups):
+            group_field[first + p] = f
+            group_start[first + p] = GROUP * p
+            return 0
+
+        lax.fori_loop(0, here, put, 0)
+        groups = groups + here
+    acc[...] = jnp.zeros_like(acc)
 
     for n in range(4):
         copies[n].wait()
-
-    def beside(src, b, n):
-        return src[pl.ds((b * HALO + n) * LANES, LANES), :].astype(F32)
+    copies += fetch(
+        [(jacobian_far, jacobian)]
+        + [
+            (inner_far.at[f], state.at[f, pl.ds(padded, (parts - 2) * padded)])
+            for f in range(fields)
+        ],
+        arrived.at[pl.ds(5, 1 + fields)],
+    )
 
     def tap_of(t, b, j):
         return taps[t, b, j : j + 1, :]
 
     end = rows - 1
     for b in range(blocks):
-        above, below = [beside(before, b, n) for n in range(2)], [beside(after, b, n) for n in range(2)]
+        above, below = get_halo(before, b, fields), get_halo(after, b, fields)
         outer_rows = (
             partial[b, 0] + tap_of(0, b, 0) * above[0] + tap_of(1, b, 0) * above[1],
             partial[b, 1] + tap_of(0, b, 1) * above[1],
@@ -313,57 +361,52 @@
         for h in range(2):
             at = pl.ds(h * CELLS, CELLS)
             both = jnp.concatenate([mixed[f, at, :], mixed[fields, at, :]], axis=1)
-            outer[f, h] = vertical(vert[f], both)
-
-    copies[5].wait()
-    copies[6].wait()
+            state[f, pl.ds(h * (parts - 1) * padded, padded), :] = vertical(vert[f], both)
+
+    for n in range(1 + fields):
+        copies[5 + n].wait()
     site = lax.broadcasted_iota(jnp.int32, (CELLS, wide), 0)
     slot = lax.broadcasted_iota(jnp.int32, (1, LANES), 1)
+    spare = (bands + 1) * sectors
+
+    def group(p, _):
+        f = group_field[p]
+        places, names, at = [], [], []
+        for n in range(GROUP):
+            b = group_start[p] + n
+            known = b < number[f]
+            k = jnp.where(known, order[f * total + jnp.where(known, b, 0)], 0)
+            count = jnp.where(known, live[k], 0)
+            places.append(jnp.where(slot < count, cells[pl.ds(k, 1), :], -1))
+            w = owner[k]
+            names.append(w)
+            to = route_of(w % bands - band, bands) * sectors + w // bands
+            at.append(jnp.where(known, to, spare))
+        place = jnp.concatenate(places, axis=1)
+        part = place // CELLS
+        onehot = (site == jnp.where(place < 0, -1, place % CELLS)).astype(F32).astype(BF)
+        j = jnp.concatenate([jacobian[w] for w in names], axis=1).astype(F32)
+        found_all = jnp.dot(state[f], onehot, preferred_element_type=F32)
+        columns = jnp.zeros_like(j)
+        for h in range(parts):
+            columns = jnp.where(part == h, found_all[h * padded : (h + 1) * padded], columns)
+        model = jnp.sum(j * columns, axis=0, keepdims=True)
+        value, precision = j[levels : levels + 1], j[levels + 1 : levels + 2]
+        res = precision * (model - value)
+        adjoint = j * res
+        adjoint = jnp.concatenate(
+            [jnp.where(part == h, adjoint, 0.0).astype(BF) for h in range(parts)], axis=0
+        )
+        for n in range(GROUP):
+            route[pl.ds(at[n], 1), :] = res[:, n * LANES : (n + 1) * LANES]
+        acc[f] += lax.dot_general(adjoint, onehot, NT, preferred_element_type=F32)
+        return 0
+
+    lax.fori_loop(0, groups, group, 0)
     leaving = []
     for f in range(fields):
-        acc[...] = jnp.zeros_like(acc)
-        found = number[f]
-
-        def group(p, _):
-            known, names, places = [], [], []
-            for n in range(GROUP):
-                known.append(GROUP * p + n < found)
-                k = order[f * total + jnp.where(known[n], GROUP * p + n, 0)]
-                count = jnp.where(known[n], live[k], 0)
-                c = cells[pl.ds(k, 1), :]
-                places.append(jnp.where(slot < count, c, -1))
-                names.append(owner[k])
-            at = [route_of(w % bands - band, bands) * sectors + w // bands for w in names]
-            place = jnp.concatenate(places, axis=1)
-            part = place // CELLS
-            onehot = (site == jnp.where(place < 0, -1, place % CELLS)).astype(F32).astype(BF)
-            j = jnp.concatenate([jacobian[w] for w in names], axis=1).astype(F32)
-            columns = jnp.zeros_like(j)
-            state = [outer[f, 0], *(inner[f, h] for h in range(parts - 2)), outer[f, 1]]
-            found_all = jnp.dot(
-                jnp.concatenate(state, axis=0), onehot, preferred_element_type=F32
-            )
-            for h in range(parts):
-                columns = jnp.where(part == h, found_all[h * padded : (h + 1) * padded], columns)
-            model = jnp.sum(j * columns, axis=0, keepdims=True)
-            value, precision = j[levels : levels + 1], j[levels + 1 : levels + 2]
-            res = precision * (model - value)
-            for n in range(GROUP):
-
-                @pl.when(known[n])
-                def _():
-                    route[pl.ds(at[n], 1), :] = res[:, n * LANES : (n + 1) * LANES]
-
-            adjoint = j * res
-            adjoint = jnp.concatenate(
-                [jnp.where(part == h, adjoint, 0.0).astype(BF) for h in range(parts)], axis=0
-            )
-            acc[...] += lax.dot_general(adjoint, onehot, NT, preferred_element_type=F32)
-            return 0
-
-        lax.fori_loop(0, (found + GROUP - 1) // GROUP, group, 0)
         for h in range(parts):
-            forcing = acc[pl.ds(h * padded, padded), :].astype(BF)
+            forcing = acc[f, pl.ds(h * padded, padded), :].astype(BF)
             out = lax.dot_general(forcing, vert[f], TN, preferred_element_type=F32)
             out = out[:, : 2 * LANES] + out[:, 2 * LANES :]
             at = pl.ds(h * CELLS, CELLS)
@@ -385,12 +428,14 @@
             (high, tap_of(0, b, 0) * line(0),
              tap_of(1, b, 0) * line(0) + tap_of(0, b, 1) * line(1)),
         ):
-            dst[pl.ds(b * HALO * LANES, LANES), :] = first.astype(BF)
-            dst[pl.ds((b * HALO + 1) * LANES, LANES), :] = second.astype(BF)
+            put_halo(dst, b, fields, first, second)
+    riding = (fields * HALO + 1) * LANES
     for n, dst in ((1, low), (2, high)):
         both = jnp.concatenate(split(route[pl.ds(n * sectors, sectors), :]), axis=0)
-        dst[pl.ds(blocks * HALO * LANES, 2 * sectors), :] = both
-    leaving += fetch([(low, low_far), (high, high_far)], left.at[pl.ds(blocks, 2)])
+        dst[pl.ds(riding, 2 * sectors), :] = both
+    leaving += fetch(
+        [(sides.at[0], first_out), (sides.at[1], second_out)], left.at[pl.ds(blocks, 2)]
+    )
     for n, dst in enumerate(residuals):
         source = 0 if n == 0 else n + 2
         dst[...] = route[pl.ds(source * sectors, sectors), :]
@@ -399,14 +444,14 @@
 
 
 def respond_kernel(
-    fields, rows, lift_far, taps_far, a_far, a_t, g_t, gq_t, gp_t, spread, lift, taps, pe_t, arrived
+    fields, rows, lift_far, taps, a_far, a_t, g_t, gq_t, gp_t, spread, lift, pe_t, arrived
 ):
     blocks = fields + 1
     per = blocks * rows
-    copies = fetch(
-        [(a_far, a_t), (taps_far, taps)] + [(lift_far.at[b], lift.at[b]) for b in range(blocks)],
-        arrived,
-    )
+    chunks = 4
+    span = LANES // chunks
+    parts = [pl.ds(c * span * per, span * per) for c in range(chunks)]
+    copies = fetch([(a_far.at[at], a_t.at[at]) for at in parts], arrived)
 
     def east(i, p):
         at = step_rows(i, per)
@@ -425,12 +470,18 @@
         return a * t, a * s
 
     one = jnp.ones((per, LANES), F32)
-    copies[0].wait()
-    lax.fori_loop(0, LANES, east, one, unroll=4)
+    p = one
+    for c, copy in enumerate(copies):
+        copy.wait()
+        if c == chunks // 2:
+            copies_lift = fetch(
+                [(lift_far.at[b], lift.at[b]) for b in range(blocks)],
+                arrived.at[pl.ds(chunks, blocks)],
+            )
+        p = lax.fori_loop(c * span, (c + 1) * span, east, p, unroll=4)
     lax.fori_loop(0, LANES, west, (jnp.zeros_like(one), one), unroll=4)
-    copies[1].wait()
     for b in range(blocks):
-        copies[2 + b].wait()
+        copies_lift[b].wait()
         for m in range(rows):
             total = taps[HALO, b, m : m + 1, :] * lift[b, pl.ds(m * LANES, LANES), :]
             for t in range(2 * HALO + 1):
@@ -440,13 +491,17 @@
             spread[pl.ds(b * rows + m, LANES, stride=per), :] = total
 
 
-def adjoint_kernel(fields, rows, spread, low, high, a_t, g_t, *rest):
-    residuals = rest[:-4]
-    u_t, ends, halo, pass_t = rest[-4:]
+def adjoint_kernel(fields, rows, spread, first, second, a_t, g_t, *rest):
+    residuals = rest[:-5]
+    u_t, ends, halo, pass_t, beside = rest[-5:]
+    odd = lax.axis_index("lat") % 2
+    beside[odd] = first[...]
+    beside[1 - odd] = second[...]
+    high, low = beside.at[0], beside.at[1]
     blocks = fields + 1
     per = blocks * rows
     sectors = residuals[0].shape[0]
-    riding = blocks * HALO * LANES
+    riding = (fields * HALO + 1) * LANES
     parts = [residuals[0][...]]
     for src in (low, high):
         two = src[pl.ds(riding, 2 * sectors), :].astype(F32)
@@ -456,11 +511,9 @@
         ends[pl.ds(2 * per + n * sectors, sectors), :] = part
 
     for b in range(blocks):
-        for n in range(HALO):
-            at = pl.ds((b * HALO + n) * LANES, LANES)
-            halo[pl.ds(b * rows + n, LANES, stride=per), :] = low[at, :].astype(F32)
-            last = b * rows + rows - HALO + n
-            halo[pl.ds(last, LANES, stride=per), :] = high[at, :].astype(F32)
+        for src, begin in ((low, b * rows), (high, b * rows + rows - HALO)):
+            for n, line in enumerate(get_halo(src, b, fields)):
+                halo[pl.ds(begin + n, LANES, stride=per), :] = line
     row = lax.broadcasted_iota(jnp.int32, (per, LANES), 0) % rows
     edge = (row < HALO) | (row >= rows - HALO)
 
@@ -572,40 +625,45 @@
     flat_smoothing = smoothing.reshape(fields * levels * rows, longitudes)
     sizes = (fields, levels, rows)
     tiles = pltpu.VMEM((lines, LANES), F32)
-    a_t, w0_t, w1_t, s_t, ends = pl.pallas_call(
+    a_far, w0_t, w1_t, s_t, ends = pl.pallas_call(
         functools.partial(filter_kernel, *sizes),
-        out_shape=[line] * 4 + [sds((4, per, LANES))],
+        out_shape=[sds((ROOM * lines, LANES))] + [line] * 3 + [sds((4, per, LANES))],
         in_specs=[HBM] * 2,
-        out_specs=[VMEM] * 5,
+        out_specs=[HBM] + [VMEM] * 4,
         scratch_shapes=[pltpu.VMEM(flat_control.shape, F32)] * 2
-        + [tiles] * 4
-        + [pltpu.VMEM((2, rows, LANES, LANES), F32), pltpu.SemaphoreType.DMA((2 * fields,))],
+        + [tiles] * 5
+        + [
+            pltpu.VMEM((2, rows, LANES, LANES), F32),
+            pltpu.SemaphoreType.DMA((2 * fields,)),
+            pltpu.SemaphoreType.DMA((1,)),
+        ],
         compiler_params=params(34),
         cost_estimate=cost(6),
         name="filter_local",
     )(flat_control, flat_smoothing)
     gathered = lax.all_gather(ends, "lon")
 
-    halo_rows = blocks * HALO * LANES
+    halo_rows = (fields * HALO + 1) * LANES
     halo_shape = sds((halo_rows, LANES), BF)
-    low, high, entering = pl.pallas_call(
+    first, second, entering = pl.pallas_call(
         functools.partial(edges_kernel, fields, rows, count),
         out_shape=[halo_shape, halo_shape, sds((2, per, LANES))],
         in_specs=[VMEM] * 4,
         out_specs=[VMEM] * 3,
+        scratch_shapes=[pltpu.VMEM((2, *halo_shape.shape), BF)],
         compiler_params=params(16),
         cost_estimate=cost(1),
         name="edges",
     )(gathered, w0_t, w1_t, s_t)
 
     bands = lax.axis_size("lat")
-    up = [(i, i + 1) for i in range(bands - 1)]
-    down = [(i + 1, i) for i in range(bands - 1)]
-    after = lax.ppermute(low, "lat", down)
-    before = lax.ppermute(high, "lat", up)
+    even = [p for i in range(0, bands - 1, 2) for p in ((i, i + 1), (i + 1, i))]
+    odd = [p for i in range(1, bands - 1, 2) for p in ((i, i + 1), (i + 1, i))]
+    first = lax.ppermute(first, "lat", even)
+    second = lax.ppermute(second, "lat", odd)
     sites = rows * longitudes
-    inner_shape = (fields, sites // CELLS - 2, padded, CELLS)
-    outer_shape = (fields, 2, padded, CELLS)
+    parts = sites // CELLS
+    inner_shape = (fields, (parts - 2) * padded, CELLS)
     partial_shape = (blocks, 2 * HALO, longitudes, LANES)
     inner, partial = pl.pallas_call(
         functools.partial(interior_kernel, fields, rows),
@@ -623,29 +681,29 @@
 
     outward = sds((halo_rows + 2 * count, LANES), BF)
     lift_shape = (blocks, sites, LANES)
-    lift, low, high, *residuals = pl.pallas_call(
+    lift, first, second, *residuals = pl.pallas_call(
         functools.partial(observe_kernel, *sizes, bands),
-        out_shape=[sds(lift_shape), outward, outward] + [sds((count, slots))] * (bands - 1),
+        out_shape=[sds((ROOM * blocks, sites, LANES)), outward, outward]
+        + [sds((count, slots))] * (bands - 1),
         in_specs=[SMEM] * 3 + [VMEM] + [HBM] * 7,
         out_specs=[HBM] * 3 + [VMEM] * (bands - 1),
         scratch_shapes=[
-            pltpu.VMEM(inner_shape, BF),
+            pltpu.VMEM((fields, parts * padded, CELLS), BF),
             pltpu.VMEM(partial_shape, F32),
-            pltpu.VMEM(halo_shape.shape, BF),
-            pltpu.VMEM(halo_shape.shape, BF),
+            pltpu.VMEM((2, *halo_shape.shape), BF),
             pltpu.VMEM(taps.shape, F32),
             pltpu.VMEM(vert.shape, BF),
             pltpu.VMEM(jacobian.shape, BF),
             pltpu.VMEM((blocks, 2 * CELLS, LANES), F32),
-            pltpu.VMEM(outer_shape, BF),
             pltpu.VMEM(lift_shape, F32),
-            pltpu.VMEM(outward.shape, BF),
-            pltpu.VMEM(outward.shape, BF),
-            pltpu.VMEM(((bands + 1) * count, slots), F32),
+            pltpu.VMEM((2, *outward.shape), BF),
+            pltpu.VMEM(((bands + 1) * count + 8, slots), F32),
             pltpu.SMEM((fields * total,), jnp.int32),
             pltpu.SMEM((fields,), jnp.int32),
-            pltpu.VMEM((sites // CELLS * padded, CELLS), F32),
-            pltpu.SemaphoreType.DMA((7,)),
+            pltpu.SMEM((total // GROUP + fields,), jnp.int32),
+            pltpu.SMEM((total // GROUP + fields,), jnp.int32),
+            pltpu.VMEM((fields, parts * padded, CELLS), F32),
+            pltpu.SemaphoreType.DMA((6 + fields,)),
             pltpu.SemaphoreType.DMA((blocks + 2,)),
         ],
         compiler_params=params(FAR_MIB),
@@ -653,42 +711,41 @@
         name="observe",
     )(
         obs_field[0], obs_owner[0], obs_count[0], obs_cell[0],
-        inner, partial, before, after, taps, vert, jacobian,
-    )
-
-    from_before = lax.ppermute(low, "lat", up)
-    from_after = lax.ppermute(high, "lat", down)
+        inner, partial, first, second, taps, vert, jacobian,
+    )
+
     swap = [(0, bands - 1), (bands - 1, 0)]
     arrived = [residuals[0], lax.ppermute(residuals[1], "lat", swap)]
     for n in range(2, bands - 1):
         ring = [(i, (i + n) % bands) for i in range(bands)]
         arrived.append(lax.ppermute(residuals[n], "lat", ring))
+    first = lax.ppermute(first, "lat", even)
+    second = lax.ppermute(second, "lat", odd)
     carried = 2 * per + (bands + 1) * count
     a_again, g_t, gq_t, gp_t, spread = pl.pallas_call(
         functools.partial(respond_kernel, fields, rows),
         out_shape=[line] * 5,
-        in_specs=[HBM] * 3,
+        in_specs=[HBM, VMEM, HBM],
         out_specs=[VMEM] * 5,
         scratch_shapes=[
             pltpu.VMEM(lift_shape, F32),
-            pltpu.VMEM(taps.shape, F32),
             tiles,
-            pltpu.SemaphoreType.DMA((2 + blocks,)),
+            pltpu.SemaphoreType.DMA((4 + blocks,)),
         ],
         compiler_params=params(36),
         cost_estimate=cost(5),
         name="respond",
-    )(lift, taps, a_t)
+    )(lift, taps, a_far)
     u_t, ends = pl.pallas_call(
         functools.partial(adjoint_kernel, fields, rows),
         out_shape=[line, sds((carried, LANES))],
         in_specs=[VMEM] * (5 + len(arrived)),
         out_specs=[VMEM] * 2,
-        scratch_shapes=[tiles] * 2,
+        scratch_shapes=[tiles] * 2 + [pltpu.VMEM((2, *outward.shape), BF)],
         compiler_params=params(20),
         cost_estimate=cost(3),
         name="adjoint_local",
-    )(spread, from_before, from_after, a_again, g_t, *arrived)
+    )(spread, first, second, a_again, g_t, *arrived)
     gathered_back = lax.all_gather(ends, "lon")
     gradient, returned = pl.pallas_call(
         functools.partial(gradient_kernel, *sizes, count, bands),

time: 93.5 us -> 86.9 us (0.929)
  starting transfers between devices: 22.7 us -> 19.1 us
  local copies, waits for them, and re-layouts: 6.99 us -> 4.27 us
    ppermute x4, starting transfers between devices: 12.2 us -> 8.06 us  [the longest x2 6.02 us: local(): first = lax.ppermute(first, 'lat', even)]
    unnamed x28 -> x22, local copies, waits for them, and re-layouts: 6.99 us -> 4.27 us
    ppermute x4, waiting for transfers between devices: 5.71 us -> 3.45 us  [the longest x2 3.44 us: local(): first = lax.ppermute(first, 'lat', even)]
    ppermute x1, waiting for transfers between devices: 0.01 us -> 1.07 us  [local(): arrived.append(lax.ppermute(residuals[n], 'lat', ring))]
  transfers between devices with their start and end apart: 7 -> 7, of which waited for: 2 -> 3; matrix products, arithmetic and copies ran while one was open for 0% -> 0% of each run, Pallas kernels for 13% -> 15%
where the time goes in v2:
time: 86.9 us; the launch traced here: 86.4 us
  Pallas kernels  35 us (40%)
  blocking collectives  22.2 us (26%)
  starting transfers between devices  19.1 us (22%)
  waiting for transfers between devices  4.9 us (6%)
  local copies, waits for them, and re-layouts  4.27 us (5%)
  between operations  0.95 us (1%)
    pallas_call x1, Pallas kernels, local(): pl.pallas_call(functools.partial(observe_kernel, *sizes, bands), out_shap...  13.9 us
    all_gather x1, blocking collectives, local(): gathered = lax.all_gather(ends, 'lon')  11.7 us
    all_gather x1, blocking collectives, local(): gathered_back = lax.all_gather(ends, 'lon')  10.5 us
    all_to_all x1, starting transfers between devices, local(): lax.all_to_all(sent, both, split_axis=0, concat_axis=0, tiled=True)  7.42 us
    ppermute x2, starting transfers between devices, local(): first = lax.ppermute(first, 'lat', even)  6.02 us
    pallas_call x1, Pallas kernels, local(): pl.pallas_call(functools.partial(filter_kernel, *sizes), out_shape=[sds((...  5.23 us
    unnamed x22, local copies, waits for them, and re-layouts  4.27 us
    pallas_call x1, Pallas kernels, local(): pl.pallas_call(functools.partial(respond_kernel, fields, rows), out_shape...  3.98 us
  transfers between devices with their start and end apart: 7, of which 3 were waited for; matrix products, arithmetic and copies ran while one was open for 0% of the time, Pallas kernels for 15%

profile of v2, /device:TPU:0, one launch (start us, length us, event | category | flops | bytes accessed | tf_op | source)
XLA Modules:
  0.0 86.4 jit_solution(17989948930648538361)
XLA Ops:
  0.6 3.1 %pack.1 = bf16[32,144,128]{2,1,0:T(8,128)(2,1)} custom-call(bf16[137,32,128]{2,1,0:T(8,128)(2,1)} %bitcast.23, bf16[32,128]{1,0:T(8,128)(2,1)} %bitcast.25, bf16[32,128]{1,0:T(8,128)(2,1)} %bitcast.26), custom_call_target="tpu_custom_call" | custom-call | bytes 10500000 | tf_op jit(solution)/shard_map/pack/pallas_call | solution.py:593
  3.8 7.4 %all-to-all-start = ((bf16[32,144,128]{2,1,0:T(8,128)(2,1)}), bf16[32,144,128]{2,1,0:T(8,128)(2,1)}, u32[]{:S(2)}, u32[]{:S(2)}) async-start(bf16[32,144,128]{2,1,0:T(8,128)(2,1)} %pack.1), calls=%async_computation | async-start | bytes 2359296 | tf_op jit(solution)/shard_map/all_to_all | solution.py:610
  11.2 0.0 copy-done
  11.2 0.0 copy-start.2
  11.2 1.6 %copy-done.2 = f32[4,137,8,128]{3,2,1,0:T(8,128)S(1)} copy-done((f32[4,137,8,128]{3,2,1,0:T(8,128)S(1)}, f32[4,137,8,128]{3,2,1,0:T(8,128)}, u32[]{:S(2)}) %copy-start.2) | copy-done | bytes 2244632
  12.8 5.2 %filter_local.1 = (f32[61440,128]{1,0:T(8,128)}, f32[5120,128]{1,0:T(8,128)S(1)}, f32[5120,128]{1,0:T(8,128)S(1)}, f32[5120,128]{1,0:T(8,128)S(1)}, f32[4,40,128]{2,1,0:T(8,128)S(1)}) custom-call(f32[4384,128]{1,0:T(8,128)S(1)} %bitcast.15, f32[4384,128]{1,0:T(8,128)S(1)} %bitcast.19), custom_call_target="tpu_custom_call" | custom-call | bytes 21000000 | tf_op jit(solution)/shard_map/filter_local/pallas_call | solution.py:628
  18.1 11.7 %all-gather = f32[32,40,128]{2,1,0:T(8,128)S(1)} all-gather(f32[4,40,128]{2,1,0:T(8,128)S(1)} %get-tuple-element.29), channel_id=2, replica_groups=mesh['lon'=8,'lat'=4] {'lon'}, dimensions={0}, use_global_device_ids=true | all-gather | bytes 737280 | tf_op jit(solution)/shard_map/all_gather | solution.py:644
  29.8 1.2 %edges.1 = (bf16[1152,128]{1,0:T(8,128)(2,1)S(1)}, bf16[1152,128]{1,0:T(8,128)(2,1)S(1)}, f32[2,40,128]{2,1,0:T(8,128)S(1)}) custom-call(f32[8,4,40,128]{3,2,1,0:T(8,128)S(1)} %bitcast.17, f32[5120,128]{1,0:T(8,128)S(1)} %get-tuple-element.30.w0_t, f32[5120,128]{1,0:T(8,128)S(1)} %get-tuple-element.31.w1_t, f32[5120,128]{1,0:T(8,128)S(1)} %get-tuple-element.32.s_t), custom_call_target="tpu_custom_call" | custom-call | bytes 3500000 | tf_op jit(solution)/shard_map/edges/pallas_call | solution.py:648
  30.9 3.6 %collective-permute-start = (bf16[1152,128]{1,0:T(8,128)(2,1)S(1)}, bf16[1152,128]{1,0:T(8,128)(2,1)S(1)}, u32[]{:S(2)}, u32[]{:S(2)}) collective-permute-start(bf16[1152,128]{1,0:T(8,128)(2,1)S(1)} %get-tuple-element.38), channel_id=1, source_target_pairs={{0,1},{1,0},{2,3},{3,2},{4,5},{5,4},{6,7},{7,6},{8,9},{9,8},{10,11... | collective-permute-start | bytes 884744 | tf_op jit(solution)/shard_map/ppermute | solution.py:662
  34.5 1.4 %collective-permute-start.1 = (bf16[1152,128]{1,0:T(8,128)(2,1)S(1)}, bf16[1152,128]{1,0:T(8,128)(2,1)}, u32[]{:S(2)}, u32[]{:S(2)}) collective-permute-start(bf16[1152,128]{1,0:T(8,128)(2,1)S(1)} %get-tuple-element.39), channel_id=1, source_target_pairs={{1,2},{2,1},{5,6},{6,5},{9,10},{10,9},{13,14},{14,13},{17,18},{18,... | collective-permute-start | bytes 884744 | tf_op jit(solution)/shard_map/ppermute | solution.py:663
  35.9 0.5 prepare.1
  36.4 2.3 %interior.1 = (bf16[4,288,256]{2,1,0:T(8,128)(2,1)S(1)}, f32[5,4,128,128]{3,2,1,0:T(8,128)S(1)}) custom-call(f32[2,40,128]{2,1,0:T(8,128)S(1)} %get-tuple-element.33.entering, f32[5120,128]{1,0:T(8,128)S(1)} %get-tuple-element.30.w0_t, f32[5120,128]{1,0:T(8,128)S(1)} %get-tuple-element.31.w1_t, f32[5120,128]{1,0:T(8,128)S(1)} %get-tuple-element.32.s_t, ...), custom_call_target="tpu_custom_call" | custom-call | bytes 10500000 | tf_op jit(solution)/shard_map/interior/pallas_call | solution.py:668
  38.7 0.0 copy-start.3
  38.7 1.0 %copy-done.3 = f32[5,4,128,128]{3,2,1,0:T(8,128)} copy-done((f32[5,4,128,128]{3,2,1,0:T(8,128)}, f32[5,4,128,128]{3,2,1,0:T(8,128)S(1)}, u32[]{:S(2)}) %copy-start.3) | copy-done | bytes 1310744
  39.7 0.8 copy-done.6
  40.6 3.4 %collective-permute-done.first_far = bf16[1152,128]{1,0:T(8,128)(2,1)S(1)} collective-permute-done((bf16[1152,128]{1,0:T(8,128)(2,1)S(1)}, bf16[1152,128]{1,0:T(8,128)(2,1)S(1)}, u32[]{:S(2)}, u32[]{:S(2)}) %collective-permute-start) | collective-permute-done | bytes 294944 | tf_op jit(solution)/shard_map/ppermute | solution.py:662
  44.0 0.0 collective-permute-done.1.second_far
  44.0 0.0 all-to-all-done.jacobian_far
  44.0 0.7 copy-done.10
  44.7 13.9 %observe.1 = (f32[60,1024,128]{2,1,0:T(8,128)}, bf16[1168,128]{1,0:T(8,128)(2,1)}, bf16[1168,128]{1,0:T(8,128)(2,1)}, f32[8,128]{1,0:T(8,128)}, f32[8,128]{1,0:T(8,128)}, /*index=5*/f32[8,128]{1,0:T(8,128)}) custom-call(s32[32]{0:T(128)} %bitcast.27, s32[32]{0:T(128)} %bitcast.28, s32[32]{0:T(128)} %bitcast.29, s32[32,128]{1,0:T(8,128)} %bitcast.24, ...), custom_call_target="tpu_custom_call" | custom-call | bytes 49000000 | tf_op jit(solution)/shard_map/observe/pallas_call | solution.py:684
  58.6 2.5 %collective-permute-start.2 = (bf16[1168,128]{1,0:T(8,128)(2,1)}, bf16[1168,128]{1,0:T(8,128)(2,1)S(1)}, u32[]{:S(2)}, u32[]{:S(2)}) collective-permute-start(bf16[1168,128]{1,0:T(8,128)(2,1)} %get-tuple-element.43), channel_id=1, source_target_pairs={{0,1},{1,0},{2,3},{3,2},{4,5},{5,4},{6,7},{7,6},{8,9},{9,8},{10,11... | collective-permute-start | bytes 897032 | tf_op jit(solution)/shard_map/ppermute | solution.py:722
  61.1 0.7 collective-permute-start.3
  61.8 2.8 %collective-permute-start.4 = (f32[8,128]{1,0:T(8,128)}, f32[8,128]{1,0:T(8,128)S(1)}, u32[]{:S(2)}, u32[]{:S(2)}) collective-permute-start(f32[8,128]{1,0:T(8,128)} %get-tuple-element.48), channel_id=1, source_target_pairs={{0,3},{3,0},{4,7},{7,4},{8,11},{11,8},{12,15},{15,12},{16,19},{19,... | collective-permute-start | bytes 12296 | tf_op jit(solution)/shard_map/ppermute | solution.py:718
  64.6 0.8 collective-permute-start.5
  65.4 4.0 %respond.1 = (f32[5120,128]{1,0:T(8,128)S(1)}, f32[5120,128]{1,0:T(8,128)S(1)}, f32[5120,128]{1,0:T(8,128)S(1)}, f32[5120,128]{1,0:T(8,128)S(1)}, f32[5120,128]{1,0:T(8,128)S(1)}) custom-call(f32[60,1024,128]{2,1,0:T(8,128)} %get-tuple-element.40.lift_far, f32[5,5,8,128]{3,2,1,0:T(8,128)S(1)} %copy-done.5, f32[61440,128]{1,0:T(8,128)} %get-tuple-element.41.a_far), custom_call_target="tpu_custom_call" | custom-call | bytes 17500000 | tf_op jit(solution)/shard_map/respond/pallas_call | solution.py:725
  69.4 0.4 collective-permute-done.4.rest_1_
  69.8 1.1 %collective-permute-done.5.rest_2_ = f32[8,128]{1,0:T(8,128)S(1)} collective-permute-done((f32[8,128]{1,0:T(8,128)}, f32[8,128]{1,0:T(8,128)S(1)}, u32[]{:S(2)}, u32[]{:S(2)}) %collective-permute-start.5) | collective-permute-done | bytes 4128 | tf_op jit(solution)/shard_map/ppermute | solution.py:721
  70.9 0.0 collective-permute-done.2.first
  70.9 0.0 collective-permute-done.3.second
  70.9 1.7 %adjoint_local.1 = (f32[5120,128]{1,0:T(8,128)S(1)}, f32[120,128]{1,0:T(8,128)S(1)}) custom-call(f32[5120,128]{1,0:T(8,128)S(1)} %get-tuple-element.42.spread, bf16[1168,128]{1,0:T(8,128)(2,1)S(1)} %collective-permute-done.2.first, bf16[1168,128]{1,0:T(8,128)(2,1)S(1)} %collective-permute-done.3.second, f32[5120,128]{1,0:T(8,128)S(1)} %get-tuple-element.45.a_t, ...), custom_call_target="tpu_custom_call" | custom-call | bytes 10500000 | tf_op jit(solution)/shard_map/adjoint_local/pallas_call | solution.py:739
  72.6 10.5 %all-gather.1 = f32[960,128]{1,0:T(8,128)S(1)} all-gather(f32[120,128]{1,0:T(8,128)S(1)} %get-tuple-element.50), channel_id=3, replica_groups=mesh['lon'=8,'lat'=4] {'lon'}, dimensions={0}, use_global_device_ids=true | all-gather | bytes 552960 | tf_op jit(solution)/shard_map/all_gather | solution.py:749
  83.1 3.2 %gradient.1 = (f32[4384,128]{1,0:T(8,128)}, f32[32,128]{1,0:T(8,128)}) custom-call(f32[8,4,40,128]{3,2,1,0:T(8,128)S(1)} %bitcast.18, f32[8,120,128]{2,1,0:T(8,128)S(1)} %bitcast.20, f32[5120,128]{1,0:T(8,128)S(1)} %get-tuple-element.51.u_t, f32[5120,128]{1,0:T(8,128)S(1)} %get-tuple-element.52.gq_t, f32[5120,128]{1,0:T(8,128)S(1)} %get-tuple-element.53.gp_t, ...), custom_call_target="tpu_custom_call" | custom-call | bytes 10500000 | tf_op jit(solution)/shard_map/gradient/pallas_call | solution.py:750
  (15 shorter events, 0.0 us)
Async XLA Ops:
  0.6 10.6 %copy-start = (f32[4,137,8,128]{3,2,1,0:T(8,128)S(1)}, f32[4,137,8,128]{3,2,1,0:T(8,128)}, u32[]{:S(2)}) copy-start(f32[4,137,8,128]{3,2,1,0:T(8,128)} %param.11) | copy-start | bytes 6733828
  3.8 40.2 %all-to-all-start = ((bf16[32,144,128]{2,1,0:T(8,128)(2,1)}), bf16[32,144,128]{2,1,0:T(8,128)(2,1)}, u32[]{:S(2)}, u32[]{:S(2)}) async-start(bf16[32,144,128]{2,1,0:T(8,128)(2,1)} %pack.1), calls=%async_computation | async-start | bytes 2359296 | tf_op jit(solution)/shard_map/all_to_all | solution.py:610
  11.2 1.6 %copy-start.2 = (f32[4,137,8,128]{3,2,1,0:T(8,128)S(1)}, f32[4,137,8,128]{3,2,1,0:T(8,128)}, u32[]{:S(2)}) copy-start(f32[4,137,8,128]{3,2,1,0:T(8,128)} %param.12) | copy-start | bytes 6733828
  29.8 6.1 %copy-start.7 = (f32[4,137,137]{2,0,1:T(4,128)S(1)}, f32[4,137,137]{2,0,1:T(4,128)}, u32[]{:S(2)}) copy-start(f32[4,137,137]{2,0,1:T(4,128)} %param.14) | copy-start | bytes 900916
  29.8 6.1 %copy-start.8 = (f32[4,5,8]{2,0,1:T(4,128)S(1)}, f32[4,5,8]{2,0,1:T(4,128)}, u32[]{:S(2)}) copy-start(f32[4,5,8]{2,0,1:T(4,128)} %param.13) | copy-start | bytes 1924
  30.9 13.1 %collective-permute-start = (bf16[1152,128]{1,0:T(8,128)(2,1)S(1)}, bf16[1152,128]{1,0:T(8,128)(2,1)S(1)}, u32[]{:S(2)}, u32[]{:S(2)}) collective-permute-start(bf16[1152,128]{1,0:T(8,128)(2,1)S(1)} %get-tuple-element.38), channel_id=1, source_target_pairs={{0,1},{1,0},{2,3},{3,2},{4,5},{5,4},{6,7},{7,6},{8,9},{9,8},{10,11... | collective-permute-start | bytes 884744 | tf_op jit(solution)/shard_map/ppermute | solution.py:662
  34.5 9.5 %collective-permute-start.1 = (bf16[1152,128]{1,0:T(8,128)(2,1)S(1)}, bf16[1152,128]{1,0:T(8,128)(2,1)}, u32[]{:S(2)}, u32[]{:S(2)}) collective-permute-start(bf16[1152,128]{1,0:T(8,128)(2,1)S(1)} %get-tuple-element.39), channel_id=1, source_target_pairs={{1,2},{2,1},{5,6},{6,5},{9,10},{10,9},{13,14},{14,13},{17,18},{18,... | collective-permute-start | bytes 884744 | tf_op jit(solution)/shard_map/ppermute | solution.py:663
  36.3 2.3 %copy-start.1 = (bf16[4,144,512]{2,1,0:T(8,128)(2,1)}, bf16[4,144,512]{2,1,0:T(8,128)(2,1)S(1)}, u32[]{:S(2)}) copy-start(bf16[4,144,512]{2,1,0:T(8,128)(2,1)S(1)} %get-tuple-element.35.vert.vert_far) | copy-start | bytes 1769476
  36.4 2.3 %copy-start.4 = (f32[5,5,8,128]{3,2,1,0:T(8,128)}, f32[5,5,8,128]{3,2,1,0:T(8,128)S(1)}, u32[]{:S(2)}) copy-start(f32[5,5,8,128]{3,2,1,0:T(8,128)S(1)} %get-tuple-element.34.taps.taps_far) | copy-start | bytes 307204
  38.7 1.1 %copy-start.3 = (f32[5,4,128,128]{3,2,1,0:T(8,128)}, f32[5,4,128,128]{3,2,1,0:T(8,128)S(1)}, u32[]{:S(2)}) copy-start(f32[5,4,128,128]{3,2,1,0:T(8,128)S(1)} %get-tuple-element.37.partial_far) | copy-start | bytes 3932164
  39.7 0.8 copy-start.6
  44.0 0.7 copy-start.10
  44.0 21.4 %copy-start.5 = (f32[5,5,8,128]{3,2,1,0:T(8,128)S(1)}, f32[5,5,8,128]{3,2,1,0:T(8,128)}, u32[]{:S(2)}) copy-start(f32[5,5,8,128]{3,2,1,0:T(8,128)} %copy-done.4) | copy-start | bytes 307204
  58.6 12.2 %collective-permute-start.2 = (bf16[1168,128]{1,0:T(8,128)(2,1)}, bf16[1168,128]{1,0:T(8,128)(2,1)S(1)}, u32[]{:S(2)}, u32[]{:S(2)}) collective-permute-start(bf16[1168,128]{1,0:T(8,128)(2,1)} %get-tuple-element.43), channel_id=1, source_target_pairs={{0,1},{1,0},{2,3},{3,2},{4,5},{5,4},{6,7},{7,6},{8,9},{9,8},{10,11... | collective-permute-start | bytes 897032 | tf_op jit(solution)/shard_map/ppermute | solution.py:722
  61.1 9.8 %collective-permute-start.3 = (bf16[1168,128]{1,0:T(8,128)(2,1)}, bf16[1168,128]{1,0:T(8,128)(2,1)S(1)}, u32[]{:S(2)}, u32[]{:S(2)}) collective-permute-start(bf16[1168,128]{1,0:T(8,128)(2,1)} %get-tuple-element.44), channel_id=1, source_target_pairs={{1,2},{2,1},{5,6},{6,5},{9,10},{10,9},{13,14},{14,13},{17,18},{18,... | collective-permute-start | bytes 897032 | tf_op jit(solution)/shard_map/ppermute | solution.py:723
  61.8 8.0 %collective-permute-start.4 = (f32[8,128]{1,0:T(8,128)}, f32[8,128]{1,0:T(8,128)S(1)}, u32[]{:S(2)}, u32[]{:S(2)}) collective-permute-start(f32[8,128]{1,0:T(8,128)} %get-tuple-element.48), channel_id=1, source_target_pairs={{0,3},{3,0},{4,7},{7,4},{8,11},{11,8},{12,15},{15,12},{16,19},{19,... | collective-permute-start | bytes 12296 | tf_op jit(solution)/shard_map/ppermute | solution.py:718
  64.6 6.2 %collective-permute-start.5 = (f32[8,128]{1,0:T(8,128)}, f32[8,128]{1,0:T(8,128)S(1)}, u32[]{:S(2)}, u32[]{:S(2)}) collective-permute-start(f32[8,128]{1,0:T(8,128)} %get-tuple-element.49), channel_id=1, source_target_pairs={{0,2},{1,3},{2,0},{3,1},{4,6},{5,7},{6,4},{7,5},{8,10},{9,11},{10,... | collective-permute-start | bytes 12296 | tf_op jit(solution)/shard_map/ppermute | solution.py:721
  65.4 5.5 %copy-start.9 = (f32[8,128]{1,0:T(8,128)S(1)}, f32[8,128]{1,0:T(8,128)}, u32[]{:S(2)}) copy-start(f32[8,128]{1,0:T(8,128)} %get-tuple-element.47.rest_0_) | copy-start | bytes 12292

commit v3 on v2

--- a/solution.py
+++ b/solution.py
@@ -9,8 +9,10 @@
 
 LANES = 128
 HALO = 2
+OBS_MIB = 28
 FAR_MIB = 60
 ROOM = 12
+FAR = 24
 CELLS = 256
 GROUP = 4
 BF = jnp.bfloat16
@@ -249,7 +251,10 @@
     return out.astype(BF)
 
 
-def interior_kernel(fields, rows, entering, w0_t, w1_t, s_t, taps, vert, state, partial, western, mixed):
+def interior_kernel(
+    fields, rows, entering, w0_t, w1_t, s_t, taps, vert, state_far, partial_far,
+    state, partial, western, mixed, left,
+):
     blocks = fields + 1
     per = blocks * rows
     for n in range(per):
@@ -267,11 +272,32 @@
             else:
                 partial[b, j if j < HALO else j - rows + 2 * HALO] = total
     padded = vert.shape[1]
+    leaving = fetch([(partial, partial_far.at[pl.ds(0, blocks)])], left.at[pl.ds(fields, 1)])
     for f in range(fields):
         for h in range(state.shape[1] // padded):
             at = pl.ds(h * CELLS, CELLS)
             both = jnp.concatenate([mixed[f, at, :], mixed[fields, at, :]], axis=1)
             state[f, pl.ds(h * padded, padded), :] = vertical(vert[f], both)
+        leaving += fetch([(state.at[f], state_far.at[f])], left.at[pl.ds(f, 1)])
+    for copy in leaving:
+        copy.wait()
+
+
+def stage_kernel(
+    fields, levels, rows, inner_far, partial_far, jacobian_far, vert_corr, lat_taps,
+    inner, partial, jacobian, vert, taps, wide, arrived,
+):
+    copies = fetch(
+        [
+            (jacobian_far, jacobian),
+            (partial_far.at[pl.ds(0, fields + 1)], partial),
+            (inner_far.at[pl.ds(0, fields)], inner),
+        ],
+        arrived,
+    )
+    prepare_kernel(fields, levels, rows, vert_corr, lat_taps, vert, taps, wide)
+    for copy in copies:
+        copy.wait()
 
 
 def route_of(delta, bands):
@@ -283,25 +309,20 @@
 
 def observe_kernel(
     fields, levels, rows, bands, field, owner, live, cells,
-    inner_far, partial_far, first_far, second_far, taps_far, vert_far, jacobian_far, *rest,
+    inner, partial, first_far, second_far, taps, vert, jacobian, *rest,
 ):
-    lift_far, first_out, second_out = rest[:3]
+    lift, first_out, second_out = rest[:3]
     residuals = rest[3 : 2 + bands]
     (
-        state, partial, beside, taps, vert, jacobian, mixed, lift, sides,
-        route, order, number, group_field, group_start, acc, arrived, left,
+        state, beside, mixed, sides,
+        route, order, number, group_field, group_start, acc, arrived,
     ) = rest[2 + bands :]
     blocks = fields + 1
     band = lax.axis_index("lat")
     odd = band % 2
     after, before = beside.at[0], beside.at[1]
     low, high = sides.at[odd], sides.at[1 - odd]
-    copies = fetch(
-        [(first_far, beside.at[odd]), (second_far, beside.at[1 - odd])]
-        + [(taps_far, taps), (partial_far, partial)]
-        + [(vert_far, vert)],
-        arrived,
-    )
+    copies = fetch([(first_far, beside.at[odd]), (second_far, beside.at[1 - odd])], arrived)
     total = field.shape[0]
     padded = vert.shape[1]
     parts = rows * LANES // CELLS
@@ -331,16 +352,10 @@
         groups = groups + here
     acc[...] = jnp.zeros_like(acc)
 
-    for n in range(4):
-        copies[n].wait()
-    copies += fetch(
-        [(jacobian_far, jacobian)]
-        + [
-            (inner_far.at[f], state.at[f, pl.ds(padded, (parts - 2) * padded)])
-            for f in range(fields)
-        ],
-        arrived.at[pl.ds(5, 1 + fields)],
-    )
+    for f in range(fields):
+        state[f, pl.ds(padded, (parts - 2) * padded), :] = inner[f]
+    for copy in copies:
+        copy.wait()
 
     def tap_of(t, b, j):
         return taps[t, b, j : j + 1, :]
@@ -356,15 +371,12 @@
         )
         for n, line in enumerate(outer_rows):
             mixed[b, pl.ds(n * LANES, LANES), :] = line
-    copies[4].wait()
     for f in range(fields):
         for h in range(2):
             at = pl.ds(h * CELLS, CELLS)
             both = jnp.concatenate([mixed[f, at, :], mixed[fields, at, :]], axis=1)
             state[f, pl.ds(h * (parts - 1) * padded, padded), :] = vertical(vert[f], both)
 
-    for n in range(1 + fields):
-        copies[5 + n].wait()
     site = lax.broadcasted_iota(jnp.int32, (CELLS, wide), 0)
     slot = lax.broadcasted_iota(jnp.int32, (1, LANES), 1)
     spare = (bands + 1) * sectors
@@ -393,9 +405,9 @@
         model = jnp.sum(j * columns, axis=0, keepdims=True)
         value, precision = j[levels : levels + 1], j[levels + 1 : levels + 2]
         res = precision * (model - value)
-        adjoint = j * res
+        adjoint = (j * res).astype(BF)
         adjoint = jnp.concatenate(
-            [jnp.where(part == h, adjoint, 0.0).astype(BF) for h in range(parts)], axis=0
+            [adjoint * (part == h).astype(F32).astype(BF) for h in range(parts)], axis=0
         )
         for n in range(GROUP):
             route[pl.ds(at[n], 1), :] = res[:, n * LANES : (n + 1) * LANES]
@@ -403,7 +415,6 @@
         return 0
 
     lax.fori_loop(0, groups, group, 0)
-    leaving = []
     for f in range(fields):
         for h in range(parts):
             forcing = acc[f, pl.ds(h * padded, padded), :].astype(BF)
@@ -415,8 +426,6 @@
                 lift[fields, at, :] = out[:, LANES:]
             else:
                 lift[fields, at, :] += out[:, LANES:]
-        leaving += fetch([(lift.at[f], lift_far.at[f])], left.at[pl.ds(f, 1)])
-    leaving += fetch([(lift.at[fields], lift_far.at[fields])], left.at[pl.ds(fields, 1)])
 
     for b in range(blocks):
         def line(j):
@@ -433,18 +442,15 @@
     for n, dst in ((1, low), (2, high)):
         both = jnp.concatenate(split(route[pl.ds(n * sectors, sectors), :]), axis=0)
         dst[pl.ds(riding, 2 * sectors), :] = both
-    leaving += fetch(
-        [(sides.at[0], first_out), (sides.at[1], second_out)], left.at[pl.ds(blocks, 2)]
-    )
+    first_out[...] = sides[0]
+    second_out[...] = sides[1]
     for n, dst in enumerate(residuals):
         source = 0 if n == 0 else n + 2
         dst[...] = route[pl.ds(source * sectors, sectors), :]
-    for copy in leaving:
-        copy.wait()
 
 
 def respond_kernel(
-    fields, rows, lift_far, taps, a_far, a_t, g_t, gq_t, gp_t, spread, lift, pe_t, arrived
+    fields, rows, lift, taps, a_far, a_t, g_t, gq_t, gp_t, spread, pe_t, arrived
 ):
     blocks = fields + 1
     per = blocks * rows
@@ -473,15 +479,9 @@
     p = one
     for c, copy in enumerate(copies):
         copy.wait()
-        if c == chunks // 2:
-            copies_lift = fetch(
-                [(lift_far.at[b], lift.at[b]) for b in range(blocks)],
-                arrived.at[pl.ds(chunks, blocks)],
-            )
         p = lax.fori_loop(c * span, (c + 1) * span, east, p, unroll=4)
     lax.fori_loop(0, LANES, west, (jnp.zeros_like(one), one), unroll=4)
     for b in range(blocks):
-        copies_lift[b].wait()
         for m in range(rows):
             total = taps[HALO, b, m : m + 1, :] * lift[b, pl.ds(m * LANES, LANES), :]
             for t in range(2 * HALO + 1):
@@ -667,35 +667,55 @@
     partial_shape = (blocks, 2 * HALO, longitudes, LANES)
     inner, partial = pl.pallas_call(
         functools.partial(interior_kernel, fields, rows),
-        out_shape=[sds(inner_shape, BF), sds(partial_shape)],
+        out_shape=[
+            sds((FAR * fields, *inner_shape[1:]), BF), sds((FAR * blocks, *partial_shape[1:]))
+        ],
         in_specs=[VMEM] * 6,
-        out_specs=[VMEM] * 2,
+        out_specs=[HBM] * 2,
         scratch_shapes=[
+            pltpu.VMEM(inner_shape, BF),
+            pltpu.VMEM(partial_shape, F32),
             pltpu.VMEM((per, longitudes, LANES), F32),
             pltpu.VMEM((blocks, sites - 2 * CELLS, LANES), F32),
+            pltpu.SemaphoreType.DMA((fields + 1,)),
         ],
-        compiler_params=params(16),
+        compiler_params=params(44),
         cost_estimate=cost(3),
         name="interior",
     )(entering, w0_t, w1_t, s_t, taps, vert)
 
     outward = sds((halo_rows + 2 * count, LANES), BF)
     lift_shape = (blocks, sites, LANES)
+    staged = [
+        sds(inner_shape, BF), sds(partial_shape), sds(jacobian.shape, BF), sds(vert.shape, BF),
+        sds(taps.shape),
+    ]
+    inner, partial, jacobian, near_vert, near_taps = pl.pallas_call(
+        functools.partial(stage_kernel, *sizes),
+        out_shape=staged,
+        in_specs=[HBM] * 3 + [VMEM] * 2,
+        out_specs=[VMEM] * 5,
+        scratch_shapes=[
+            pltpu.VMEM((fields, padded, 2 * LANES), F32),
+            pltpu.SemaphoreType.DMA((3,)),
+        ],
+        compiler_params=params(44),
+        cost_estimate=cost(3),
+        name="stage",
+    )(
+        inner, partial, jacobian,
+        jnp.transpose(vert_corr, (1, 0, 2)), jnp.transpose(lat_taps, (1, 0, 2)),
+    )
     lift, first, second, *residuals = pl.pallas_call(
         functools.partial(observe_kernel, *sizes, bands),
-        out_shape=[sds((ROOM * blocks, sites, LANES)), outward, outward]
+        out_shape=[sds(lift_shape), outward, outward]
         + [sds((count, slots))] * (bands - 1),
-        in_specs=[SMEM] * 3 + [VMEM] + [HBM] * 7,
-        out_specs=[HBM] * 3 + [VMEM] * (bands - 1),
+        in_specs=[SMEM] * 3 + [VMEM] * 3 + [HBM] * 2 + [VMEM] * 3,
+        out_specs=[VMEM] * (bands + 2),
         scratch_shapes=[
             pltpu.VMEM((fields, parts * padded, CELLS), BF),
-            pltpu.VMEM(partial_shape, F32),
             pltpu.VMEM((2, *halo_shape.shape), BF),
-            pltpu.VMEM(taps.shape, F32),
-            pltpu.VMEM(vert.shape, BF),
-            pltpu.VMEM(jacobian.shape, BF),
             pltpu.VMEM((blocks, 2 * CELLS, LANES), F32),
-            pltpu.VMEM(lift_shape, F32),
             pltpu.VMEM((2, *outward.shape), BF),
             pltpu.VMEM(((bands + 1) * count + 8, slots), F32),
             pltpu.SMEM((fields * total,), jnp.int32),
@@ -703,15 +723,14 @@
             pltpu.SMEM((total // GROUP + fields,), jnp.int32),
             pltpu.SMEM((total // GROUP + fields,), jnp.int32),
             pltpu.VMEM((fields, parts * padded, CELLS), F32),
-            pltpu.SemaphoreType.DMA((6 + fields,)),
-            pltpu.SemaphoreType.DMA((blocks + 2,)),
+            pltpu.SemaphoreType.DMA((2,)),
         ],
-        compiler_params=params(FAR_MIB),
+        compiler_params=params(OBS_MIB),
         cost_estimate=cost(14),
         name="observe",
     )(
         obs_field[0], obs_owner[0], obs_count[0], obs_cell[0],
-        inner, partial, first, second, taps, vert, jacobian,
+        inner, partial, first, second, near_taps, near_vert, jacobian,
     )
 
     swap = [(0, bands - 1), (bands - 1, 0)]
@@ -725,13 +744,9 @@
     a_again, g_t, gq_t, gp_t, spread = pl.pallas_call(
         functools.partial(respond_kernel, fields, rows),
         out_shape=[line] * 5,
-        in_specs=[HBM, VMEM, HBM],
+        in_specs=[VMEM, VMEM, HBM],
         out_specs=[VMEM] * 5,
-        scratch_shapes=[
-            pltpu.VMEM(lift_shape, F32),
-            tiles,
-            pltpu.SemaphoreType.DMA((4 + blocks,)),
-        ],
+        scratch_shapes=[tiles, pltpu.SemaphoreType.DMA((4,))],
         compiler_params=params(36),
         cost_estimate=cost(5),
         name="respond",

time: 86.9 us -> 84 us (0.967)
  waiting for transfers between devices: 4.9 us -> 2.36 us
  local copies, waits for them, and re-layouts: 4.27 us -> 2.31 us
  starting transfers between devices: 19.1 us -> 20.5 us
    pallas_call x1, Pallas kernels: 13.9 us -> 10.5 us  [local(): pl.pallas_call(functools.partial(observe_kernel, *sizes, bands), out_shap...]
    ppermute x1, starting transfers between devices: 2.85 us -> 5.42 us  [local(): arrived = [residuals[0], lax.ppermute(residuals[1], 'lat', swap)]]
    ppermute x2, waiting for transfers between devices: 3.44 us -> 1.42 us  [local(): first = lax.ppermute(first, 'lat', even)]
    unnamed x22 -> x20, local copies, waits for them, and re-layouts: 4.27 us -> 2.31 us
    pallas_call x0 -> x1, Pallas kernels: none -> 1.88 us  [local(): pl.pallas_call(functools.partial(stage_kernel, *sizes), out_shape=staged,...]
    pallas_call x1, Pallas kernels: 2.28 us -> 3.46 us  [local(): pl.pallas_call(functools.partial(interior_kernel, fields, rows), out_shap...]
  transfers between devices with their start and end apart: 7 -> 7, of which waited for: 3 -> 2; matrix products, arithmetic and copies ran while one was open for 0% -> 0% of each run, Pallas kernels for 15% -> 20%
where the time goes in v3:
time: 84 us
  Pallas kernels  35.8 us (43%)
  blocking collectives  22.1 us (26%)
  starting transfers between devices  20.5 us (24%)
  waiting for transfers between devices  2.36 us (3%)
  local copies, waits for them, and re-layouts  2.31 us (3%)
  between operations  0.98 us (1%)
    all_gather x1, blocking collectives, local(): gathered = lax.all_gather(ends, 'lon')  11.7 us
    pallas_call x1, Pallas kernels, local(): pl.pallas_call(functools.partial(observe_kernel, *sizes, bands), out_shap...  10.5 us
    all_gather x1, blocking collectives, local(): gathered_back = lax.all_gather(ends, 'lon')  10.4 us
    all_to_all x1, starting transfers between devices, local(): lax.all_to_all(sent, both, split_axis=0, concat_axis=0, tiled=True)  7.42 us
    ppermute x1, starting transfers between devices, local(): arrived = [residuals[0], lax.ppermute(residuals[1], 'lat', swap)]  5.42 us
    ppermute x2, starting transfers between devices, local(): first = lax.ppermute(first, 'lat', even)  5.35 us
    pallas_call x1, Pallas kernels, local(): pl.pallas_call(functools.partial(filter_kernel, *sizes), out_shape=[sds((...  5.23 us
    pallas_call x1, Pallas kernels, local(): pl.pallas_call(functools.partial(respond_kernel, fields, rows), out_shape...  3.96 us
  transfers between devices with their start and end apart: 7, of which 2 were waited for; matrix products, arithmetic and copies ran while one was open for 0% of the time, Pallas kernels for 20%

profile of v3, /device:TPU:0, one launch (start us, length us, event | category | flops | bytes accessed | tf_op | source)
XLA Modules:
  0.0 84.0 jit_solution(6425193169266651042)
XLA Ops:
  0.6 0.0 copy-start
  0.6 3.1 %pack.1 = bf16[32,144,128]{2,1,0:T(8,128)(2,1)} custom-call(bf16[137,32,128]{2,1,0:T(8,128)(2,1)} %bitcast.29, bf16[32,128]{1,0:T(8,128)(2,1)} %bitcast.30, bf16[32,128]{1,0:T(8,128)(2,1)} %bitcast.31), custom_call_target="tpu_custom_call" | custom-call | bytes 10500000 | tf_op jit(solution)/shard_map/pack/pallas_call | solution.py:593
  3.8 7.4 %all-to-all-start = ((bf16[32,144,128]{2,1,0:T(8,128)(2,1)}), bf16[32,144,128]{2,1,0:T(8,128)(2,1)}, u32[]{:S(2)}, u32[]{:S(2)}) async-start(bf16[32,144,128]{2,1,0:T(8,128)(2,1)} %pack.1), calls=%async_computation | async-start | bytes 2359296 | tf_op jit(solution)/shard_map/all_to_all | solution.py:610
  11.2 0.0 copy-start.1
  11.2 1.6 %copy-done.1 = f32[4,137,8,128]{3,2,1,0:T(8,128)S(1)} copy-done((f32[4,137,8,128]{3,2,1,0:T(8,128)S(1)}, f32[4,137,8,128]{3,2,1,0:T(8,128)}, u32[]{:S(2)}) %copy-start.1) | copy-done | bytes 2244632
  12.8 5.2 %filter_local.1 = (f32[61440,128]{1,0:T(8,128)}, f32[5120,128]{1,0:T(8,128)S(1)}, f32[5120,128]{1,0:T(8,128)S(1)}, f32[5120,128]{1,0:T(8,128)S(1)}, f32[4,40,128]{2,1,0:T(8,128)S(1)}) custom-call(f32[4384,128]{1,0:T(8,128)S(1)} %bitcast.15, f32[4384,128]{1,0:T(8,128)S(1)} %bitcast.19), custom_call_target="tpu_custom_call" | custom-call | bytes 21000000 | tf_op jit(solution)/shard_map/filter_local/pallas_call | solution.py:628
  18.1 11.7 %all-gather = f32[32,40,128]{2,1,0:T(8,128)S(1)} all-gather(f32[4,40,128]{2,1,0:T(8,128)S(1)} %get-tuple-element.34), channel_id=2, replica_groups=mesh['lon'=8,'lat'=4] {'lon'}, dimensions={0}, use_global_device_ids=true | all-gather | bytes 737280 | tf_op jit(solution)/shard_map/all_gather | solution.py:644
  29.8 2.0 %edges.1 = (bf16[1152,128]{1,0:T(8,128)(2,1)}, bf16[1152,128]{1,0:T(8,128)(2,1)}, f32[2,40,128]{2,1,0:T(8,128)S(1)}) custom-call(f32[8,4,40,128]{3,2,1,0:T(8,128)S(1)} %bitcast.17, f32[5120,128]{1,0:T(8,128)S(1)} %get-tuple-element.35.w0_t, f32[5120,128]{1,0:T(8,128)S(1)} %get-tuple-element.36.w1_t, f32[5120,128]{1,0:T(8,128)S(1)} %get-tuple-element.37.s_t), custom_call_target="tpu_custom_call" | custom-call | bytes 3500000 | tf_op jit(solution)/shard_map/edges/pallas_call | solution.py:648
  31.8 3.5 %collective-permute-start = (bf16[1152,128]{1,0:T(8,128)(2,1)}, bf16[1152,128]{1,0:T(8,128)(2,1)}, u32[]{:S(2)}, u32[]{:S(2)}) collective-permute-start(bf16[1152,128]{1,0:T(8,128)(2,1)} %get-tuple-element.45), channel_id=1, source_target_pairs={{0,1},{1,0},{2,3},{3,2},{4,5},{5,4},{6,7},{7,6},{8,9},{9,8},{10,11... | collective-permute-start | bytes 884744 | tf_op jit(solution)/shard_map/ppermute | solution.py:662
  35.3 1.4 %collective-permute-start.1 = (bf16[1152,128]{1,0:T(8,128)(2,1)}, bf16[1152,128]{1,0:T(8,128)(2,1)}, u32[]{:S(2)}, u32[]{:S(2)}) collective-permute-start(bf16[1152,128]{1,0:T(8,128)(2,1)} %get-tuple-element.46), channel_id=1, source_target_pairs={{1,2},{2,1},{5,6},{6,5},{9,10},{10,9},{13,14},{14,13},{17,18},{18,... | collective-permute-start | bytes 884744 | tf_op jit(solution)/shard_map/ppermute | solution.py:663
  36.6 0.0 copy-done.2
  36.7 0.5 prepare.1
  37.1 3.5 %interior.1 = (bf16[96,288,256]{2,1,0:T(8,128)(2,1)}, f32[120,4,128,128]{3,2,1,0:T(8,128)}) custom-call(f32[2,40,128]{2,1,0:T(8,128)S(1)} %get-tuple-element.38.entering, f32[5120,128]{1,0:T(8,128)S(1)} %get-tuple-element.35.w0_t, f32[5120,128]{1,0:T(8,128)S(1)} %get-tuple-element.36.w1_t, f32[5120,128]{1,0:T(8,128)S(1)} %get-tuple-element.37.s_t, ...), custom_call_target="tpu_custom_call" | custom-call | bytes 10500000 | tf_op jit(solution)/shard_map/interior/pallas_call | solution.py:668
  40.6 0.7 copy-done.3
  41.2 0.0 all-to-all-done.jacobian_far
  41.3 0.0 copy-start.9
  41.3 1.9 %stage.1 = (bf16[4,288,256]{2,1,0:T(8,128)(2,1)S(1)}, f32[5,4,128,128]{3,2,1,0:T(8,128)S(1)}, bf16[32,144,128]{2,1,0:T(8,128)(2,1)S(1)}, bf16[4,144,512]{2,1,0:T(8,128)(2,1)S(1)}, f32[5,5,8,128]{3,2,1,0:T(8,128)S(1)}) custom-call(bf16[96,288,256]{2,1,0:T(8,128)(2,1)} %get-tuple-element.41.inner_far, f32[120,4,128,128]{3,2,1,0:T(8,128)} %get-tuple-element.42.partial_far, ...), custom_call_target="tpu_custom_call" | custom-call | bytes 10500000 | tf_op jit(solution)/shard_map/stage/pallas_call | solution.py:693
  43.2 1.4 %collective-permute-done.first_far = bf16[1152,128]{1,0:T(8,128)(2,1)} collective-permute-done((bf16[1152,128]{1,0:T(8,128)(2,1)}, bf16[1152,128]{1,0:T(8,128)(2,1)}, u32[]{:S(2)}, u32[]{:S(2)}) %collective-permute-start) | collective-permute-done | bytes 294944 | tf_op jit(solution)/shard_map/ppermute | solution.py:662
  44.6 0.0 collective-permute-done.1.second_far
  44.6 10.5 %observe.1 = (f32[5,1024,128]{2,1,0:T(8,128)S(1)}, bf16[1168,128]{1,0:T(8,128)(2,1)S(1)}, bf16[1168,128]{1,0:T(8,128)(2,1)S(1)}, f32[8,128]{1,0:T(8,128)S(1)}, f...) custom-call(s32[32]{0:T(128)S(1)} %bitcast.26, s32[32]{0:T(128)S(1)} %bitcast.27, s32[32]{0:T(128)S(1)} %bitcast.28, ...), custom_call_target="tpu_custom_call" | custom-call | bytes 49000000 | tf_op jit(solution)/shard_map/observe/pallas_call | solution.py:709
  55.1 1.9 %collective-permute-start.2 = (bf16[1168,128]{1,0:T(8,128)(2,1)S(1)}, bf16[1168,128]{1,0:T(8,128)(2,1)S(1)}, u32[]{:S(2)}, u32[]{:S(2)}) collective-permute-start(bf16[1168,128]{1,0:T(8,128)(2,1)S(1)} %get-tuple-element.53), channel_id=1, source_target_pairs={{0,1},{1,0},{2,3},{3,2},{4,5},{5,4},{6,7},{7,6},{8,9},{9,8},{10,11... | collective-permute-start | bytes 897032 | tf_op jit(solution)/shard_map/ppermute | solution.py:741
  57.0 0.8 %collective-permute-start.3 = (bf16[1168,128]{1,0:T(8,128)(2,1)S(1)}, bf16[1168,128]{1,0:T(8,128)(2,1)S(1)}, u32[]{:S(2)}, u32[]{:S(2)}) collective-permute-start(bf16[1168,128]{1,0:T(8,128)(2,1)S(1)} %get-tuple-element.54), channel_id=1, source_target_pairs={{1,2},{2,1},{5,6},{6,5},{9,10},{10,9},{13,14},{14,13},{17,18},{18,... | collective-permute-start | bytes 897032 | tf_op jit(solution)/shard_map/ppermute | solution.py:742
  57.8 5.4 %collective-permute-start.4 = (f32[8,128]{1,0:T(8,128)S(1)}, f32[8,128]{1,0:T(8,128)S(1)}, u32[]{:S(2)}, u32[]{:S(2)}) collective-permute-start(f32[8,128]{1,0:T(8,128)S(1)} %get-tuple-element.58), channel_id=1, source_target_pairs={{0,3},{3,0},{4,7},{7,4},{8,11},{11,8},{12,15},{15,12},{16,19},{19,... | collective-permute-start | bytes 12296 | tf_op jit(solution)/shard_map/ppermute | solution.py:737
  63.3 0.1 collective-permute-start.5
  63.3 4.0 %respond.1 = (f32[5120,128]{1,0:T(8,128)S(1)}, f32[5120,128]{1,0:T(8,128)S(1)}, f32[5120,128]{1,0:T(8,128)S(1)}, f32[5120,128]{1,0:T(8,128)S(1)}, f32[5120,128]{1,0:T(8,128)S(1)}) custom-call(f32[5,1024,128]{2,1,0:T(8,128)S(1)} %get-tuple-element.50.lift, f32[5,5,8,128]{3,2,1,0:T(8,128)S(1)} %copy-done.4, f32[61440,128]{1,0:T(8,128)} %get-tuple-element.51.a_far), custom_call_target="tpu_custom_call" | custom-call | bytes 17500000 | tf_op jit(solution)/shard_map/respond/pallas_call | solution.py:744
  67.3 0.0 collective-permute-done.4.rest_1_
  67.3 0.9 %collective-permute-done.5.rest_2_ = f32[8,128]{1,0:T(8,128)S(1)} collective-permute-done((f32[8,128]{1,0:T(8,128)S(1)}, f32[8,128]{1,0:T(8,128)S(1)}, u32[]{:S(2)}, u32[]{:S(2)}) %collective-permute-start.5) | collective-permute-done | bytes 4128 | tf_op jit(solution)/shard_map/ppermute | solution.py:740
  68.3 0.0 collective-permute-done.2.first
  68.3 0.0 collective-permute-done.3.second
  68.3 2.0 %adjoint_local.1 = (f32[5120,128]{1,0:T(8,128)S(1)}, f32[120,128]{1,0:T(8,128)S(1)}) custom-call(f32[5120,128]{1,0:T(8,128)S(1)} %get-tuple-element.52.spread, bf16[1168,128]{1,0:T(8,128)(2,1)S(1)} %collective-permute-done.2.first, bf16[1168,128]{1,0:T(8,128)(2,1)S(1)} %collective-permute-done.3.second, f32[5120,128]{1,0:T(8,128)S(1)} %get-tuple-element.55.a_t, ...), custom_call_target="tpu_custom_call" | custom-call | bytes 10500000 | tf_op jit(solution)/shard_map/adjoint_local/pallas_call | solution.py:754
  70.3 10.4 %all-gather.1 = f32[960,128]{1,0:T(8,128)S(1)} all-gather(f32[120,128]{1,0:T(8,128)S(1)} %get-tuple-element.60), channel_id=3, replica_groups=mesh['lon'=8,'lat'=4] {'lon'}, dimensions={0}, use_global_device_ids=true | all-gather | bytes 552960 | tf_op jit(solution)/shard_map/all_gather | solution.py:764
  80.7 3.2 %gradient.1 = (f32[4384,128]{1,0:T(8,128)}, f32[32,128]{1,0:T(8,128)}) custom-call(f32[8,4,40,128]{3,2,1,0:T(8,128)S(1)} %bitcast.18, f32[8,120,128]{2,1,0:T(8,128)S(1)} %bitcast.22, f32[5120,128]{1,0:T(8,128)S(1)} %get-tuple-element.61.u_t, f32[5120,128]{1,0:T(8,128)S(1)} %get-tuple-element.62.gq_t, f32[5120,128]{1,0:T(8,128)S(1)} %get-tuple-element.63.gp_t, ...), custom_call_target="tpu_custom_call" | custom-call | bytes 10500000 | tf_op jit(solution)/shard_map/gradient/pallas_call | solution.py:765
  (14 shorter events, 0.0 us)
Async XLA Ops:
  0.6 10.6 %copy-start = (f32[4,137,8,128]{3,2,1,0:T(8,128)S(1)}, f32[4,137,8,128]{3,2,1,0:T(8,128)}, u32[]{:S(2)}) copy-start(f32[4,137,8,128]{3,2,1,0:T(8,128)} %param.11) | copy-start | bytes 6733828
  3.8 37.5 %all-to-all-start = ((bf16[32,144,128]{2,1,0:T(8,128)(2,1)}), bf16[32,144,128]{2,1,0:T(8,128)(2,1)}, u32[]{:S(2)}, u32[]{:S(2)}) async-start(bf16[32,144,128]{2,1,0:T(8,128)(2,1)} %pack.1), calls=%async_computation | async-start | bytes 2359296 | tf_op jit(solution)/shard_map/all_to_all | solution.py:610
  11.2 1.6 %copy-start.1 = (f32[4,137,8,128]{3,2,1,0:T(8,128)S(1)}, f32[4,137,8,128]{3,2,1,0:T(8,128)}, u32[]{:S(2)}) copy-start(f32[4,137,8,128]{3,2,1,0:T(8,128)} %param.12) | copy-start | bytes 6733828
  29.8 6.9 %copy-start.2 = (f32[4,137,137]{2,0,1:T(4,128)S(1)}, f32[4,137,137]{2,0,1:T(4,128)}, u32[]{:S(2)}) copy-start(f32[4,137,137]{2,0,1:T(4,128)} %param.14) | copy-start | bytes 900916
  29.8 6.9 %copy-start.5 = (f32[4,5,8]{2,0,1:T(4,128)S(1)}, f32[4,5,8]{2,0,1:T(4,128)}, u32[]{:S(2)}) copy-start(f32[4,5,8]{2,0,1:T(4,128)} %param.13) | copy-start | bytes 1924
  31.8 12.8 %collective-permute-start = (bf16[1152,128]{1,0:T(8,128)(2,1)}, bf16[1152,128]{1,0:T(8,128)(2,1)}, u32[]{:S(2)}, u32[]{:S(2)}) collective-permute-start(bf16[1152,128]{1,0:T(8,128)(2,1)} %get-tuple-element.45), channel_id=1, source_target_pairs={{0,1},{1,0},{2,3},{3,2},{4,5},{5,4},{6,7},{7,6},{8,9},{9,8},{10,11... | collective-permute-start | bytes 884744 | tf_op jit(solution)/shard_map/ppermute | solution.py:662
  35.3 9.3 %collective-permute-start.1 = (bf16[1152,128]{1,0:T(8,128)(2,1)}, bf16[1152,128]{1,0:T(8,128)(2,1)}, u32[]{:S(2)}, u32[]{:S(2)}) collective-permute-start(bf16[1152,128]{1,0:T(8,128)(2,1)} %get-tuple-element.46), channel_id=1, source_target_pairs={{1,2},{2,1},{5,6},{6,5},{9,10},{10,9},{13,14},{14,13},{17,18},{18,... | collective-permute-start | bytes 884744 | tf_op jit(solution)/shard_map/ppermute | solution.py:663
  40.6 0.7 copy-start.3
  41.2 3.3 %copy-start.6 = (s32[1,32,128]{2,1,0:T(8,128)S(1)}, s32[1,32,128]{2,1,0:T(8,128)}, u32[]{:S(2)}) copy-start(s32[1,32,128]{2,1,0:T(8,128)} %param.15) | copy-start | bytes 49156
  41.2 3.3 %copy-start.7 = (s32[1,32]{1,0:T(1,128)S(1)}, s32[1,32]{1,0:T(1,128)}, u32[]{:S(2)}) copy-start(s32[1,32]{1,0:T(1,128)} %param.16) | copy-start | bytes 388
  41.2 3.4 %copy-start.8 = (s32[1,32]{1,0:T(1,128)S(1)}, s32[1,32]{1,0:T(1,128)}, u32[]{:S(2)}) copy-start(s32[1,32]{1,0:T(1,128)} %param.18) | copy-start | bytes 388
  41.3 3.4 %copy-start.9 = (s32[1,32]{1,0:T(1,128)S(1)}, s32[1,32]{1,0:T(1,128)}, u32[]{:S(2)}) copy-start(s32[1,32]{1,0:T(1,128)} %param.17) | copy-start | bytes 388
  43.2 20.2 %copy-start.4 = (f32[5,5,8,128]{3,2,1,0:T(8,128)S(1)}, f32[5,5,8,128]{3,2,1,0:T(8,128)}, u32[]{:S(2)}) copy-start(f32[5,5,8,128]{3,2,1,0:T(8,128)} %copy-done.3) | copy-start | bytes 307204
  55.1 13.1 %collective-permute-start.2 = (bf16[1168,128]{1,0:T(8,128)(2,1)S(1)}, bf16[1168,128]{1,0:T(8,128)(2,1)S(1)}, u32[]{:S(2)}, u32[]{:S(2)}) collective-permute-start(bf16[1168,128]{1,0:T(8,128)(2,1)S(1)} %get-tuple-element.53), channel_id=1, source_target_pairs={{0,1},{1,0},{2,3},{3,2},{4,5},{5,4},{6,7},{7,6},{8,9},{9,8},{10,11... | collective-permute-start | bytes 897032 | tf_op jit(solution)/shard_map/ppermute | solution.py:741
  57.0 11.3 %collective-permute-start.3 = (bf16[1168,128]{1,0:T(8,128)(2,1)S(1)}, bf16[1168,128]{1,0:T(8,128)(2,1)S(1)}, u32[]{:S(2)}, u32[]{:S(2)}) collective-permute-start(bf16[1168,128]{1,0:T(8,128)(2,1)S(1)} %get-tuple-element.54), channel_id=1, source_target_pairs={{1,2},{2,1},{5,6},{6,5},{9,10},{10,9},{13,14},{14,13},{17,18},{18,... | collective-permute-start | bytes 897032 | tf_op jit(solution)/shard_map/ppermute | solution.py:742
  57.8 9.5 %collective-permute-start.4 = (f32[8,128]{1,0:T(8,128)S(1)}, f32[8,128]{1,0:T(8,128)S(1)}, u32[]{:S(2)}, u32[]{:S(2)}) collective-permute-start(f32[8,128]{1,0:T(8,128)S(1)} %get-tuple-element.58), channel_id=1, source_target_pairs={{0,3},{3,0},{4,7},{7,4},{8,11},{11,8},{12,15},{15,12},{16,19},{19,... | collective-permute-start | bytes 12296 | tf_op jit(solution)/shard_map/ppermute | solution.py:737
  63.3 5.0 %collective-permute-start.5 = (f32[8,128]{1,0:T(8,128)S(1)}, f32[8,128]{1,0:T(8,128)S(1)}, u32[]{:S(2)}, u32[]{:S(2)}) collective-permute-start(f32[8,128]{1,0:T(8,128)S(1)} %get-tuple-element.59), channel_id=1, source_target_pairs={{0,2},{1,3},{2,0},{3,1},{4,6},{5,7},{6,4},{7,5},{8,10},{9,11},{10,... | collective-permute-start | bytes 12296 | tf_op jit(solution)/shard_map/ppermute | solution.py:740

commit v4 on v3

--- a/solution.py
+++ b/solution.py
@@ -14,7 +14,7 @@
 ROOM = 12
 FAR = 24
 CELLS = 256
-GROUP = 4
+GROUP = 6
 BF = jnp.bfloat16
 F32 = jnp.float32
 NT = (((1,), (1,)), ((), ()))
@@ -72,6 +72,36 @@
     return east_in, west_in
 
 
+def pile_kernel(*refs):
+    for n, ref in enumerate(refs[:-1]):
+        refs[-1][n] = ref[...]
+
+
+def gather_sectors(x):
+    count = lax.axis_size("lon")
+
+    def swap(y, mask):
+        return lax.ppermute(y, "lon", [(i, i ^ mask) for i in range(count)])
+
+    pieces = [x] + [swap(x, mask) for mask in range(2, count, 2)]
+    near = pl.pallas_call(
+        pile_kernel,
+        out_shape=sds((len(pieces), *x.shape)),
+        in_specs=[VMEM] * len(pieces),
+        out_specs=VMEM,
+        compiler_params=params(8),
+        cost_estimate=cost(1),
+        name="pile",
+    )(*pieces)
+    return near, swap(near, 1)
+
+
+def sector_rows(pair, sector, me, rows):
+    near, far = pair
+    apart = jnp.bitwise_xor(sector, me)
+    return jnp.where(apart % 2 == 0, near[apart // 2, rows], far[apart // 2, rows])
+
+
 def fetch(pairs, arrived):
     copies = [pltpu.make_async_copy(a, b, arrived.at[n]) for n, (a, b) in enumerate(pairs)]
     for copy in copies:
@@ -196,10 +226,8 @@
         return w0, w1, s
 
     w0, w1, _ = lax.fori_loop(0, LANES, west, (zero, zero, one), unroll=4)
-    ends[0] = p
-    ends[1] = e
-    ends[2] = w0
-    ends[3] = w1
+    for n, end in enumerate((p, e, w0, w1)):
+        ends[pl.ds(n * per, per), :] = end
     for copy in leaving:
         copy.wait()
 
@@ -221,10 +249,14 @@
     return first, pltpu.roll(first, LANES - LANES // fields // 2, 1)
 
 
-def edges_kernel(fields, rows, count, gathered, w0_t, w1_t, s_t, first, second, entering, sides):
+def edges_kernel(fields, rows, count, near, far, w0_t, w1_t, s_t, first, second, entering, sides):
     per = (fields + 1) * rows
-    part = [[gathered[s, q] for s in range(count)] for q in range(4)]
-    east_in, west_in = solve_sectors(lax.axis_index("lon"), part[0], part[1], part[3], part[2])
+    me = lax.axis_index("lon")
+    part = [
+        [sector_rows((near, far), s, me, pl.ds(q * per, per)) for s in range(count)]
+        for q in range(4)
+    ]
+    east_in, west_in = solve_sectors(me, part[0], part[1], part[3], part[2])
     entering[0] = east_in
     entering[1] = west_in
     odd = lax.axis_index("lat") % 2
@@ -535,7 +567,7 @@
 
 
 def gradient_kernel(
-    fields, levels, rows, count, bands, before, gathered, u_t, gq_t, gp_t, control,
+    fields, levels, rows, count, bands, near, far, near_back, far_back, u_t, gq_t, gp_t, control,
     gradient, residual, full, extra, held, arrived,
 ):
     per = (fields + 1) * rows
@@ -543,15 +575,17 @@
     me = lax.axis_index("lon")
     east_in, west_in = solve_sectors(
         me,
-        [before[s, 0] for s in range(count)],
-        [gathered[s, :per] for s in range(count)],
-        [before[s, 3] for s in range(count)],
-        [gathered[s, per : 2 * per] for s in range(count)],
+        [sector_rows((near, far), s, me, pl.ds(0, per)) for s in range(count)],
+        [sector_rows((near_back, far_back), s, me, pl.ds(0, per)) for s in range(count)],
+        [sector_rows((near, far), s, me, pl.ds(3 * per, per)) for s in range(count)],
+        [sector_rows((near_back, far_back), s, me, pl.ds(per, per)) for s in range(count)],
     )
     for source in range(bands):
         route = route_of(lax.axis_index("lat") - source, bands)
         for s in range(count):
-            line = gathered[s, pl.ds(2 * per + route * count + me, 1), :]
+            line = sector_rows(
+                (near_back, far_back), s, me, pl.ds(2 * per + route * count + me, 1)
+            )
             residual[pl.ds(s * bands + source, 1), :] = line
 
     def one(i, _):
@@ -627,7 +661,7 @@
     tiles = pltpu.VMEM((lines, LANES), F32)
     a_far, w0_t, w1_t, s_t, ends = pl.pallas_call(
         functools.partial(filter_kernel, *sizes),
-        out_shape=[sds((ROOM * lines, LANES))] + [line] * 3 + [sds((4, per, LANES))],
+        out_shape=[sds((ROOM * lines, LANES))] + [line] * 3 + [sds((4 * per, LANES))],
         in_specs=[HBM] * 2,
         out_specs=[HBM] + [VMEM] * 4,
         scratch_shapes=[pltpu.VMEM(flat_control.shape, F32)] * 2
@@ -641,20 +675,20 @@
         cost_estimate=cost(6),
         name="filter_local",
     )(flat_control, flat_smoothing)
-    gathered = lax.all_gather(ends, "lon")
+    near, far = gather_sectors(ends)
 
     halo_rows = (fields * HALO + 1) * LANES
     halo_shape = sds((halo_rows, LANES), BF)
     first, second, entering = pl.pallas_call(
         functools.partial(edges_kernel, fields, rows, count),
         out_shape=[halo_shape, halo_shape, sds((2, per, LANES))],
-        in_specs=[VMEM] * 4,
+        in_specs=[VMEM] * 5,
         out_specs=[VMEM] * 3,
         scratch_shapes=[pltpu.VMEM((2, *halo_shape.shape), BF)],
         compiler_params=params(16),
         cost_estimate=cost(1),
         name="edges",
-    )(gathered, w0_t, w1_t, s_t)
+    )(near, far, w0_t, w1_t, s_t)
 
     bands = lax.axis_size("lat")
     even = [p for i in range(0, bands - 1, 2) for p in ((i, i + 1), (i + 1, i))]
@@ -761,11 +795,11 @@
         cost_estimate=cost(3),
         name="adjoint_local",
     )(spread, first, second, a_again, g_t, *arrived)
-    gathered_back = lax.all_gather(ends, "lon")
+    near_back, far_back = gather_sectors(ends)
     gradient, returned = pl.pallas_call(
         functools.partial(gradient_kernel, *sizes, count, bands),
         out_shape=[sds(flat_control.shape), sds((total, slots))],
-        in_specs=[VMEM] * 6,
+        in_specs=[VMEM] * 8,
         out_specs=[HBM, VMEM],
         scratch_shapes=[
             tiles,
@@ -776,7 +810,7 @@
         compiler_params=params(20),
         cost_estimate=cost(3),
         name="gradient",
-    )(gathered, gathered_back, u_t, gq_t, gp_t, flat_control)
+    )(near, far, near_back, far_back, u_t, gq_t, gp_t, flat_control)
     return gradient.reshape(control.shape), returned[None]
 
 

time: 84 us -> 83.1 us (0.989)
  blocking collectives: 22.1 us -> 0 us
  waiting for transfers between devices: 2.36 us -> 17.1 us
  starting transfers between devices: 20.5 us -> 26.7 us
    all_gather x2 -> x0, blocking collectives: 22.1 us -> none  [the longest x1 11.7 us: local(): gathered = lax.all_gather(ends, 'lon')]
    ppermute x0 -> x8, waiting for transfers between devices: none -> 14.4 us  [swap(): return lax.ppermute(y, 'lon', [(i, i ^ mask) for i in range(count)])]
    ppermute x0 -> x8, starting transfers between devices: none -> 7.25 us  [swap(): return lax.ppermute(y, 'lon', [(i, i ^ mask) for i in range(count)])]
    unnamed x20 -> x26, local copies, waits for them, and re-layouts: 2.31 us -> 2.72 us
  transfers between devices with their start and end apart: 7 -> 15, of which waited for: 2 -> 11; matrix products, arithmetic and copies ran while one was open for 0% -> 0% of each run, Pallas kernels for 20% -> 21%
where the time goes in v4:
time: 83.1 us; the launch traced here: 82.8 us
  Pallas kernels  35.3 us (42%)
  starting transfers between devices  26.7 us (32%)
  waiting for transfers between devices  17.1 us (21%)
  local copies, waits for them, and re-layouts  2.72 us (3%)
  between operations  1 us (1%)
    ppermute x8, waiting for transfers between devices, swap(): return lax.ppermute(y, 'lon', [(i, i ^ mask) for i in range(count)])  14.4 us
    pallas_call x1, Pallas kernels, local(): pl.pallas_call(functools.partial(observe_kernel, *sizes, bands), out_shap...  9.97 us
    all_to_all x1, starting transfers between devices, local(): lax.all_to_all(sent, both, split_axis=0, concat_axis=0, tiled=True)  7.3 us
    ppermute x8, starting transfers between devices, swap(): return lax.ppermute(y, 'lon', [(i, i ^ mask) for i in range(count)])  7.25 us
    pallas_call x1, Pallas kernels, local(): pl.pallas_call(functools.partial(filter_kernel, *sizes), out_shape=[sds((...  5.23 us
    ppermute x1, starting transfers between devices, local(): arrived = [residuals[0], lax.ppermute(residuals[1], 'lat', swap)]  5.09 us
    ppermute x2, starting transfers between devices, local(): first = lax.ppermute(first, 'lat', even)  4.8 us
    pallas_call x1, Pallas kernels, local(): pl.pallas_call(functools.partial(respond_kernel, fields, rows), out_shape...  3.9 us
  transfers between devices with their start and end apart: 15, of which 11 were waited for; matrix products, arithmetic and copies ran while one was open for 0% of the time, Pallas kernels for 21%

profile of v4, /device:TPU:0, one launch (start us, length us, event | category | flops | bytes accessed | tf_op | source)
XLA Modules:
  0.0 82.8 jit_solution(10767702931632015619)
XLA Ops:
  0.6 3.1 %pack.1 = bf16[32,144,128]{2,1,0:T(8,128)(2,1)} custom-call(bf16[137,32,128]{2,1,0:T(8,128)(2,1)} %bitcast.24, bf16[32,128]{1,0:T(8,128)(2,1)} %bitcast.25, bf16[32,128]{1,0:T(8,128)(2,1)} %bitcast.26), custom_call_target="tpu_custom_call" | custom-call | bytes 10500000 | tf_op jit(solution)/shard_map/pack/pallas_call | solution.py:627
  3.8 7.3 %all-to-all-start = ((bf16[32,144,128]{2,1,0:T(8,128)(2,1)}), bf16[32,144,128]{2,1,0:T(8,128)(2,1)S(1)}, u32[]{:S(2)}, u32[]{:S(2)}) async-start(bf16[32,144,128]{2,1,0:T(8,128)(2,1)} %pack.1), calls=%async_computation | async-start | bytes 2359296 | tf_op jit(solution)/shard_map/all_to_all | solution.py:644
  11.1 1.6 %copy-done.3 = f32[4,137,8,128]{3,2,1,0:T(8,128)S(1)} copy-done((f32[4,137,8,128]{3,2,1,0:T(8,128)S(1)}, f32[4,137,8,128]{3,2,1,0:T(8,128)}, u32[]{:S(2)}) %copy-start.3) | copy-done | bytes 2244632
  12.7 5.2 %filter_local.1 = (f32[61440,128]{1,0:T(8,128)}, f32[5120,128]{1,0:T(8,128)S(1)}, f32[5120,128]{1,0:T(8,128)S(1)}, f32[5120,128]{1,0:T(8,128)S(1)}, f32[160,128]{1,0:T(8,128)S(1)}) custom-call(f32[4384,128]{1,0:T(8,128)S(1)} %bitcast.13, f32[4384,128]{1,0:T(8,128)S(1)} %bitcast.15), custom_call_target="tpu_custom_call" | custom-call | bytes 21000000 | tf_op jit(solution)/shard_map/filter_local/pallas_call | solution.py:662
  18.0 1.8 %collective-permute-start = (f32[160,128]{1,0:T(8,128)S(1)}, f32[160,128]{1,0:T(8,128)S(1)}, u32[]{:S(2)}, u32[]{:S(2)}) collective-permute-start(f32[160,128]{1,0:T(8,128)S(1)} %get-tuple-element.34.refs_0_), channel_id=1, source_target_pairs={{0,8},{4,12},{8,0},{12,4},{16,24},{20,28},{24,16},{28,20},{1,9},{5... | collective-permute-start | bytes 245768 | tf_op jit(solution)/shard_map/ppermute | solution.py:84
  19.8 1.5 %collective-permute-start.1 = (f32[160,128]{1,0:T(8,128)S(1)}, f32[160,128]{1,0:T(8,128)S(1)}, u32[]{:S(2)}, u32[]{:S(2)}) collective-permute-start(f32[160,128]{1,0:T(8,128)S(1)} %get-tuple-element.34.refs_0_), channel_id=1, source_target_pairs={{0,16},{4,20},{8,24},{12,28},{16,0},{20,4},{24,8},{28,12},{1,17},{... | collective-permute-start | bytes 245768 | tf_op jit(solution)/shard_map/ppermute | solution.py:84
  21.5 3.1 %collective-permute-done.refs_1_ = f32[160,128]{1,0:T(8,128)S(1)} collective-permute-done((f32[160,128]{1,0:T(8,128)S(1)}, f32[160,128]{1,0:T(8,128)S(1)}, u32[]{:S(2)}, u32[]{:S(2)}) %collective-permute-start) | collective-permute-done | bytes 81952 | tf_op jit(solution)/shard_map/ppermute | solution.py:84
  24.7 1.2 %collective-permute-done.1.refs_2_ = f32[160,128]{1,0:T(8,128)S(1)} collective-permute-done((f32[160,128]{1,0:T(8,128)S(1)}, f32[160,128]{1,0:T(8,128)S(1)}, u32[]{:S(2)}, u32[]{:S(2)}) %collective-permute-start.1) | collective-permute-done | bytes 81952 | tf_op jit(solution)/shard_map/ppermute | solution.py:84
  25.8 2.3 %collective-permute-done.2.refs_3_ = f32[160,128]{1,0:T(8,128)S(1)} collective-permute-done((f32[160,128]{1,0:T(8,128)S(1)}, f32[160,128]{1,0:T(8,128)S(1)}, u32[]{:S(2)}, u32[]{:S(2)}) %collective-permute-start.2) | collective-permute-done | bytes 81952 | tf_op jit(solution)/shard_map/ppermute | solution.py:84
  28.2 1.6 %collective-permute-done.3.far = f32[4,160,128]{2,1,0:T(8,128)S(1)} collective-permute-done((f32[4,160,128]{2,1,0:T(8,128)S(1)}, f32[4,160,128]{2,1,0:T(8,128)S(1)}, u32[]{:S(2)}, u32[]{:S(2)}) %collective-permute-start.3) | collective-permute-done | bytes 327712 | tf_op jit(solution)/shard_map/ppermute | solution.py:84
  29.8 2.2 %edges.1 = (bf16[1152,128]{1,0:T(8,128)(2,1)}, bf16[1152,128]{1,0:T(8,128)(2,1)}, f32[2,40,128]{2,1,0:T(8,128)S(1)}) custom-call(f32[4,160,128]{2,1,0:T(8,128)S(1)} %pile.2.near, f32[4,160,128]{2,1,0:T(8,128)S(1)} %collective-permute-done.3.far, f32[5120,128]{1,0:T(8,128)S(1)} %get-tuple-element.35.w0_t, f32[5120,128]{1,0:T(8,128)S(1)} %get-tuple-element.36.w1_t, ...), custom_call_target="tpu_custom_call" | custom-call | bytes 3500000 | tf_op jit(solution)/shard_map/edges/pallas_call | solution.py:682
  32.0 1.4 %collective-permute-start.4 = (bf16[1152,128]{1,0:T(8,128)(2,1)}, bf16[1152,128]{1,0:T(8,128)(2,1)}, u32[]{:S(2)}, u32[]{:S(2)}) collective-permute-start(bf16[1152,128]{1,0:T(8,128)(2,1)} %get-tuple-element.45), channel_id=1, source_target_pairs={{0,1},{1,0},{2,3},{3,2},{4,5},{5,4},{6,7},{7,6},{8,9},{9,8},{10,11... | collective-permute-start | bytes 884744 | tf_op jit(solution)/shard_map/ppermute | solution.py:696
  33.4 1.4 %collective-permute-start.5 = (bf16[1152,128]{1,0:T(8,128)(2,1)}, bf16[1152,128]{1,0:T(8,128)(2,1)}, u32[]{:S(2)}, u32[]{:S(2)}) collective-permute-start(bf16[1152,128]{1,0:T(8,128)(2,1)} %get-tuple-element.46), channel_id=1, source_target_pairs={{1,2},{2,1},{5,6},{6,5},{9,10},{10,9},{13,14},{14,13},{17,18},{18,... | collective-permute-start | bytes 884744 | tf_op jit(solution)/shard_map/ppermute | solution.py:697
  34.8 0.5 prepare.1
  35.3 3.5 %interior.1 = (bf16[96,288,256]{2,1,0:T(8,128)(2,1)}, f32[120,4,128,128]{3,2,1,0:T(8,128)}) custom-call(f32[2,40,128]{2,1,0:T(8,128)S(1)} %get-tuple-element.38.entering, f32[5120,128]{1,0:T(8,128)S(1)} %get-tuple-element.35.w0_t, f32[5120,128]{1,0:T(8,128)S(1)} %get-tuple-element.36.w1_t, f32[5120,128]{1,0:T(8,128)S(1)} %get-tuple-element.37.s_t, ...), custom_call_target="tpu_custom_call" | custom-call | bytes 10500000 | tf_op jit(solution)/shard_map/interior/pallas_call | solution.py:702
  38.9 1.1 %copy-done.5 = f32[4,137,137]{2,0,1:T(4,128)S(1)} copy-done((f32[4,137,137]{2,0,1:T(4,128)S(1)}, f32[4,137,137]{2,0,1:T(4,128)}, u32[]{:S(2)}) %copy-start.5) | copy-done | bytes 300328
  39.9 1.8 %stage.1 = (bf16[4,288,256]{2,1,0:T(8,128)(2,1)S(1)}, f32[5,4,128,128]{3,2,1,0:T(8,128)S(1)}, bf16[32,144,128]{2,1,0:T(8,128)(2,1)S(1)}, bf16[4,144,512]{2,1,0:T(8,128)(2,1)S(1)}, f32[5,5,8,128]{3,2,1,0:T(8,128)S(1)}) custom-call(bf16[96,288,256]{2,1,0:T(8,128)(2,1)} %get-tuple-element.41.inner_far, f32[120,4,128,128]{3,2,1,0:T(8,128)} %get-tuple-element.42.partial_far, ...), custom_call_target="tpu_custom_call" | custom-call | bytes 10500000 | tf_op jit(solution)/shard_map/stage/pallas_call | solution.py:727
  41.8 2.0 %collective-permute-done.4.first_far = bf16[1152,128]{1,0:T(8,128)(2,1)} collective-permute-done((bf16[1152,128]{1,0:T(8,128)(2,1)}, bf16[1152,128]{1,0:T(8,128)(2,1)}, u32[]{:S(2)}, u32[]{:S(2)}) %collective-permute-start.4) | collective-permute-done | bytes 294944 | tf_op jit(solution)/shard_map/ppermute | solution.py:696
  43.8 10.0 %observe.1 = (f32[5,1024,128]{2,1,0:T(8,128)S(1)}, bf16[1168,128]{1,0:T(8,128)(2,1)S(1)}, bf16[1168,128]{1,0:T(8,128)(2,1)S(1)}, f32[8,128]{1,0:T(8,128)S(1)}, f...) custom-call(s32[32]{0:T(128)S(1)} %bitcast.21, s32[32]{0:T(128)S(1)} %bitcast.22, s32[32]{0:T(128)S(1)} %bitcast.23, ...), custom_call_target="tpu_custom_call" | custom-call | bytes 49000000 | tf_op jit(solution)/shard_map/observe/pallas_call | solution.py:743
  53.8 3.4 %collective-permute-start.6 = (bf16[1168,128]{1,0:T(8,128)(2,1)S(1)}, bf16[1168,128]{1,0:T(8,128)(2,1)S(1)}, u32[]{:S(2)}, u32[]{:S(2)}) collective-permute-start(bf16[1168,128]{1,0:T(8,128)(2,1)S(1)} %get-tuple-element.53), channel_id=1, source_target_pairs={{0,1},{1,0},{2,3},{3,2},{4,5},{5,4},{6,7},{7,6},{8,9},{9,8},{10,11... | collective-permute-start | bytes 897032 | tf_op jit(solution)/shard_map/ppermute | solution.py:775
  57.2 0.8 %collective-permute-start.7 = (bf16[1168,128]{1,0:T(8,128)(2,1)S(1)}, bf16[1168,128]{1,0:T(8,128)(2,1)S(1)}, u32[]{:S(2)}, u32[]{:S(2)}) collective-permute-start(bf16[1168,128]{1,0:T(8,128)(2,1)S(1)} %get-tuple-element.54), channel_id=1, source_target_pairs={{1,2},{2,1},{5,6},{6,5},{9,10},{10,9},{13,14},{14,13},{17,18},{18,... | collective-permute-start | bytes 897032 | tf_op jit(solution)/shard_map/ppermute | solution.py:776
  58.1 5.1 %collective-permute-start.8 = (f32[8,128]{1,0:T(8,128)S(1)}, f32[8,128]{1,0:T(8,128)S(1)}, u32[]{:S(2)}, u32[]{:S(2)}) collective-permute-start(f32[8,128]{1,0:T(8,128)S(1)} %get-tuple-element.58), channel_id=1, source_target_pairs={{0,3},{3,0},{4,7},{7,4},{8,11},{11,8},{12,15},{15,12},{16,19},{19,... | collective-permute-start | bytes 12296 | tf_op jit(solution)/shard_map/ppermute | solution.py:771
  63.2 3.9 %respond.1 = (f32[5120,128]{1,0:T(8,128)S(1)}, f32[5120,128]{1,0:T(8,128)S(1)}, f32[5120,128]{1,0:T(8,128)S(1)}, f32[5120,128]{1,0:T(8,128)S(1)}, f32[5120,128]{1,0:T(8,128)S(1)}) custom-call(f32[5,1024,128]{2,1,0:T(8,128)S(1)} %get-tuple-element.50.lift, f32[5,5,8,128]{3,2,1,0:T(8,128)S(1)} %get-tuple-element.39.taps, f32[61440,128]{1,0:T(8,128)} %get-tuple-element.51.a_far), custom_call_target="tpu_custom_call" | custom-call | bytes 17500000 | tf_op jit(solution)/shard_map/respond/pallas_call | solution.py:778
  67.1 0.6 collective-permute-done.9.rest_2_
  67.7 2.0 %adjoint_local.1 = (f32[5120,128]{1,0:T(8,128)S(1)}, f32[120,128]{1,0:T(8,128)S(1)}) custom-call(f32[5120,128]{1,0:T(8,128)S(1)} %get-tuple-element.52.spread, bf16[1168,128]{1,0:T(8,128)(2,1)S(1)} %collective-permute-done.6.first, bf16[1168,128]{1,0:T(8,128)(2,1)S(1)} %collective-permute-done.7.second, f32[5120,128]{1,0:T(8,128)S(1)} %get-tuple-element.55.a_t, ...), custom_call_target="tpu_custom_call" | custom-call | bytes 10500000 | tf_op jit(solution)/shard_map/adjoint_local/pallas_call | solution.py:788
  69.7 1.4 %collective-permute-start.10 = (f32[120,128]{1,0:T(8,128)S(1)}, f32[120,128]{1,0:T(8,128)S(1)}, u32[]{:S(2)}, u32[]{:S(2)}) collective-permute-start(f32[120,128]{1,0:T(8,128)S(1)} %get-tuple-element.60.refs_0_), channel_id=1, source_target_pairs={{0,8},{4,12},{8,0},{12,4},{16,24},{20,28},{24,16},{28,20},{1,9},{5... | collective-permute-start | bytes 184328 | tf_op jit(solution)/shard_map/ppermute | solution.py:84
  71.1 1.7 %collective-permute-start.11 = (f32[120,128]{1,0:T(8,128)S(1)}, f32[120,128]{1,0:T(8,128)S(1)}, u32[]{:S(2)}, u32[]{:S(2)}) collective-permute-start(f32[120,128]{1,0:T(8,128)S(1)} %get-tuple-element.60.refs_0_), channel_id=1, source_target_pairs={{0,16},{4,20},{8,24},{12,28},{16,0},{20,4},{24,8},{28,12},{1,17},{... | collective-permute-start | bytes 184328 | tf_op jit(solution)/shard_map/ppermute | solution.py:84
  73.3 0.7 collective-permute-done.10.refs_1_
  74.0 1.4 %collective-permute-done.11.refs_2_ = f32[120,128]{1,0:T(8,128)S(1)} collective-permute-done((f32[120,128]{1,0:T(8,128)S(1)}, f32[120,128]{1,0:T(8,128)S(1)}, u32[]{:S(2)}, u32[]{:S(2)}) %collective-permute-start.11) | collective-permute-done | bytes 61472 | tf_op jit(solution)/shard_map/ppermute | solution.py:84
  75.4 2.6 %collective-permute-done.12.refs_3_ = f32[120,128]{1,0:T(8,128)S(1)} collective-permute-done((f32[120,128]{1,0:T(8,128)S(1)}, f32[120,128]{1,0:T(8,128)S(1)}, u32[]{:S(2)}, u32[]{:S(2)}) %collective-permute-start.12) | collective-permute-done | bytes 61472 | tf_op jit(solution)/shard_map/ppermute | solution.py:84
  78.0 1.5 %collective-permute-done.13.far_back = f32[4,120,128]{2,1,0:T(8,128)S(1)} collective-permute-done((f32[4,120,128]{2,1,0:T(8,128)S(1)}, f32[4,120,128]{2,1,0:T(8,128)S(1)}, u32[]{:S(2)}, u32[]{:S(2)}) %collective-permute-start.13) | collective-permute-done | bytes 245792 | tf_op jit(solution)/shard_map/ppermute | solution.py:84
  79.5 3.1 %gradient.1 = (f32[4384,128]{1,0:T(8,128)}, f32[32,128]{1,0:T(8,128)}) custom-call(f32[4,160,128]{2,1,0:T(8,128)S(1)} %copy-done.2, f32[4,160,128]{2,1,0:T(8,128)S(1)} %copy-done.7, f32[4,120,128]{2,1,0:T(8,128)S(1)} %pile.3.near_back, f32[4,120,128]{2,1,0:T(8,128)S(1)} %collective-permute-done.13.far_back, f32[5120,128]{1,0:T(8,128)S(1)} %get-tuple-element.61.u_t, ...), custom_call_target="tpu_custom_call" | custom-call | bytes 10500000 | tf_op jit(solution)/shard_map/gradient/pallas_call | solution.py:799
  (36 shorter events, 1.1 us)
Async XLA Ops:
  0.6 10.5 %copy-start = (f32[4,137,8,128]{3,2,1,0:T(8,128)S(1)}, f32[4,137,8,128]{3,2,1,0:T(8,128)}, u32[]{:S(2)}) copy-start(f32[4,137,8,128]{3,2,1,0:T(8,128)} %param.11) | copy-start | bytes 6733828
  3.8 35.1 %all-to-all-start = ((bf16[32,144,128]{2,1,0:T(8,128)(2,1)}), bf16[32,144,128]{2,1,0:T(8,128)(2,1)S(1)}, u32[]{:S(2)}, u32[]{:S(2)}) async-start(bf16[32,144,128]{2,1,0:T(8,128)(2,1)} %pack.1), calls=%async_computation | async-start | bytes 2359296 | tf_op jit(solution)/shard_map/all_to_all | solution.py:644
  11.1 1.6 %copy-start.3 = (f32[4,137,8,128]{3,2,1,0:T(8,128)S(1)}, f32[4,137,8,128]{3,2,1,0:T(8,128)}, u32[]{:S(2)}) copy-start(f32[4,137,8,128]{3,2,1,0:T(8,128)} %param.12) | copy-start | bytes 6733828
  18.0 6.7 %collective-permute-start = (f32[160,128]{1,0:T(8,128)S(1)}, f32[160,128]{1,0:T(8,128)S(1)}, u32[]{:S(2)}, u32[]{:S(2)}) collective-permute-start(f32[160,128]{1,0:T(8,128)S(1)} %get-tuple-element.34.refs_0_), channel_id=1, source_target_pairs={{0,8},{4,12},{8,0},{12,4},{16,24},{20,28},{24,16},{28,20},{1,9},{5... | collective-permute-start | bytes 245768 | tf_op jit(solution)/shard_map/ppermute | solution.py:84
  19.8 6.0 %collective-permute-start.1 = (f32[160,128]{1,0:T(8,128)S(1)}, f32[160,128]{1,0:T(8,128)S(1)}, u32[]{:S(2)}, u32[]{:S(2)}) collective-permute-start(f32[160,128]{1,0:T(8,128)S(1)} %get-tuple-element.34.refs_0_), channel_id=1, source_target_pairs={{0,16},{4,20},{8,24},{12,28},{16,0},{20,4},{24,8},{28,12},{1,17},{... | collective-permute-start | bytes 245768 | tf_op jit(solution)/shard_map/ppermute | solution.py:84
  21.3 6.8 %collective-permute-start.2 = (f32[160,128]{1,0:T(8,128)S(1)}, f32[160,128]{1,0:T(8,128)S(1)}, u32[]{:S(2)}, u32[]{:S(2)}) collective-permute-start(f32[160,128]{1,0:T(8,128)S(1)} %get-tuple-element.34.refs_0_), channel_id=1, source_target_pairs={{0,24},{4,28},{8,16},{12,20},{16,8},{20,12},{24,0},{28,4},{1,25},{... | collective-permute-start | bytes 245768 | tf_op jit(solution)/shard_map/ppermute | solution.py:84
  28.1 3.9 %copy-start.1 = (f32[4,160,128]{2,1,0:T(8,128)}, f32[4,160,128]{2,1,0:T(8,128)S(1)}, u32[]{:S(2)}) copy-start(f32[4,160,128]{2,1,0:T(8,128)S(1)} %pile.2.near) | copy-start | bytes 983044
  28.1 1.7 %collective-permute-start.3 = (f32[4,160,128]{2,1,0:T(8,128)S(1)}, f32[4,160,128]{2,1,0:T(8,128)S(1)}, u32[]{:S(2)}, u32[]{:S(2)}) collective-permute-start(f32[4,160,128]{2,1,0:T(8,128)S(1)} %pile.2.near), channel_id=1, source_target_pairs={{0,4},{4,0},{8,12},{12,8},{16,20},{20,16},{24,28},{28,24},{1,5},{5... | collective-permute-start | bytes 983048 | tf_op jit(solution)/shard_map/ppermute | solution.py:84
  29.8 2.2 %copy-start.6 = (f32[4,160,128]{2,1,0:T(8,128)}, f32[4,160,128]{2,1,0:T(8,128)S(1)}, u32[]{:S(2)}) copy-start(f32[4,160,128]{2,1,0:T(8,128)S(1)} %collective-permute-done.3.far) | copy-start | bytes 983044
  29.8 5.0 %copy-start.4 = (f32[4,137,137]{2,0,1:T(4,128)S(1)}, f32[4,137,137]{2,0,1:T(4,128)}, u32[]{:S(2)}) copy-start(f32[4,137,137]{2,0,1:T(4,128)} %param.14) | copy-start | bytes 900916
  29.8 5.0 %copy-start.8 = (f32[4,5,8]{2,0,1:T(4,128)S(1)}, f32[4,5,8]{2,0,1:T(4,128)}, u32[]{:S(2)}) copy-start(f32[4,5,8]{2,0,1:T(4,128)} %param.13) | copy-start | bytes 1924
  32.0 11.8 %collective-permute-start.4 = (bf16[1152,128]{1,0:T(8,128)(2,1)}, bf16[1152,128]{1,0:T(8,128)(2,1)}, u32[]{:S(2)}, u32[]{:S(2)}) collective-permute-start(bf16[1152,128]{1,0:T(8,128)(2,1)} %get-tuple-element.45), channel_id=1, source_target_pairs={{0,1},{1,0},{2,3},{3,2},{4,5},{5,4},{6,7},{7,6},{8,9},{9,8},{10,11... | collective-permute-start | bytes 884744 | tf_op jit(solution)/shard_map/ppermute | solution.py:696
  33.4 10.4 %collective-permute-start.5 = (bf16[1152,128]{1,0:T(8,128)(2,1)}, bf16[1152,128]{1,0:T(8,128)(2,1)}, u32[]{:S(2)}, u32[]{:S(2)}) collective-permute-start(bf16[1152,128]{1,0:T(8,128)(2,1)} %get-tuple-element.46), channel_id=1, source_target_pairs={{1,2},{2,1},{5,6},{6,5},{9,10},{10,9},{13,14},{14,13},{17,18},{18,... | collective-permute-start | bytes 884744 | tf_op jit(solution)/shard_map/ppermute | solution.py:697
  38.9 1.1 %copy-start.5 = (f32[4,137,137]{2,0,1:T(4,128)S(1)}, f32[4,137,137]{2,0,1:T(4,128)}, u32[]{:S(2)}) copy-start(f32[4,137,137]{2,0,1:T(4,128)} %param.14) | copy-start | bytes 900916
  39.9 3.9 %copy-start.9 = (s32[1,32,128]{2,1,0:T(8,128)S(1)}, s32[1,32,128]{2,1,0:T(8,128)}, u32[]{:S(2)}) copy-start(s32[1,32,128]{2,1,0:T(8,128)} %param.15) | copy-start | bytes 49156
  39.9 3.9 %copy-start.10 = (s32[1,32]{1,0:T(1,128)S(1)}, s32[1,32]{1,0:T(1,128)}, u32[]{:S(2)}) copy-start(s32[1,32]{1,0:T(1,128)} %param.16) | copy-start | bytes 388
  39.9 3.9 %copy-start.11 = (s32[1,32]{1,0:T(1,128)S(1)}, s32[1,32]{1,0:T(1,128)}, u32[]{:S(2)}) copy-start(s32[1,32]{1,0:T(1,128)} %param.18) | copy-start | bytes 388
  39.9 3.9 %copy-start.12 = (s32[1,32]{1,0:T(1,128)S(1)}, s32[1,32]{1,0:T(1,128)}, u32[]{:S(2)}) copy-start(s32[1,32]{1,0:T(1,128)} %param.17) | copy-start | bytes 388
  53.8 13.9 %collective-permute-start.6 = (bf16[1168,128]{1,0:T(8,128)(2,1)S(1)}, bf16[1168,128]{1,0:T(8,128)(2,1)S(1)}, u32[]{:S(2)}, u32[]{:S(2)}) collective-permute-start(bf16[1168,128]{1,0:T(8,128)(2,1)S(1)} %get-tuple-element.53), channel_id=1, source_target_pairs={{0,1},{1,0},{2,3},{3,2},{4,5},{5,4},{6,7},{7,6},{8,9},{9,8},{10,11... | collective-permute-start | bytes 897032 | tf_op jit(solution)/shard_map/ppermute | solution.py:775
  57.2 10.5 %collective-permute-start.7 = (bf16[1168,128]{1,0:T(8,128)(2,1)S(1)}, bf16[1168,128]{1,0:T(8,128)(2,1)S(1)}, u32[]{:S(2)}, u32[]{:S(2)}) collective-permute-start(bf16[1168,128]{1,0:T(8,128)(2,1)S(1)} %get-tuple-element.54), channel_id=1, source_target_pairs={{1,2},{2,1},{5,6},{6,5},{9,10},{10,9},{13,14},{14,13},{17,18},{18,... | collective-permute-start | bytes 897032 | tf_op jit(solution)/shard_map/ppermute | solution.py:776
  58.1 9.1 %collective-permute-start.8 = (f32[8,128]{1,0:T(8,128)S(1)}, f32[8,128]{1,0:T(8,128)S(1)}, u32[]{:S(2)}, u32[]{:S(2)}) collective-permute-start(f32[8,128]{1,0:T(8,128)S(1)} %get-tuple-element.58), channel_id=1, source_target_pairs={{0,3},{3,0},{4,7},{7,4},{8,11},{11,8},{12,15},{15,12},{16,19},{19,... | collective-permute-start | bytes 12296 | tf_op jit(solution)/shard_map/ppermute | solution.py:771
  63.2 4.6 %collective-permute-start.9 = (f32[8,128]{1,0:T(8,128)S(1)}, f32[8,128]{1,0:T(8,128)S(1)}, u32[]{:S(2)}, u32[]{:S(2)}) collective-permute-start(f32[8,128]{1,0:T(8,128)S(1)} %get-tuple-element.59), channel_id=1, source_target_pairs={{0,2},{1,3},{2,0},{3,1},{4,6},{5,7},{6,4},{7,5},{8,10},{9,11},{10,... | collective-permute-start | bytes 12296 | tf_op jit(solution)/shard_map/ppermute | solution.py:774
  67.7 11.8 %copy-start.2 = (f32[4,160,128]{2,1,0:T(8,128)S(1)}, f32[4,160,128]{2,1,0:T(8,128)}, u32[]{:S(2)}) copy-start(f32[4,160,128]{2,1,0:T(8,128)} %copy-done.1) | copy-start | bytes 983044
  67.7 11.8 %copy-start.7 = (f32[4,160,128]{2,1,0:T(8,128)S(1)}, f32[4,160,128]{2,1,0:T(8,128)}, u32[]{:S(2)}) copy-start(f32[4,160,128]{2,1,0:T(8,128)} %copy-done.6) | copy-start | bytes 983044
  69.7 4.3 %collective-permute-start.10 = (f32[120,128]{1,0:T(8,128)S(1)}, f32[120,128]{1,0:T(8,128)S(1)}, u32[]{:S(2)}, u32[]{:S(2)}) collective-permute-start(f32[120,128]{1,0:T(8,128)S(1)} %get-tuple-element.60.refs_0_), channel_id=1, source_target_pairs={{0,8},{4,12},{8,0},{12,4},{16,24},{20,28},{24,16},{28,20},{1,9},{5... | collective-permute-start | bytes 184328 | tf_op jit(solution)/shard_map/ppermute | solution.py:84
  71.1 4.2 %collective-permute-start.11 = (f32[120,128]{1,0:T(8,128)S(1)}, f32[120,128]{1,0:T(8,128)S(1)}, u32[]{:S(2)}, u32[]{:S(2)}) collective-permute-start(f32[120,128]{1,0:T(8,128)S(1)} %get-tuple-element.60.refs_0_), channel_id=1, source_target_pairs={{0,16},{4,20},{8,24},{12,28},{16,0},{20,4},{24,8},{28,12},{1,17},{... | collective-permute-start | bytes 184328 | tf_op jit(solution)/shard_map/ppermute | solution.py:84
  72.8 5.1 %collective-permute-start.12 = (f32[120,128]{1,0:T(8,128)S(1)}, f32[120,128]{1,0:T(8,128)S(1)}, u32[]{:S(2)}, u32[]{:S(2)}) collective-permute-start(f32[120,128]{1,0:T(8,128)S(1)} %get-tuple-element.60.refs_0_), channel_id=1, source_target_pairs={{0,24},{4,28},{8,16},{12,20},{16,8},{20,12},{24,0},{28,4},{1,25},{... | collective-permute-start | bytes 184328 | tf_op jit(solution)/shard_map/ppermute | solution.py:84
  78.0 1.6 %collective-permute-start.13 = (f32[4,120,128]{2,1,0:T(8,128)S(1)}, f32[4,120,128]{2,1,0:T(8,128)S(1)}, u32[]{:S(2)}, u32[]{:S(2)}) collective-permute-start(f32[4,120,128]{2,1,0:T(8,128)S(1)} %pile.3.near_back), channel_id=1, source_target_pairs={{0,4},{4,0},{8,12},{12,8},{16,20},{20,16},{24,28},{28,24},{1,5},{5... | collective-permute-start | bytes 737288 | tf_op jit(solution)/shard_map/ppermute | solution.py:84

commit v5 on v4

--- a/solution.py
+++ b/solution.py
@@ -507,12 +507,6 @@
         gp_t[at, :] = g * s
         return a * t, a * s
 
-    one = jnp.ones((per, LANES), F32)
-    p = one
-    for c, copy in enumerate(copies):
-        copy.wait()
-        p = lax.fori_loop(c * span, (c + 1) * span, east, p, unroll=4)
-    lax.fori_loop(0, LANES, west, (jnp.zeros_like(one), one), unroll=4)
     for b in range(blocks):
         for m in range(rows):
             total = taps[HALO, b, m : m + 1, :] * lift[b, pl.ds(m * LANES, LANES), :]
@@ -521,6 +515,12 @@
                 if t != HALO and 0 <= j < rows:
                     total += taps[t, b, j : j + 1, :] * lift[b, pl.ds(j * LANES, LANES), :]
             spread[pl.ds(b * rows + m, LANES, stride=per), :] = total
+    one = jnp.ones((per, LANES), F32)
+    p = one
+    for c, copy in enumerate(copies):
+        copy.wait()
+        p = lax.fori_loop(c * span, (c + 1) * span, east, p, unroll=4)
+    lax.fori_loop(0, LANES, west, (jnp.zeros_like(one), one), unroll=4)
 
 
 def adjoint_kernel(fields, rows, spread, first, second, a_t, g_t, *rest):

time: 83.1 us -> 83.1 us (level)
  waiting for transfers between devices: 17.1 us -> 18.7 us
  Pallas kernels: 35.3 us -> 34.4 us
    ppermute x1, waiting for transfers between devices: 0.58 us -> 1.9 us  [local(): arrived.append(lax.ppermute(residuals[n], 'lat', ring))]
    pallas_call x1, Pallas kernels: 3.9 us -> 3.01 us  [local(): pl.pallas_call(functools.partial(respond_kernel, fields, rows), out_shape...]
    ppermute x2, starting transfers between devices: 4.8 us -> 3.95 us  [local(): first = lax.ppermute(first, 'lat', even)]
  transfers between devices with their start and end apart: 15 -> 15, of which waited for: 11 -> 12; matrix products, arithmetic and copies ran while one was open for 0% -> 0% of each run, Pallas kernels for 21% -> 20%
where the time goes in v5:
time: 83.1 us; the launch traced here: 82.7 us
  Pallas kernels  34.4 us (41%)
  starting transfers between devices  25.9 us (31%)
  waiting for transfers between devices  18.7 us (23%)
  local copies, waits for them, and re-layouts  2.72 us (3%)
  between operations  0.99 us (1%)
    ppermute x8, waiting for transfers between devices, swap(): return lax.ppermute(y, 'lon', [(i, i ^ mask) for i in range(count)])  14.3 us
    pallas_call x1, Pallas kernels, local(): pl.pallas_call(functools.partial(observe_kernel, *sizes, bands), out_shap...  9.98 us
    all_to_all x1, starting transfers between devices, local(): lax.all_to_all(sent, both, split_axis=0, concat_axis=0, tiled=True)  7.3 us
    ppermute x8, starting transfers between devices, swap(): return lax.ppermute(y, 'lon', [(i, i ^ mask) for i in range(count)])  7.25 us
    pallas_call x1, Pallas kernels, local(): pl.pallas_call(functools.partial(filter_kernel, *sizes), out_shape=[sds((...  5.23 us
    ppermute x1, starting transfers between devices, local(): arrived = [residuals[0], lax.ppermute(residuals[1], 'lat', swap)]  5.08 us
    ppermute x2, starting transfers between devices, local(): first = lax.ppermute(first, 'lat', even)  3.95 us
    pallas_call x1, Pallas kernels, local(): pl.pallas_call(functools.partial(interior_kernel, fields, rows), out_shap...  3.48 us
  transfers between devices with their start and end apart: 15, of which 12 were waited for; matrix products, arithmetic and copies ran while one was open for 0% of the time, Pallas kernels for 20%

profile of v5, /device:TPU:0, one launch (start us, length us, event | category | flops | bytes accessed | tf_op | source)
XLA Modules:
  0.0 82.7 jit_solution(16685615702743415014)
XLA Ops:
  0.6 3.1 %pack.1 = bf16[32,144,128]{2,1,0:T(8,128)(2,1)} custom-call(bf16[137,32,128]{2,1,0:T(8,128)(2,1)} %bitcast.24, bf16[32,128]{1,0:T(8,128)(2,1)} %bitcast.25, bf16[32,128]{1,0:T(8,128)(2,1)} %bitcast.26), custom_call_target="tpu_custom_call" | custom-call | bytes 10500000 | tf_op jit(solution)/shard_map/pack/pallas_call | solution.py:627
  3.8 7.3 %all-to-all-start = ((bf16[32,144,128]{2,1,0:T(8,128)(2,1)}), bf16[32,144,128]{2,1,0:T(8,128)(2,1)S(1)}, u32[]{:S(2)}, u32[]{:S(2)}) async-start(bf16[32,144,128]{2,1,0:T(8,128)(2,1)} %pack.1), calls=%async_computation | async-start | bytes 2359296 | tf_op jit(solution)/shard_map/all_to_all | solution.py:644
  11.1 1.6 %copy-done.3 = f32[4,137,8,128]{3,2,1,0:T(8,128)S(1)} copy-done((f32[4,137,8,128]{3,2,1,0:T(8,128)S(1)}, f32[4,137,8,128]{3,2,1,0:T(8,128)}, u32[]{:S(2)}) %copy-start.3) | copy-done | bytes 2244632
  12.7 5.2 %filter_local.1 = (f32[61440,128]{1,0:T(8,128)}, f32[5120,128]{1,0:T(8,128)S(1)}, f32[5120,128]{1,0:T(8,128)S(1)}, f32[5120,128]{1,0:T(8,128)S(1)}, f32[160,128]{1,0:T(8,128)S(1)}) custom-call(f32[4384,128]{1,0:T(8,128)S(1)} %bitcast.13, f32[4384,128]{1,0:T(8,128)S(1)} %bitcast.15), custom_call_target="tpu_custom_call" | custom-call | bytes 21000000 | tf_op jit(solution)/shard_map/filter_local/pallas_call | solution.py:662
  18.0 1.8 %collective-permute-start = (f32[160,128]{1,0:T(8,128)S(1)}, f32[160,128]{1,0:T(8,128)S(1)}, u32[]{:S(2)}, u32[]{:S(2)}) collective-permute-start(f32[160,128]{1,0:T(8,128)S(1)} %get-tuple-element.34.refs_0_), channel_id=1, source_target_pairs={{0,8},{4,12},{8,0},{12,4},{16,24},{20,28},{24,16},{28,20},{1,9},{5... | collective-permute-start | bytes 245768 | tf_op jit(solution)/shard_map/ppermute | solution.py:84
  19.8 1.5 %collective-permute-start.1 = (f32[160,128]{1,0:T(8,128)S(1)}, f32[160,128]{1,0:T(8,128)S(1)}, u32[]{:S(2)}, u32[]{:S(2)}) collective-permute-start(f32[160,128]{1,0:T(8,128)S(1)} %get-tuple-element.34.refs_0_), channel_id=1, source_target_pairs={{0,16},{4,20},{8,24},{12,28},{16,0},{20,4},{24,8},{28,12},{1,17},{... | collective-permute-start | bytes 245768 | tf_op jit(solution)/shard_map/ppermute | solution.py:84
  21.5 3.1 %collective-permute-done.refs_1_ = f32[160,128]{1,0:T(8,128)S(1)} collective-permute-done((f32[160,128]{1,0:T(8,128)S(1)}, f32[160,128]{1,0:T(8,128)S(1)}, u32[]{:S(2)}, u32[]{:S(2)}) %collective-permute-start) | collective-permute-done | bytes 81952 | tf_op jit(solution)/shard_map/ppermute | solution.py:84
  24.7 1.2 %collective-permute-done.1.refs_2_ = f32[160,128]{1,0:T(8,128)S(1)} collective-permute-done((f32[160,128]{1,0:T(8,128)S(1)}, f32[160,128]{1,0:T(8,128)S(1)}, u32[]{:S(2)}, u32[]{:S(2)}) %collective-permute-start.1) | collective-permute-done | bytes 81952 | tf_op jit(solution)/shard_map/ppermute | solution.py:84
  25.8 2.3 %collective-permute-done.2.refs_3_ = f32[160,128]{1,0:T(8,128)S(1)} collective-permute-done((f32[160,128]{1,0:T(8,128)S(1)}, f32[160,128]{1,0:T(8,128)S(1)}, u32[]{:S(2)}, u32[]{:S(2)}) %collective-permute-start.2) | collective-permute-done | bytes 81952 | tf_op jit(solution)/shard_map/ppermute | solution.py:84
  28.2 1.6 %collective-permute-done.3.far = f32[4,160,128]{2,1,0:T(8,128)S(1)} collective-permute-done((f32[4,160,128]{2,1,0:T(8,128)S(1)}, f32[4,160,128]{2,1,0:T(8,128)S(1)}, u32[]{:S(2)}, u32[]{:S(2)}) %collective-permute-start.3) | collective-permute-done | bytes 327712 | tf_op jit(solution)/shard_map/ppermute | solution.py:84
  29.8 2.2 %edges.1 = (bf16[1152,128]{1,0:T(8,128)(2,1)}, bf16[1152,128]{1,0:T(8,128)(2,1)}, f32[2,40,128]{2,1,0:T(8,128)S(1)}) custom-call(f32[4,160,128]{2,1,0:T(8,128)S(1)} %pile.2.near, f32[4,160,128]{2,1,0:T(8,128)S(1)} %collective-permute-done.3.far, f32[5120,128]{1,0:T(8,128)S(1)} %get-tuple-element.35.w0_t, f32[5120,128]{1,0:T(8,128)S(1)} %get-tuple-element.36.w1_t, ...), custom_call_target="tpu_custom_call" | custom-call | bytes 3500000 | tf_op jit(solution)/shard_map/edges/pallas_call | solution.py:682
  32.0 1.4 %collective-permute-start.4 = (bf16[1152,128]{1,0:T(8,128)(2,1)}, bf16[1152,128]{1,0:T(8,128)(2,1)}, u32[]{:S(2)}, u32[]{:S(2)}) collective-permute-start(bf16[1152,128]{1,0:T(8,128)(2,1)} %get-tuple-element.45), channel_id=1, source_target_pairs={{0,1},{1,0},{2,3},{3,2},{4,5},{5,4},{6,7},{7,6},{8,9},{9,8},{10,11... | collective-permute-start | bytes 884744 | tf_op jit(solution)/shard_map/ppermute | solution.py:696
  33.4 1.4 %collective-permute-start.5 = (bf16[1152,128]{1,0:T(8,128)(2,1)}, bf16[1152,128]{1,0:T(8,128)(2,1)}, u32[]{:S(2)}, u32[]{:S(2)}) collective-permute-start(bf16[1152,128]{1,0:T(8,128)(2,1)} %get-tuple-element.46), channel_id=1, source_target_pairs={{1,2},{2,1},{5,6},{6,5},{9,10},{10,9},{13,14},{14,13},{17,18},{18,... | collective-permute-start | bytes 884744 | tf_op jit(solution)/shard_map/ppermute | solution.py:697
  35.3 3.5 %interior.1 = (bf16[96,288,256]{2,1,0:T(8,128)(2,1)}, f32[120,4,128,128]{3,2,1,0:T(8,128)}) custom-call(f32[2,40,128]{2,1,0:T(8,128)S(1)} %get-tuple-element.38.entering, f32[5120,128]{1,0:T(8,128)S(1)} %get-tuple-element.35.w0_t, f32[5120,128]{1,0:T(8,128)S(1)} %get-tuple-element.36.w1_t, f32[5120,128]{1,0:T(8,128)S(1)} %get-tuple-element.37.s_t, ...), custom_call_target="tpu_custom_call" | custom-call | bytes 10500000 | tf_op jit(solution)/shard_map/interior/pallas_call | solution.py:702
  38.9 1.1 %copy-done.5 = f32[4,137,137]{2,0,1:T(4,128)S(1)} copy-done((f32[4,137,137]{2,0,1:T(4,128)S(1)}, f32[4,137,137]{2,0,1:T(4,128)}, u32[]{:S(2)}) %copy-start.5) | copy-done | bytes 300328
  39.9 1.8 %stage.1 = (bf16[4,288,256]{2,1,0:T(8,128)(2,1)S(1)}, f32[5,4,128,128]{3,2,1,0:T(8,128)S(1)}, bf16[32,144,128]{2,1,0:T(8,128)(2,1)S(1)}, bf16[4,144,512]{2,1,0:T(8,128)(2,1)S(1)}, f32[5,5,8,128]{3,2,1,0:T(8,128)S(1)}) custom-call(bf16[96,288,256]{2,1,0:T(8,128)(2,1)} %get-tuple-element.41.inner_far, f32[120,4,128,128]{3,2,1,0:T(8,128)} %get-tuple-element.42.partial_far, ...), custom_call_target="tpu_custom_call" | custom-call | bytes 10500000 | tf_op jit(solution)/shard_map/stage/pallas_call | solution.py:727
  41.8 2.0 %collective-permute-done.4.first_far = bf16[1152,128]{1,0:T(8,128)(2,1)} collective-permute-done((bf16[1152,128]{1,0:T(8,128)(2,1)}, bf16[1152,128]{1,0:T(8,128)(2,1)}, u32[]{:S(2)}, u32[]{:S(2)}) %collective-permute-start.4) | collective-permute-done | bytes 294944 | tf_op jit(solution)/shard_map/ppermute | solution.py:696
  43.8 10.0 %observe.1 = (f32[5,1024,128]{2,1,0:T(8,128)S(1)}, bf16[1168,128]{1,0:T(8,128)(2,1)S(1)}, bf16[1168,128]{1,0:T(8,128)(2,1)S(1)}, f32[8,128]{1,0:T(8,128)S(1)}, f...) custom-call(s32[32]{0:T(128)S(1)} %bitcast.21, s32[32]{0:T(128)S(1)} %bitcast.22, s32[32]{0:T(128)S(1)} %bitcast.23, ...), custom_call_target="tpu_custom_call" | custom-call | bytes 49000000 | tf_op jit(solution)/shard_map/observe/pallas_call | solution.py:743
  53.8 2.5 %collective-permute-start.6 = (bf16[1168,128]{1,0:T(8,128)(2,1)S(1)}, bf16[1168,128]{1,0:T(8,128)(2,1)S(1)}, u32[]{:S(2)}, u32[]{:S(2)}) collective-permute-start(bf16[1168,128]{1,0:T(8,128)(2,1)S(1)} %get-tuple-element.53), channel_id=1, source_target_pairs={{0,1},{1,0},{2,3},{3,2},{4,5},{5,4},{6,7},{7,6},{8,9},{9,8},{10,11... | collective-permute-start | bytes 897032 | tf_op jit(solution)/shard_map/ppermute | solution.py:775
  56.4 0.8 %collective-permute-start.7 = (bf16[1168,128]{1,0:T(8,128)(2,1)S(1)}, bf16[1168,128]{1,0:T(8,128)(2,1)S(1)}, u32[]{:S(2)}, u32[]{:S(2)}) collective-permute-start(bf16[1168,128]{1,0:T(8,128)(2,1)S(1)} %get-tuple-element.54), channel_id=1, source_target_pairs={{1,2},{2,1},{5,6},{6,5},{9,10},{10,9},{13,14},{14,13},{17,18},{18,... | collective-permute-start | bytes 897032 | tf_op jit(solution)/shard_map/ppermute | solution.py:776
  57.2 5.1 %collective-permute-start.8 = (f32[8,128]{1,0:T(8,128)S(1)}, f32[8,128]{1,0:T(8,128)S(1)}, u32[]{:S(2)}, u32[]{:S(2)}) collective-permute-start(f32[8,128]{1,0:T(8,128)S(1)} %get-tuple-element.58), channel_id=1, source_target_pairs={{0,3},{3,0},{4,7},{7,4},{8,11},{11,8},{12,15},{15,12},{16,19},{19,... | collective-permute-start | bytes 12296 | tf_op jit(solution)/shard_map/ppermute | solution.py:771
  62.4 3.0 %respond.1 = (f32[5120,128]{1,0:T(8,128)S(1)}, f32[5120,128]{1,0:T(8,128)S(1)}, f32[5120,128]{1,0:T(8,128)S(1)}, f32[5120,128]{1,0:T(8,128)S(1)}, f32[5120,128]{1,0:T(8,128)S(1)}) custom-call(f32[5,1024,128]{2,1,0:T(8,128)S(1)} %get-tuple-element.50.lift, f32[5,5,8,128]{3,2,1,0:T(8,128)S(1)} %get-tuple-element.39.taps, f32[61440,128]{1,0:T(8,128)} %get-tuple-element.51.a_far), custom_call_target="tpu_custom_call" | custom-call | bytes 17500000 | tf_op jit(solution)/shard_map/respond/pallas_call | solution.py:778
  65.7 1.9 %collective-permute-done.9.rest_2_ = f32[8,128]{1,0:T(8,128)S(1)} collective-permute-done((f32[8,128]{1,0:T(8,128)S(1)}, f32[8,128]{1,0:T(8,128)S(1)}, u32[]{:S(2)}, u32[]{:S(2)}) %collective-permute-start.9) | collective-permute-done | bytes 4128 | tf_op jit(solution)/shard_map/ppermute | solution.py:774
  67.6 2.0 %adjoint_local.1 = (f32[5120,128]{1,0:T(8,128)S(1)}, f32[120,128]{1,0:T(8,128)S(1)}) custom-call(f32[5120,128]{1,0:T(8,128)S(1)} %get-tuple-element.52.spread, bf16[1168,128]{1,0:T(8,128)(2,1)S(1)} %collective-permute-done.6.first, bf16[1168,128]{1,0:T(8,128)(2,1)S(1)} %collective-permute-done.7.second, f32[5120,128]{1,0:T(8,128)S(1)} %get-tuple-element.55.a_t, ...), custom_call_target="tpu_custom_call" | custom-call | bytes 10500000 | tf_op jit(solution)/shard_map/adjoint_local/pallas_call | solution.py:788
  69.6 1.1 %collective-permute-start.10 = (f32[120,128]{1,0:T(8,128)S(1)}, f32[120,128]{1,0:T(8,128)S(1)}, u32[]{:S(2)}, u32[]{:S(2)}) collective-permute-start(f32[120,128]{1,0:T(8,128)S(1)} %get-tuple-element.60.refs_0_), channel_id=1, source_target_pairs={{0,8},{4,12},{8,0},{12,4},{16,24},{20,28},{24,16},{28,20},{1,9},{5... | collective-permute-start | bytes 184328 | tf_op jit(solution)/shard_map/ppermute | solution.py:84
  70.7 2.0 %collective-permute-start.11 = (f32[120,128]{1,0:T(8,128)S(1)}, f32[120,128]{1,0:T(8,128)S(1)}, u32[]{:S(2)}, u32[]{:S(2)}) collective-permute-start(f32[120,128]{1,0:T(8,128)S(1)} %get-tuple-element.60.refs_0_), channel_id=1, source_target_pairs={{0,16},{4,20},{8,24},{12,28},{16,0},{20,4},{24,8},{28,12},{1,17},{... | collective-permute-start | bytes 184328 | tf_op jit(solution)/shard_map/ppermute | solution.py:84
  72.6 0.5 collective-permute-start.12
  73.1 1.0 %collective-permute-done.10.refs_1_ = f32[120,128]{1,0:T(8,128)S(1)} collective-permute-done((f32[120,128]{1,0:T(8,128)S(1)}, f32[120,128]{1,0:T(8,128)S(1)}, u32[]{:S(2)}, u32[]{:S(2)}) %collective-permute-start.10) | collective-permute-done | bytes 61472 | tf_op jit(solution)/shard_map/ppermute | solution.py:84
  74.2 1.3 %collective-permute-done.11.refs_2_ = f32[120,128]{1,0:T(8,128)S(1)} collective-permute-done((f32[120,128]{1,0:T(8,128)S(1)}, f32[120,128]{1,0:T(8,128)S(1)}, u32[]{:S(2)}, u32[]{:S(2)}) %collective-permute-start.11) | collective-permute-done | bytes 61472 | tf_op jit(solution)/shard_map/ppermute | solution.py:84
  75.5 2.3 %collective-permute-done.12.refs_3_ = f32[120,128]{1,0:T(8,128)S(1)} collective-permute-done((f32[120,128]{1,0:T(8,128)S(1)}, f32[120,128]{1,0:T(8,128)S(1)}, u32[]{:S(2)}, u32[]{:S(2)}) %collective-permute-start.12) | collective-permute-done | bytes 61472 | tf_op jit(solution)/shard_map/ppermute | solution.py:84
  77.9 1.5 %collective-permute-done.13.far_back = f32[4,120,128]{2,1,0:T(8,128)S(1)} collective-permute-done((f32[4,120,128]{2,1,0:T(8,128)S(1)}, f32[4,120,128]{2,1,0:T(8,128)S(1)}, u32[]{:S(2)}, u32[]{:S(2)}) %collective-permute-start.13) | collective-permute-done | bytes 245792 | tf_op jit(solution)/shard_map/ppermute | solution.py:84
  79.4 3.1 %gradient.1 = (f32[4384,128]{1,0:T(8,128)}, f32[32,128]{1,0:T(8,128)}) custom-call(f32[4,160,128]{2,1,0:T(8,128)S(1)} %copy-done.2, f32[4,160,128]{2,1,0:T(8,128)S(1)} %copy-done.7, f32[4,120,128]{2,1,0:T(8,128)S(1)} %pile.3.near_back, f32[4,120,128]{2,1,0:T(8,128)S(1)} %collective-permute-done.13.far_back, f32[5120,128]{1,0:T(8,128)S(1)} %get-tuple-element.61.u_t, ...), custom_call_target="tpu_custom_call" | custom-call | bytes 10500000 | tf_op jit(solution)/shard_map/gradient/pallas_call | solution.py:799
  (36 shorter events, 1.4 us)
Async XLA Ops:
  0.6 10.5 %copy-start = (f32[4,137,8,128]{3,2,1,0:T(8,128)S(1)}, f32[4,137,8,128]{3,2,1,0:T(8,128)}, u32[]{:S(2)}) copy-start(f32[4,137,8,128]{3,2,1,0:T(8,128)} %param.11) | copy-start | bytes 6733828
  3.8 35.1 %all-to-all-start = ((bf16[32,144,128]{2,1,0:T(8,128)(2,1)}), bf16[32,144,128]{2,1,0:T(8,128)(2,1)S(1)}, u32[]{:S(2)}, u32[]{:S(2)}) async-start(bf16[32,144,128]{2,1,0:T(8,128)(2,1)} %pack.1), calls=%async_computation | async-start | bytes 2359296 | tf_op jit(solution)/shard_map/all_to_all | solution.py:644
  11.1 1.6 %copy-start.3 = (f32[4,137,8,128]{3,2,1,0:T(8,128)S(1)}, f32[4,137,8,128]{3,2,1,0:T(8,128)}, u32[]{:S(2)}) copy-start(f32[4,137,8,128]{3,2,1,0:T(8,128)} %param.12) | copy-start | bytes 6733828
  18.0 6.7 %collective-permute-start = (f32[160,128]{1,0:T(8,128)S(1)}, f32[160,128]{1,0:T(8,128)S(1)}, u32[]{:S(2)}, u32[]{:S(2)}) collective-permute-start(f32[160,128]{1,0:T(8,128)S(1)} %get-tuple-element.34.refs_0_), channel_id=1, source_target_pairs={{0,8},{4,12},{8,0},{12,4},{16,24},{20,28},{24,16},{28,20},{1,9},{5... | collective-permute-start | bytes 245768 | tf_op jit(solution)/shard_map/ppermute | solution.py:84
  19.8 6.0 %collective-permute-start.1 = (f32[160,128]{1,0:T(8,128)S(1)}, f32[160,128]{1,0:T(8,128)S(1)}, u32[]{:S(2)}, u32[]{:S(2)}) collective-permute-start(f32[160,128]{1,0:T(8,128)S(1)} %get-tuple-element.34.refs_0_), channel_id=1, source_target_pairs={{0,16},{4,20},{8,24},{12,28},{16,0},{20,4},{24,8},{28,12},{1,17},{... | collective-permute-start | bytes 245768 | tf_op jit(solution)/shard_map/ppermute | solution.py:84
  21.3 6.8 %collective-permute-start.2 = (f32[160,128]{1,0:T(8,128)S(1)}, f32[160,128]{1,0:T(8,128)S(1)}, u32[]{:S(2)}, u32[]{:S(2)}) collective-permute-start(f32[160,128]{1,0:T(8,128)S(1)} %get-tuple-element.34.refs_0_), channel_id=1, source_target_pairs={{0,24},{4,28},{8,16},{12,20},{16,8},{20,12},{24,0},{28,4},{1,25},{... | collective-permute-start | bytes 245768 | tf_op jit(solution)/shard_map/ppermute | solution.py:84
  28.1 3.9 %copy-start.1 = (f32[4,160,128]{2,1,0:T(8,128)}, f32[4,160,128]{2,1,0:T(8,128)S(1)}, u32[]{:S(2)}) copy-start(f32[4,160,128]{2,1,0:T(8,128)S(1)} %pile.2.near) | copy-start | bytes 983044
  28.1 1.7 %collective-permute-start.3 = (f32[4,160,128]{2,1,0:T(8,128)S(1)}, f32[4,160,128]{2,1,0:T(8,128)S(1)}, u32[]{:S(2)}, u32[]{:S(2)}) collective-permute-start(f32[4,160,128]{2,1,0:T(8,128)S(1)} %pile.2.near), channel_id=1, source_target_pairs={{0,4},{4,0},{8,12},{12,8},{16,20},{20,16},{24,28},{28,24},{1,5},{5... | collective-permute-start | bytes 983048 | tf_op jit(solution)/shard_map/ppermute | solution.py:84
  29.8 2.2 %copy-start.6 = (f32[4,160,128]{2,1,0:T(8,128)}, f32[4,160,128]{2,1,0:T(8,128)S(1)}, u32[]{:S(2)}) copy-start(f32[4,160,128]{2,1,0:T(8,128)S(1)} %collective-permute-done.3.far) | copy-start | bytes 983044
  29.8 5.0 %copy-start.4 = (f32[4,137,137]{2,0,1:T(4,128)S(1)}, f32[4,137,137]{2,0,1:T(4,128)}, u32[]{:S(2)}) copy-start(f32[4,137,137]{2,0,1:T(4,128)} %param.14) | copy-start | bytes 900916
  29.8 5.0 %copy-start.8 = (f32[4,5,8]{2,0,1:T(4,128)S(1)}, f32[4,5,8]{2,0,1:T(4,128)}, u32[]{:S(2)}) copy-start(f32[4,5,8]{2,0,1:T(4,128)} %param.13) | copy-start | bytes 1924
  32.0 11.8 %collective-permute-start.4 = (bf16[1152,128]{1,0:T(8,128)(2,1)}, bf16[1152,128]{1,0:T(8,128)(2,1)}, u32[]{:S(2)}, u32[]{:S(2)}) collective-permute-start(bf16[1152,128]{1,0:T(8,128)(2,1)} %get-tuple-element.45), channel_id=1, source_target_pairs={{0,1},{1,0},{2,3},{3,2},{4,5},{5,4},{6,7},{7,6},{8,9},{9,8},{10,11... | collective-permute-start | bytes 884744 | tf_op jit(solution)/shard_map/ppermute | solution.py:696
  33.4 10.4 %collective-permute-start.5 = (bf16[1152,128]{1,0:T(8,128)(2,1)}, bf16[1152,128]{1,0:T(8,128)(2,1)}, u32[]{:S(2)}, u32[]{:S(2)}) collective-permute-start(bf16[1152,128]{1,0:T(8,128)(2,1)} %get-tuple-element.46), channel_id=1, source_target_pairs={{1,2},{2,1},{5,6},{6,5},{9,10},{10,9},{13,14},{14,13},{17,18},{18,... | collective-permute-start | bytes 884744 | tf_op jit(solution)/shard_map/ppermute | solution.py:697
  38.9 1.1 %copy-start.5 = (f32[4,137,137]{2,0,1:T(4,128)S(1)}, f32[4,137,137]{2,0,1:T(4,128)}, u32[]{:S(2)}) copy-start(f32[4,137,137]{2,0,1:T(4,128)} %param.14) | copy-start | bytes 900916
  39.9 3.9 %copy-start.9 = (s32[1,32,128]{2,1,0:T(8,128)S(1)}, s32[1,32,128]{2,1,0:T(8,128)}, u32[]{:S(2)}) copy-start(s32[1,32,128]{2,1,0:T(8,128)} %param.15) | copy-start | bytes 49156
  39.9 3.9 %copy-start.10 = (s32[1,32]{1,0:T(1,128)S(1)}, s32[1,32]{1,0:T(1,128)}, u32[]{:S(2)}) copy-start(s32[1,32]{1,0:T(1,128)} %param.16) | copy-start | bytes 388
  39.9 3.9 %copy-start.11 = (s32[1,32]{1,0:T(1,128)S(1)}, s32[1,32]{1,0:T(1,128)}, u32[]{:S(2)}) copy-start(s32[1,32]{1,0:T(1,128)} %param.18) | copy-start | bytes 388
  39.9 3.9 %copy-start.12 = (s32[1,32]{1,0:T(1,128)S(1)}, s32[1,32]{1,0:T(1,128)}, u32[]{:S(2)}) copy-start(s32[1,32]{1,0:T(1,128)} %param.17) | copy-start | bytes 388
  53.8 13.8 %collective-permute-start.6 = (bf16[1168,128]{1,0:T(8,128)(2,1)S(1)}, bf16[1168,128]{1,0:T(8,128)(2,1)S(1)}, u32[]{:S(2)}, u32[]{:S(2)}) collective-permute-start(bf16[1168,128]{1,0:T(8,128)(2,1)S(1)} %get-tuple-element.53), channel_id=1, source_target_pairs={{0,1},{1,0},{2,3},{3,2},{4,5},{5,4},{6,7},{7,6},{8,9},{9,8},{10,11... | collective-permute-start | bytes 897032 | tf_op jit(solution)/shard_map/ppermute | solution.py:775
  56.4 11.2 %collective-permute-start.7 = (bf16[1168,128]{1,0:T(8,128)(2,1)S(1)}, bf16[1168,128]{1,0:T(8,128)(2,1)S(1)}, u32[]{:S(2)}, u32[]{:S(2)}) collective-permute-start(bf16[1168,128]{1,0:T(8,128)(2,1)S(1)} %get-tuple-element.54), channel_id=1, source_target_pairs={{1,2},{2,1},{5,6},{6,5},{9,10},{10,9},{13,14},{14,13},{17,18},{18,... | collective-permute-start | bytes 897032 | tf_op jit(solution)/shard_map/ppermute | solution.py:776
  57.2 8.5 %collective-permute-start.8 = (f32[8,128]{1,0:T(8,128)S(1)}, f32[8,128]{1,0:T(8,128)S(1)}, u32[]{:S(2)}, u32[]{:S(2)}) collective-permute-start(f32[8,128]{1,0:T(8,128)S(1)} %get-tuple-element.58), channel_id=1, source_target_pairs={{0,3},{3,0},{4,7},{7,4},{8,11},{11,8},{12,15},{15,12},{16,19},{19,... | collective-permute-start | bytes 12296 | tf_op jit(solution)/shard_map/ppermute | solution.py:771
  62.3 5.3 %collective-permute-start.9 = (f32[8,128]{1,0:T(8,128)S(1)}, f32[8,128]{1,0:T(8,128)S(1)}, u32[]{:S(2)}, u32[]{:S(2)}) collective-permute-start(f32[8,128]{1,0:T(8,128)S(1)} %get-tuple-element.59), channel_id=1, source_target_pairs={{0,2},{1,3},{2,0},{3,1},{4,6},{5,7},{6,4},{7,5},{8,10},{9,11},{10,... | collective-permute-start | bytes 12296 | tf_op jit(solution)/shard_map/ppermute | solution.py:774
  67.6 11.8 %copy-start.2 = (f32[4,160,128]{2,1,0:T(8,128)S(1)}, f32[4,160,128]{2,1,0:T(8,128)}, u32[]{:S(2)}) copy-start(f32[4,160,128]{2,1,0:T(8,128)} %copy-done.1) | copy-start | bytes 983044
  67.6 11.8 %copy-start.7 = (f32[4,160,128]{2,1,0:T(8,128)S(1)}, f32[4,160,128]{2,1,0:T(8,128)}, u32[]{:S(2)}) copy-start(f32[4,160,128]{2,1,0:T(8,128)} %copy-done.6) | copy-start | bytes 983044
  69.6 4.6 %collective-permute-start.10 = (f32[120,128]{1,0:T(8,128)S(1)}, f32[120,128]{1,0:T(8,128)S(1)}, u32[]{:S(2)}, u32[]{:S(2)}) collective-permute-start(f32[120,128]{1,0:T(8,128)S(1)} %get-tuple-element.60.refs_0_), channel_id=1, source_target_pairs={{0,8},{4,12},{8,0},{12,4},{16,24},{20,28},{24,16},{28,20},{1,9},{5... | collective-permute-start | bytes 184328 | tf_op jit(solution)/shard_map/ppermute | solution.py:84
  70.7 4.8 %collective-permute-start.11 = (f32[120,128]{1,0:T(8,128)S(1)}, f32[120,128]{1,0:T(8,128)S(1)}, u32[]{:S(2)}, u32[]{:S(2)}) collective-permute-start(f32[120,128]{1,0:T(8,128)S(1)} %get-tuple-element.60.refs_0_), channel_id=1, source_target_pairs={{0,16},{4,20},{8,24},{12,28},{16,0},{20,4},{24,8},{28,12},{1,17},{... | collective-permute-start | bytes 184328 | tf_op jit(solution)/shard_map/ppermute | solution.py:84
  72.6 5.1 %collective-permute-start.12 = (f32[120,128]{1,0:T(8,128)S(1)}, f32[120,128]{1,0:T(8,128)S(1)}, u32[]{:S(2)}, u32[]{:S(2)}) collective-permute-start(f32[120,128]{1,0:T(8,128)S(1)} %get-tuple-element.60.refs_0_), channel_id=1, source_target_pairs={{0,24},{4,28},{8,16},{12,20},{16,8},{20,12},{24,0},{28,4},{1,25},{... | collective-permute-start | bytes 184328 | tf_op jit(solution)/shard_map/ppermute | solution.py:84
  77.8 1.6 %collective-permute-start.13 = (f32[4,120,128]{2,1,0:T(8,128)S(1)}, f32[4,120,128]{2,1,0:T(8,128)S(1)}, u32[]{:S(2)}, u32[]{:S(2)}) collective-permute-start(f32[4,120,128]{2,1,0:T(8,128)S(1)} %pile.3.near_back), channel_id=1, source_target_pairs={{0,4},{4,0},{8,12},{12,8},{16,20},{20,16},{24,28},{28,24},{1,5},{5... | collective-permute-start | bytes 737288 | tf_op jit(solution)/shard_map/ppermute | solution.py:84
